TPU v7x, 256 devices: a whole 4x4x8 slice. The times are simulated.
256 devices in a mesh: ctx: 32 (over y, x, core), exp: 8 (over z).
Axes of the slice: x: 4, y: 4, z: 8, core: 2. Of those that a mesh axis runs over, the one named last changes fastest.
Arguments:
- query: bfloat16 [3584, 6144], P('ctx', 'exp'), may hold values from -6 to 6
- keys: bfloat16 [3584, 6144], P('ctx', 'exp'), may hold values from -6 to 6
- values: bfloat16 [3584, 6144], P('ctx', 'exp'), may hold values from -6 to 6
- stream: bfloat16 [3584, 6144], P('ctx', 'exp'), may hold values from -6 to 6
- log_decay: float32 [3584, 48], P('ctx', 'exp'), may hold values from 0 to 1, as said below
- attn_gain: float32 [6144], P('exp'), may hold values from 0.1 to 1.9
- routes: int32 [3584, 2], P('ctx'), may hold values from 0 to 7, all different within a row; in each aligned block of 112 rows (0 to 111, 112 to 223, ...) at most 30 rows name the same one
- gate_weights: float32 [3584, 2], P('ctx'), may hold values from 0.2 to 1
- moe_gain: float32 [6144], replicated, may hold values from 0.1 to 1.9
- w_gate: bfloat16 [8, 6144, 9216], P('exp', None, 'ctx'), may hold values from -0.078125 to 0.078125
- w_up: bfloat16 [8, 6144, 9216], P('exp', None, 'ctx'), may hold values from -0.078125 to 0.078125
- w_down: bfloat16 [8, 9216, 6144], P('exp', 'ctx'), may hold values from -0.0625 to 0.0625
Outputs:
- mixed: bfloat16 [3584, 6144], P('ctx', 'exp')
Inputs may be any that keep to these rules, and one draw needn't show every extreme that they name: The two experts of a position differ. In each aligned block of 112 positions no expert is named by more than 30 routes, and some expert reaches 30 in some block. `log_decay`: nonnegative decay rates, one for each head and position.
All inputs are finite; a program needn't handle non-finite values.
Results may differ from a plain program's by a relative error of at most 0.023.
Values may be sent and summed in bfloat16 or wider, within the bound.
No kernel may reach another device: no remote copies, remote signals or barrier semaphores. Data moves between devices by JAX's collectives and lax.ppermute only.
A program may use at most 128 MiB of HBM per device.

v0:
```python
import jax
import jax.numpy as jnp
from jax import lax
from jax.experimental import pallas as pl
from jax.experimental.pallas import tpu as pltpu
from jax.sharding import PartitionSpec as P

STABILIZER = 1e-05
HIGHEST = lax.Precision.HIGHEST
F32 = jnp.float32
BF16 = jnp.bfloat16
NT = (((1,), (1,)), ((), ()))
TN = (((0,), (0,)), ((), ()))
SIDE = 4
CORES = 2
SLOTS = 32
GROUP = SIDE * SLOTS
PIECE = 24
FEATURES = 6144
HALF = FEATURES // 2


def whole(memory=pltpu.VMEM):
    return pl.BlockSpec(memory_space=memory)


def params(mib):
    return pltpu.CompilerParams(vmem_limit_bytes=mib << 20)


def chip_pairs(step, flip=0):
    pairs = []
    for y in range(SIDE):
        for x in range(SIDE):
            for core in range(CORES):
                dy, dx = step(core)
                to = (y + dy) % SIDE * SIDE + (x + dx) % SIDE
                pairs.append(((y * SIDE + x) * CORES + core, to * CORES + (core + flip) % CORES))
    return pairs


def send(rows, axis, distance):
    along_x = ((0, distance), (distance, 0))
    return lax.ppermute(rows, "ctx", chip_pairs(lambda core: along_x[(core + axis) % CORES]))


def silu(v):
    return v / (1.0 + jnp.exp(-v))


def local_kernel(q_ref, k_ref, v_ref, rate_ref, piece_ref, inside_ref, decayed_ref, wide):
    length, width = q_ref.shape
    heads = rate_ref.shape[1]
    head = width // heads
    wide[...] = jnp.zeros_like(wide)
    wide[:, :heads] = rate_ref[...]
    rates = wide[...]
    row = lax.broadcasted_iota(jnp.int32, (length, length), 0)
    col = lax.broadcasted_iota(jnp.int32, (length, length), 1)
    causal = row >= col
    lower = causal.astype(F32)
    cumulated = jnp.dot(lower, rates, precision=HIGHEST, preferred_element_type=F32)
    across = lax.dot_general(
        rates, lower, (((0,), (1,)), ((), ())), precision=HIGHEST, preferred_element_type=F32
    )
    total = cumulated[length - 1 : length, :]
    states = []
    for h in range(heads):
        part = slice(h * head, (h + 1) * head)
        qa = silu(q_ref[:, part].astype(F32))
        ka = silu(k_ref[:, part].astype(F32))
        v = v_ref[:, part]
        down = cumulated[:, h : h + 1]
        spread = jnp.where(causal, down - across[h : h + 1, :], 0.0)
        weights = jnp.where(causal, jnp.exp(-spread), 0.0)
        scores = lax.dot_general(qa.astype(BF16), ka.astype(BF16), NT, preferred_element_type=F32)
        inside_ref[:, part] = jnp.dot(
            (scores * weights).astype(BF16), v, preferred_element_type=F32
        )
        tails = jnp.exp(down - total[:, h : h + 1])
        states.append(
            lax.dot_general((ka * tails).astype(BF16), v, TN, preferred_element_type=F32)
        )
        decayed_ref[:, part] = (qa * jnp.exp(-down)).astype(BF16)
    first = total.astype(BF16).astype(F32)
    second = (total - first).astype(BF16).astype(F32)
    third = total - first - second
    line = lax.broadcasted_iota(jnp.int32, (8, total.shape[1]), 0)
    notes = jnp.where(line == 0, first, jnp.where(line == 1, second, jnp.where(line == 2, third, 0.0)))
    count = piece_ref.shape[0]
    state = jnp.concatenate(states, axis=0).reshape(count, PIECE, head)
    notes = jnp.broadcast_to(notes[None], (count,) + notes.shape)
    piece_ref[...] = jnp.concatenate([state, notes], axis=1).astype(BF16)


def attend_locally(query, keys, values, log_decay, count):
    length, width = query.shape
    return pl.pallas_call(
        local_kernel,
        out_shape=(
            jax.ShapeDtypeStruct((count, PIECE + 8, 128), BF16),
            jax.ShapeDtypeStruct((length, width), F32),
            jax.ShapeDtypeStruct((length, width), BF16),
        ),
        in_specs=[whole()] * 4,
        out_specs=[whole()] * 3,
        scratch_shapes=[pltpu.VMEM((length, 128), F32)],
        compiler_params=params(56),
    )(query, keys, values, log_decay)


def scan_kernel(place_ref, pieces_ref, out_ref):
    count, rows, lanes = pieces_ref.shape
    pieces = pieces_ref[...].astype(F32)
    notes = pieces[:, PIECE:]
    total = notes[:, 0:1] + notes[:, 1:2] + notes[:, 2:3]
    row = lax.broadcasted_iota(jnp.int32, (PIECE, lanes), 0) + place_ref[0] * PIECE
    own = lax.shift_right_logical(row, 7) == lax.broadcasted_iota(jnp.int32, (PIECE, lanes), 1)
    decay = jnp.sum(jnp.where(own[None], jnp.exp(-total), 0.0), axis=-1, keepdims=True)
    state = jnp.zeros((PIECE, lanes), F32)
    blank = jnp.zeros((rows - PIECE, lanes), F32)
    for i in range(count):
        out_ref[i] = jnp.concatenate([state, blank], axis=0).astype(BF16)
        state = decay[i] * state + pieces[i, :PIECE]


def scan_states(place, pieces):
    return pl.pallas_call(
        scan_kernel,
        out_shape=jax.ShapeDtypeStruct(pieces.shape, BF16),
        in_specs=[whole(pltpu.SMEM), whole()],
        out_specs=whole(),
        compiler_params=params(16),
    )(place, pieces)


def hidden_kernel(
    state_ref, inside_ref, decayed_ref, stream_ref, gain_ref, routes_ref, hidden_ref, sent_ref, lead_ref, next_ref
):
    length, width = stream_ref.shape
    head = 128
    state = state_ref[...].astype(F32)[:, :PIECE].reshape(width, head).astype(BF16)
    for h in range(width // head):
        part = slice(h * head, (h + 1) * head)
        carried = jnp.dot(decayed_ref[:, part], state[part], preferred_element_type=F32)
        attended = inside_ref[:, part] + carried
        scale = lax.rsqrt(jnp.mean(attended * attended, axis=-1, keepdims=True) + STABILIZER)
        hidden_ref[:, part] = (
            stream_ref[:, part].astype(F32) + attended * scale * gain_ref[:, part]
        ).astype(BF16)
    lane = lax.broadcasted_iota(jnp.int32, (length, 128), 1)
    one = (lane == routes_ref[:, 0:1]).astype(F32)
    two = (lane == routes_ref[:, 1:2]).astype(F32)
    row = lax.broadcasted_iota(jnp.int32, (length, length), 0)
    col = lax.broadcasted_iota(jnp.int32, (length, length), 1)
    before = jnp.dot(
        (row > col).astype(BF16), (one + two).astype(BF16), preferred_element_type=F32
    )
    slot_one = jnp.sum(before * one, axis=-1, keepdims=True).astype(jnp.int32)
    slot_two = jnp.sum(before * two, axis=-1, keepdims=True).astype(jnp.int32)
    target = lax.broadcasted_iota(jnp.int32, lead_ref.shape, 1)
    lead = (target == routes_ref[:, 0:1] * SLOTS + slot_one).astype(F32).astype(BF16)
    follow = (target == routes_ref[:, 1:2] * SLOTS + slot_two).astype(F32).astype(BF16)
    lead_ref[...] = lead
    next_ref[...] = follow
    sent = lax.dot_general(lead + follow, hidden_ref[...], TN, preferred_element_type=F32)
    sent_ref[...] = sent.astype(BF16).reshape(sent_ref.shape)


def finish_attention(state, inside, decayed, stream, gain, routes, experts):
    length, width = stream.shape
    return pl.pallas_call(
        hidden_kernel,
        out_shape=(
            jax.ShapeDtypeStruct((length, width), BF16),
            jax.ShapeDtypeStruct((experts, SLOTS, width), BF16),
            jax.ShapeDtypeStruct((length, experts * SLOTS), BF16),
            jax.ShapeDtypeStruct((length, experts * SLOTS), BF16),
        ),
        in_specs=[whole()] * 6,
        out_specs=[whole()] * 4,
        compiler_params=params(56),
    )(state, inside, decayed, stream, gain, routes)


def norm_kernel(rows_ref, gain_ref, out_ref):
    parts, _, width = rows_ref.shape
    rows = [rows_ref[i].astype(F32) for i in range(parts)]
    squares = sum(jnp.sum(r * r, axis=-1, keepdims=True) for r in rows)
    scale = lax.rsqrt(squares / (parts * width) + STABILIZER)
    for i, r in enumerate(rows):
        part = slice(i * width, (i + 1) * width)
        out_ref[:, part] = (r * scale * gain_ref[:, part]).astype(BF16)


def norm_rows(rows, gain):
    return pl.pallas_call(
        norm_kernel,
        out_shape=jax.ShapeDtypeStruct((SLOTS, FEATURES), BF16),
        in_specs=[whole()] * 2,
        out_specs=whole(),
        compiler_params=params(16),
    )(rows, gain)


PACKED = 640
CHUNK = 1536
LIMIT = 18


def expert_kernel(groups, *refs):
    x_refs, refs = refs[:groups], refs[groups:]
    up_refs, down_refs, refs = refs[:4], refs[4:6], refs[6:]
    out_refs, sums = refs[:-1], refs[-1]
    hidden = up_refs[0].shape[0]
    width = x_refs[0].shape[1]
    for at in range(0, width, CHUNK):
        part = slice(at, at + CHUNK)
        x = jnp.concatenate([ref[:, part] for ref in x_refs], axis=0)
        for w, ref in enumerate(up_refs):
            product = lax.dot_general(ref[:, part], x, NT, preferred_element_type=F32)
            sums[w] = product if at == 0 else sums[w] + product

    rows = groups * GROUP
    blank = PACKED - 2 * hidden
    activated = [silu(sums[2 * w]) * sums[2 * w + 1] for w in range(2)]
    activated.append(jnp.zeros((blank, rows), F32))
    activated = jnp.transpose(jnp.concatenate(activated, axis=0)).astype(BF16)

    for at in range(0, FEATURES, CHUNK):
        half, start = divmod(at, HALF)
        weights = [ref[:, at : at + CHUNK] for ref in down_refs]
        weights = jnp.concatenate(weights + [jnp.zeros((blank, CHUNK), BF16)], axis=0)
        product = jnp.dot(activated, weights, preferred_element_type=F32).astype(BF16)
        for g in range(groups):
            out_refs[2 * g + half][:, start : start + CHUNK] = product[g * GROUP : (g + 1) * GROUP]


def expert(xs, ups, downs):
    groups = len(xs)
    hidden = ups[0].shape[0]
    rows = groups * GROUP
    return pl.pallas_call(
        lambda *refs: expert_kernel(groups, *refs),
        out_shape=(jax.ShapeDtypeStruct((GROUP, HALF), BF16),) * (2 * groups),
        in_specs=[whole()] * (groups + 6),
        out_specs=(whole(),) * (2 * groups),
        scratch_shapes=[pltpu.VMEM((4, hidden, rows), F32)],
        compiler_params=params(LIMIT),
        cost_estimate=pl.CostEstimate(
            flops=2 * 256 * FEATURES * 6 * hidden,
            bytes_accessed=FEATURES * 6 * hidden * 2,
            transcendentals=0,
        ),
    )(*xs, *ups, *downs)


def mix_kernel(back_ref, lead_ref, next_ref, gates_ref, hidden_ref, out_ref):
    rows = back_ref[...].reshape(lead_ref.shape[1], out_ref.shape[1])
    one = jnp.dot(lead_ref[...], rows, preferred_element_type=F32)
    two = jnp.dot(next_ref[...], rows, preferred_element_type=F32)
    gates = gates_ref[...]
    moe = gates[:, 0:1] * one + gates[:, 1:2] * two
    out_ref[...] = (hidden_ref[...].astype(F32) + moe).astype(BF16)


def mix(back, lead, follow, gates, hidden):
    return pl.pallas_call(
        mix_kernel,
        out_shape=jax.ShapeDtypeStruct(hidden.shape, BF16),
        in_specs=[whole()] * 5,
        out_specs=whole(),
        compiler_params=params(16),
    )(back, lead, follow, gates, hidden)


FIRST, SECOND = 0, 1


def gather_first(block):
    after = send(block, FIRST, -1)
    before = send(block, FIRST, 1)
    opposite = send(block, FIRST, 2)
    blocks = (block, after, before, opposite)
    return jnp.concatenate(blocks, axis=0)


def added(*terms):
    return sum(t.astype(F32) for t in terms)


def body(
    query,
    keys,
    values,
    stream,
    log_decay,
    attn_gain,
    routes,
    gate_weights,
    moe_gain,
    w_gate,
    w_up,
    w_down,
):
    experts = w_gate.shape[0] * lax.axis_size("exp")
    blocks = lax.axis_size("ctx")
    gate, up, down = w_gate[0].T, w_up[0].T, w_down[0]
    sibling = chip_pairs(lambda core: (0, 0), 1)
    other_gate = lax.ppermute(gate, "ctx", sibling)
    other_up = lax.ppermute(up, "ctx", sibling)
    other_down = lax.ppermute(down, "ctx", sibling)

    pieces, inside, decayed = attend_locally(query, keys, values, log_decay, blocks)
    pieces = lax.all_to_all(pieces, "ctx", split_axis=0, concat_axis=0, tiled=True)
    place = lax.axis_index("ctx").astype(jnp.int32).reshape(1)
    states = scan_states(place, pieces)
    states = lax.all_to_all(states, "ctx", split_axis=0, concat_axis=0, tiled=True)
    states, other_gate, other_up, other_down = lax.optimization_barrier(
        (states, other_gate, other_up, other_down)
    )
    hidden, sent, lead, follow = finish_attention(
        states, inside, decayed, stream, attn_gain.reshape(1, -1), routes, experts
    )
    arrived = lax.all_to_all(sent, "exp", split_axis=0, concat_axis=0, tiled=True)
    rows = norm_rows(arrived, moe_gain.reshape(1, -1))
    ups, downs = (gate, up, other_gate, other_up), (down, other_down)

    own = gather_first(rows)
    after = send(own, SECOND, -1)
    before = send(own, SECOND, 1)
    here_one, here_two = expert((own,), ups, downs)
    after, before, here_one, here_two = lax.optimization_barrier(
        (after, before, here_one, here_two)
    )
    opposite_one = send(after[:, :HALF], SECOND, -1)
    opposite_two = send(before[:, HALF:], SECOND, 1)
    to_after_one, to_after_two, to_before_one, to_before_two = expert((after, before), ups, downs)
    from_after_one = send(to_before_one, SECOND, -1)
    from_before_two = send(to_after_two, SECOND, 1)
    opposite = jnp.concatenate([opposite_one, opposite_two], axis=1)
    opposite, to_after_one, to_after_two, to_before_one, to_before_two = lax.optimization_barrier(
        (opposite, to_after_one, to_after_two, to_before_one, to_before_two)
    )
    far_one, far_two = expert((opposite,), ups, downs)
    far_one, far_two, from_after_one, from_before_two = lax.optimization_barrier(
        (far_one, far_two, from_after_one, from_before_two)
    )
    through_after = send(far_one, SECOND, 1)
    through_before = send(far_two, SECOND, -1)
    from_before_one = send(added(to_after_one, through_after).astype(BF16), SECOND, 1)
    from_after_two = send(added(to_before_two, through_before).astype(BF16), SECOND, -1)
    sums = jnp.concatenate(
        [
            added(here_one, from_after_one, from_before_one),
            added(here_two, from_after_two, from_before_two),
        ],
        axis=1,
    ).reshape(SIDE, SLOTS, FEATURES)
    rounded = sums.astype(BF16)
    from_before = send(rounded[1], FIRST, 1)
    from_after = send(rounded[2], FIRST, -1)
    from_opposite = send(rounded[3], FIRST, 2)
    summed = added(sums[0], from_before, from_after, from_opposite).astype(BF16)
    summed = jnp.transpose(summed.reshape(SLOTS, experts, -1), (1, 0, 2))
    returned = lax.all_to_all(summed, "exp", split_axis=0, concat_axis=0, tiled=True)
    return mix(returned, lead, follow, gate_weights, hidden)


def solution(mesh):
    return jax.shard_map(
        body,
        mesh=mesh,
        in_specs=(
            P("ctx", "exp"),
            P("ctx", "exp"),
            P("ctx", "exp"),
            P("ctx", "exp"),
            P("ctx", "exp"),
            P("exp"),
            P("ctx", None),
            P("ctx", None),
            P(),
            P("exp", None, "ctx"),
            P("exp", None, "ctx"),
            P("exp", "ctx", None),
        ),
        out_specs=P("ctx", "exp"),
        check_vma=False,
    )
```

profile of v0, /device:TPU:2, one launch (start us, length us, event | category | flops | bytes accessed | tf_op | source)
XLA Modules:
  0.0 191.7 jit_solution(13641016910683292263)
XLA Ops:
  2.0 3.1 %shard_map.118 = (bf16[32,32,128]{2,1,0:T(8,128)(2,1)}, f32[112,768]{1,0:T(8,128)}, bf16[112,768]{1,0:T(8,128)(2,1)}) custom-call(bf16[112,768]{1,0:T(8,128)(2,1)} %q_ref.1, bf16[112,768]{1,0:T(8,128)(2,1)} %k_ref.1, bf16[112,768]{1,0:T(8,128)(2,1)} %v_ref.1, f32[112,6]{1,0:T(8,128)} %copy.16.rate_ref), custom_call_target="tpu_custom_call" | custom-call | tf_op jit(solution)/shard_map/pallas_call | solution.py:98
  5.1 8.0 %all-to-all-start = ((bf16[32,32,128]{2,1,0:T(8,128)(2,1)}), bf16[32,32,128]{2,1,0:T(8,128)(2,1)}, u32[]{:S(2)}, u32[]{:S(2)}) async-start(bf16[32,32,128]{2,1,0:T(8,128)(2,1)} %get-tuple-element.35), calls=%async_computation | async-start | bytes 524288 | tf_op jit(solution)/shard_map/all_to_all | solution.py:315
  13.1 7.7 %all-to-all-done.pieces_ref = bf16[32,32,128]{2,1,0:T(8,128)(2,1)} async-done(((bf16[32,32,128]{2,1,0:T(8,128)(2,1)}), bf16[32,32,128]{2,1,0:T(8,128)(2,1)}, u32[]{:S(2)}, u32[]{:S(2)}) %all-to-all-start) | async-done | bytes 262176 | tf_op jit(solution)/shard_map/all_to_all | solution.py:315
  22.7 5.6 %all-to-all-start.1 = ((bf16[32,32,128]{2,1,0:T(8,128)(2,1)}), bf16[32,32,128]{2,1,0:T(8,128)(2,1)}, u32[]{:S(2)}, u32[]{:S(2)}) async-start(bf16[32,32,128]{2,1,0:T(8,128)(2,1)} %copy-done.4), calls=%async_computation.1 | async-start | bytes 524288 | tf_op jit(solution)/shard_map/all_to_all | solution.py:318
  29.6 6.5 %all-to-all-done.1.state_ref = bf16[32,32,128]{2,1,0:T(8,128)(2,1)} async-done(((bf16[32,32,128]{2,1,0:T(8,128)(2,1)}), bf16[32,32,128]{2,1,0:T(8,128)(2,1)}, u32[]{:S(2)}, u32[]{:S(2)}) %all-to-all-start.1) | async-done | bytes 262176 | tf_op jit(solution)/shard_map/all_to_all | solution.py:318
  36.2 2.8 %shard_map.120 = (bf16[112,768]{1,0:T(8,128)(2,1)}, bf16[8,32,768]{2,1,0:T(8,128)(2,1)}, bf16[112,256]{1,0:T(8,128)(2,1)}, bf16[112,256]{1,0:T(8,128)(2,1)}) custom-call(bf16[32,32,128]{2,1,0:T(8,128)(2,1)} %all-to-all-done.1.state_ref, f32[112,768]{1,0:T(8,128)} %get-tuple-element.37.inside_ref, bf16[112,768]{1,0:T(8,128)(2,1)} %get-tuple-element.38.decayed_ref, ...), custom_call_target="tpu_custom_call" | custom-call | tf_op jit(solution)/shard_map/pallas_call | solution.py:172
  38.9 23.8 %all_to_all.20.rows_ref = bf16[8,32,768]{2,1,0:T(8,128)(2,1)S(1)} all-to-all(bf16[8,32,768]{2,1,0:T(8,128)(2,1)} %get-tuple-element.39), channel_id=1, replica_groups=mesh['ctx'=32,'exp'=8] {'exp'}, dimensions={0} | all-to-all | bytes 786432 | tf_op jit(solution)/shard_map/all_to_all | solution.py:325
  65.7 2.7 %collective-permute-start.5 = (bf16[32,6144]{1,0:T(8,128)(2,1)S(1)}, bf16[32,6144]{1,0:T(8,128)(2,1)S(1)}, u32[]{:S(2)}, u32[]{:S(2)}) collective-permute-start(bf16[32,6144]{1,0:T(8,128)(2,1)S(1)} %shard_map.121), channel_id=1, source_target_pairs={{0,32},{8,136},{16,48},{24,152},{32,0},{40,168},{48,16},{56,184},{... | collective-permute-start | bytes 1179656 | tf_op jit(solution)/shard_map/ppermute | solution.py:44
  68.5 7.2 %collective-permute-done.3 = bf16[32,6144]{1,0:T(8,128)(2,1)S(1)} collective-permute-done((bf16[32,6144]{1,0:T(8,128)(2,1)S(1)}, bf16[32,6144]{1,0:T(8,128)(2,1)S(1)}, u32[]{:S(2)}, u32[]{:S(2)}) %collective-permute-start.3) | collective-permute-done | bytes 393248 | tf_op jit(solution)/shard_map/ppermute | solution.py:44
  80.0 9.3 %shard_map.122 = (bf16[128,3072]{1,0:T(8,128)(2,1)S(1)}, bf16[128,3072]{1,0:T(8,128)(2,1)S(1)}) custom-call(bf16[128,6144]{1,0:T(8,128)(2,1)S(1)} %pad_maximum_fusion.1.refs_0_, bf16[288,6144]{1,0:T(8,128)(2,1)S(1)} %bitcast.17, bf16[288,6144]{1,0:T(8,128)(2,1)S(1)} %bitcast.21, bf16[288,6144]{1,0:T(8,128)(2,1)} %collective-permute-done.refs_3_.refs_4_, ...), custom_call_target="tpu_custom_call" | custom-call | flops 5435817984 | bytes 21233664 | tf_op jit(solution)/shard_map/pallas_call | solution.py:243
  89.3 7.1 %collective-permute-done.6.refs_0_ = bf16[128,6144]{1,0:T(8,128)(2,1)S(1)} collective-permute-done((bf16[128,6144]{1,0:T(8,128)(2,1)S(1)}, bf16[128,6144]{1,0:T(8,128)(2,1)S(1)}, u32[]{:S(2)}, u32[]{:S(2)}) %collective-permute-start.6) | collective-permute-done | bytes 1572896 | tf_op jit(solution)/shard_map/ppermute | solution.py:44
  96.4 2.3 %collective-permute-done.7.refs_1_ = bf16[128,6144]{1,0:T(8,128)(2,1)S(1)} collective-permute-done((bf16[128,6144]{1,0:T(8,128)(2,1)S(1)}, bf16[128,6144]{1,0:T(8,128)(2,1)S(1)}, u32[]{:S(2)}, u32[]{:S(2)}) %collective-permute-start.7) | collective-permute-done | bytes 1572896 | tf_op jit(solution)/shard_map/ppermute | solution.py:44
  98.9 2.1 %collective-permute-start.9 = (bf16[128,3072]{1,0:T(8,128)(2,1)S(1)}, bf16[128,3072]{1,0:T(8,128)(2,1)S(1)}, u32[]{:S(2)}, u32[]{:S(2)}) collective-permute-start(bf16[128,3072]{1,0:T(8,128)(2,1)S(1)} %slice.23), channel_id=1, source_target_pairs={{0,64},{8,24},{16,80},{24,40},{32,96},{40,56},{48,112},{56,8},{64,... | collective-permute-start | bytes 2359304 | tf_op jit(solution)/shard_map/ppermute | solution.py:44
  101.0 10.6 %shard_map.123 = (bf16[128,3072]{1,0:T(8,128)(2,1)S(1)}, bf16[128,3072]{1,0:T(8,128)(2,1)S(1)}, bf16[128,3072]{1,0:T(8,128)(2,1)S(1)}, bf16[128,3072]{1,0:T(8,128)(2,1)S(1)}) custom-call(bf16[128,6144]{1,0:T(8,128)(2,1)S(1)} %collective-permute-done.6.refs_0_, bf16[128,6144]{1,0:T(8,128)(2,1)S(1)} %collective-permute-done.7.refs_1_, ...), custom_call_target="tpu_custom_call" | custom-call | flops 5435817984 | bytes 21233664 | tf_op jit(solution)/shard_map/pallas_call | solution.py:243
  113.9 9.3 %shard_map.124 = (bf16[128,3072]{1,0:T(8,128)(2,1)S(1)}, bf16[128,3072]{1,0:T(8,128)(2,1)S(1)}) custom-call(bf16[128,6144]{1,0:T(8,128)(2,1)S(1)} %pad_maximum_fusion.2.refs_0_, bf16[288,6144]{1,0:T(8,128)(2,1)S(1)} %bitcast.19, bf16[288,6144]{1,0:T(8,128)(2,1)S(1)} %bitcast.23, bf16[288,6144]{1,0:T(8,128)(2,1)} %collective-permute-done.refs_3_.refs_4_, ...), custom_call_target="tpu_custom_call" | custom-call | flops 5435817984 | bytes 21233664 | tf_op jit(solution)/shard_map/pallas_call | solution.py:243
  123.7 2.4 %collective-permute-done.11 = bf16[128,3072]{1,0:T(8,128)(2,1)S(1)} collective-permute-done((bf16[128,3072]{1,0:T(8,128)(2,1)S(1)}, bf16[128,3072]{1,0:T(8,128)(2,1)S(1)}, u32[]{:S(2)}, u32[]{:S(2)}) %collective-permute-start.11) | collective-permute-done | bytes 786464 | tf_op jit(solution)/shard_map/ppermute | solution.py:44
  128.2 10.0 %collective-permute-done.14 = bf16[128,3072]{1,0:T(8,128)(2,1)S(1)} collective-permute-done((bf16[128,3072]{1,0:T(8,128)(2,1)S(1)}, bf16[128,3072]{1,0:T(8,128)(2,1)S(1)}, u32[]{:S(2)}, u32[]{:S(2)}) %collective-permute-start.14) | collective-permute-done | bytes 786464 | tf_op jit(solution)/shard_map/ppermute | solution.py:44
  140.7 9.7 %collective-permute-done.15 = bf16[128,3072]{1,0:T(8,128)(2,1)S(1)} collective-permute-done((bf16[128,3072]{1,0:T(8,128)(2,1)S(1)}, bf16[128,3072]{1,0:T(8,128)(2,1)S(1)}, u32[]{:S(2)}, u32[]{:S(2)}) %collective-permute-start.15) | collective-permute-done | bytes 786464 | tf_op jit(solution)/shard_map/ppermute | solution.py:44
  150.7 2.4 %collective-permute-done.13 = bf16[128,3072]{1,0:T(8,128)(2,1)S(1)} collective-permute-done((bf16[128,3072]{1,0:T(8,128)(2,1)S(1)}, bf16[128,3072]{1,0:T(8,128)(2,1)S(1)}, u32[]{:S(2)}, u32[]{:S(2)}) %collective-permute-start.13) | collective-permute-done | bytes 786464 | tf_op jit(solution)/shard_map/ppermute | solution.py:44
  153.7 4.9 %collective-permute-start.16 = (bf16[32,6144]{1,0:T(8,128)(2,1)S(1)}, bf16[32,6144]{1,0:T(8,128)(2,1)S(1)}, u32[]{:S(2)}, u32[]{:S(2)}) collective-permute-start(bf16[32,6144]{1,0:T(8,128)(2,1)S(1)} %get-tuple-element.65), channel_id=1, source_target_pairs={{0,16},{8,72},{16,32},{24,88},{32,48},{40,104},{48,0},{56,120},{64... | collective-permute-start | bytes 1179656 | tf_op jit(solution)/shard_map/ppermute | solution.py:44
  160.6 7.6 %collective-permute-done.16 = bf16[32,6144]{1,0:T(8,128)(2,1)S(1)} collective-permute-done((bf16[32,6144]{1,0:T(8,128)(2,1)S(1)}, bf16[32,6144]{1,0:T(8,128)(2,1)S(1)}, u32[]{:S(2)}, u32[]{:S(2)}) %collective-permute-start.16) | collective-permute-done | bytes 393248 | tf_op jit(solution)/shard_map/ppermute | solution.py:44
  168.1 2.4 %collective-permute-done.18 = bf16[32,6144]{1,0:T(8,128)(2,1)S(1)} collective-permute-done((bf16[32,6144]{1,0:T(8,128)(2,1)S(1)}, bf16[32,6144]{1,0:T(8,128)(2,1)S(1)}, u32[]{:S(2)}, u32[]{:S(2)}) %collective-permute-start.18) | collective-permute-done | bytes 393248 | tf_op jit(solution)/shard_map/ppermute | solution.py:44
  171.6 7.3 %all-to-all-start.3 = ((bf16[8,32,768]{2,1,0:T(8,128)(2,1)}), bf16[8,32,768]{2,1,0:T(8,128)(2,1)S(1)}, u32[]{:S(2)}, u32[]{:S(2)}) async-start(bf16[8,32,768]{2,1,0:T(8,128)(2,1)} %bitcast.15), calls=%async_computation.3 | async-start | bytes 786432 | tf_op jit(solution)/shard_map/all_to_all | solution.py:366
  179.0 11.8 %all-to-all-done.3.back_ref = bf16[8,32,768]{2,1,0:T(8,128)(2,1)S(1)} async-done(((bf16[8,32,768]{2,1,0:T(8,128)(2,1)}), bf16[8,32,768]{2,1,0:T(8,128)(2,1)S(1)}, u32[]{:S(2)}, u32[]{:S(2)}) %all-to-all-start.3) | async-done | bytes 393248 | tf_op jit(solution)/shard_map/all_to_all | solution.py:366
  (69 shorter events, 25.0 us)
Async XLA Ops:
  0.0 29.0 %copy-start.9 = (f32[768]{0:T(1024)S(1)}, f32[768]{0:T(1024)}, u32[]{:S(2)}) copy-start(f32[768]{0:T(1024)} %param.17) | copy-start | bytes 9220
  0.0 36.1 %collective-permute-start = (bf16[288,6144]{1,0:T(8,128)(2,1)}, bf16[288,6144]{1,0:T(8,128)(2,1)}, u32[]{:S(2)}, u32[]{:S(2)}) collective-permute-start(bf16[288,6144]{1,0:T(8,128)(2,1)} %bitcast.16), channel_id=1, source_target_pairs={{0,8},{8,0},{16,24},{24,16},{32,40},{40,32},{48,56},{56,48},{64,72... | collective-permute-start | bytes 10616840 | tf_op jit(solution)/shard_map/ppermute | solution.py:310
  0.0 36.1 %collective-permute-start.1 = (bf16[288,6144]{1,0:T(8,128)(2,1)}, bf16[288,6144]{1,0:T(8,128)(2,1)}, u32[]{:S(2)}, u32[]{:S(2)}) collective-permute-start(bf16[288,6144]{1,0:T(8,128)(2,1)} %bitcast.20), channel_id=1, source_target_pairs={{0,8},{8,0},{16,24},{24,16},{32,40},{40,32},{48,56},{56,48},{64,72... | collective-permute-start | bytes 10616840 | tf_op jit(solution)/shard_map/ppermute | solution.py:311
  0.5 35.6 %collective-permute-start.2 = (bf16[288,6144]{1,0:T(8,128)(2,1)}, bf16[288,6144]{1,0:T(8,128)(2,1)}, u32[]{:S(2)}, u32[]{:S(2)}) collective-permute-start(bf16[288,6144]{1,0:T(8,128)(2,1)} %bitcast.24), channel_id=1, source_target_pairs={{0,8},{8,0},{16,24},{24,16},{32,40},{40,32},{48,56},{56,48},{64,72... | collective-permute-start | bytes 10616840 | tf_op jit(solution)/shard_map/ppermute | solution.py:312
  5.1 72.9 %copy-start.1 = (bf16[1,6144,288]{1,2,0:T(8,128)(2,1)S(1)}, bf16[1,6144,288]{1,2,0:T(8,128)(2,1)}, u32[]{:S(2)}) copy-start(bf16[1,6144,288]{1,2,0:T(8,128)(2,1)} %param.22) | copy-start | bytes 10616836
  5.1 15.7 %all-to-all-start = ((bf16[32,32,128]{2,1,0:T(8,128)(2,1)}), bf16[32,32,128]{2,1,0:T(8,128)(2,1)}, u32[]{:S(2)}, u32[]{:S(2)}) async-start(bf16[32,32,128]{2,1,0:T(8,128)(2,1)} %get-tuple-element.35), calls=%async_computation | async-start | bytes 524288 | tf_op jit(solution)/shard_map/all_to_all | solution.py:315
  22.7 13.5 %all-to-all-start.1 = ((bf16[32,32,128]{2,1,0:T(8,128)(2,1)}), bf16[32,32,128]{2,1,0:T(8,128)(2,1)}, u32[]{:S(2)}, u32[]{:S(2)}) async-start(bf16[32,32,128]{2,1,0:T(8,128)(2,1)} %copy-done.4), calls=%async_computation.1 | async-start | bytes 524288 | tf_op jit(solution)/shard_map/all_to_all | solution.py:318
  63.6 12.1 %collective-permute-start.3 = (bf16[32,6144]{1,0:T(8,128)(2,1)S(1)}, bf16[32,6144]{1,0:T(8,128)(2,1)S(1)}, u32[]{:S(2)}, u32[]{:S(2)}) collective-permute-start(bf16[32,6144]{1,0:T(8,128)(2,1)S(1)} %shard_map.121), channel_id=1, source_target_pairs={{0,48},{8,200},{16,0},{24,216},{32,16},{40,232},{48,32},{56,248},{... | collective-permute-start | bytes 1179656 | tf_op jit(solution)/shard_map/ppermute | solution.py:44
  65.0 10.7 %collective-permute-start.4 = (bf16[32,6144]{1,0:T(8,128)(2,1)S(1)}, bf16[32,6144]{1,0:T(8,128)(2,1)S(1)}, u32[]{:S(2)}, u32[]{:S(2)}) collective-permute-start(bf16[32,6144]{1,0:T(8,128)(2,1)S(1)} %shard_map.121), channel_id=1, source_target_pairs={{0,16},{8,72},{16,32},{24,88},{32,48},{40,104},{48,0},{56,120},{64... | collective-permute-start | bytes 1179656 | tf_op jit(solution)/shard_map/ppermute | solution.py:44
  65.7 10.0 %collective-permute-start.5 = (bf16[32,6144]{1,0:T(8,128)(2,1)S(1)}, bf16[32,6144]{1,0:T(8,128)(2,1)S(1)}, u32[]{:S(2)}, u32[]{:S(2)}) collective-permute-start(bf16[32,6144]{1,0:T(8,128)(2,1)S(1)} %shard_map.121), channel_id=1, source_target_pairs={{0,32},{8,136},{16,48},{24,152},{32,0},{40,168},{48,16},{56,184},{... | collective-permute-start | bytes 1179656 | tf_op jit(solution)/shard_map/ppermute | solution.py:44
  75.9 20.5 %collective-permute-start.6 = (bf16[128,6144]{1,0:T(8,128)(2,1)S(1)}, bf16[128,6144]{1,0:T(8,128)(2,1)S(1)}, u32[]{:S(2)}, u32[]{:S(2)}) collective-permute-start(bf16[128,6144]{1,0:T(8,128)(2,1)S(1)} %pad_maximum_fusion.1.refs_0_), channel_id=1, source_target_pairs={{0,192},{8,56},{16,208},{24,8},{32,224},{40,24},{48,240},{56,40},{... | collective-permute-start | bytes 4718600 | tf_op jit(solution)/shard_map/ppermute | solution.py:44
  77.1 21.6 %collective-permute-start.7 = (bf16[128,6144]{1,0:T(8,128)(2,1)S(1)}, bf16[128,6144]{1,0:T(8,128)(2,1)S(1)}, u32[]{:S(2)}, u32[]{:S(2)}) collective-permute-start(bf16[128,6144]{1,0:T(8,128)(2,1)S(1)} %pad_maximum_fusion.1.refs_0_), channel_id=1, source_target_pairs={{0,64},{8,24},{16,80},{24,40},{32,96},{40,56},{48,112},{56,8},{64,... | collective-permute-start | bytes 4718600 | tf_op jit(solution)/shard_map/ppermute | solution.py:44
  98.8 15.0 %collective-permute-start.8 = (bf16[128,3072]{1,0:T(8,128)(2,1)S(1)}, bf16[128,3072]{1,0:T(8,128)(2,1)S(1)}, u32[]{:S(2)}, u32[]{:S(2)}) collective-permute-start(bf16[128,3072]{1,0:T(8,128)(2,1)S(1)} %slice.22), channel_id=1, source_target_pairs={{0,192},{8,56},{16,208},{24,8},{32,224},{40,24},{48,240},{56,40},{... | collective-permute-start | bytes 2359304 | tf_op jit(solution)/shard_map/ppermute | solution.py:44
  98.9 14.9 %collective-permute-start.9 = (bf16[128,3072]{1,0:T(8,128)(2,1)S(1)}, bf16[128,3072]{1,0:T(8,128)(2,1)S(1)}, u32[]{:S(2)}, u32[]{:S(2)}) collective-permute-start(bf16[128,3072]{1,0:T(8,128)(2,1)S(1)} %slice.23), channel_id=1, source_target_pairs={{0,64},{8,24},{16,80},{24,40},{32,96},{40,56},{48,112},{56,8},{64,... | collective-permute-start | bytes 2359304 | tf_op jit(solution)/shard_map/ppermute | solution.py:44
  111.7 12.1 %collective-permute-start.10 = (bf16[128,3072]{1,0:T(8,128)(2,1)S(1)}, bf16[128,3072]{1,0:T(8,128)(2,1)S(1)}, u32[]{:S(2)}, u32[]{:S(2)}) collective-permute-start(bf16[128,3072]{1,0:T(8,128)(2,1)S(1)} %get-tuple-element.50), channel_id=1, source_target_pairs={{0,192},{8,56},{16,208},{24,8},{32,224},{40,24},{48,240},{56,40},{... | collective-permute-start | bytes 2359304 | tf_op jit(solution)/shard_map/ppermute | solution.py:44
  113.0 13.2 %collective-permute-start.11 = (bf16[128,3072]{1,0:T(8,128)(2,1)S(1)}, bf16[128,3072]{1,0:T(8,128)(2,1)S(1)}, u32[]{:S(2)}, u32[]{:S(2)}) collective-permute-start(bf16[128,3072]{1,0:T(8,128)(2,1)S(1)} %get-tuple-element.49), channel_id=1, source_target_pairs={{0,64},{8,24},{16,80},{24,40},{32,96},{40,56},{48,112},{56,8},{64,... | collective-permute-start | bytes 2359304 | tf_op jit(solution)/shard_map/ppermute | solution.py:44
  126.2 12.0 %collective-permute-start.14 = (bf16[128,3072]{1,0:T(8,128)(2,1)S(1)}, bf16[128,3072]{1,0:T(8,128)(2,1)S(1)}, u32[]{:S(2)}, u32[]{:S(2)}) collective-permute-start(bf16[128,3072]{1,0:T(8,128)(2,1)S(1)} %get-tuple-element.60), channel_id=1, source_target_pairs={{0,192},{8,56},{16,208},{24,8},{32,224},{40,24},{48,240},{56,40},{... | collective-permute-start | bytes 2359304 | tf_op jit(solution)/shard_map/ppermute | solution.py:44
  126.2 13.5 %collective-permute-start.12 = (bf16[128,3072]{1,0:T(8,128)(2,1)S(1)}, bf16[128,3072]{1,0:T(8,128)(2,1)S(1)}, u32[]{:S(2)}, u32[]{:S(2)}) collective-permute-start(bf16[128,3072]{1,0:T(8,128)(2,1)S(1)} %get-tuple-element.57), channel_id=1, source_target_pairs={{0,64},{8,24},{16,80},{24,40},{32,96},{40,56},{48,112},{56,8},{64,... | collective-permute-start | bytes 2359304 | tf_op jit(solution)/shard_map/ppermute | solution.py:44
  138.3 12.1 %collective-permute-start.15 = (bf16[128,3072]{1,0:T(8,128)(2,1)S(1)}, bf16[128,3072]{1,0:T(8,128)(2,1)S(1)}, u32[]{:S(2)}, u32[]{:S(2)}) collective-permute-start(bf16[128,3072]{1,0:T(8,128)(2,1)S(1)} %add_convert_fusion), channel_id=1, source_target_pairs={{0,192},{8,56},{16,208},{24,8},{32,224},{40,24},{48,240},{56,40},{... | collective-permute-start | bytes 2359304 | tf_op jit(solution)/shard_map/ppermute | solution.py:44
  139.8 13.3 %collective-permute-start.13 = (bf16[128,3072]{1,0:T(8,128)(2,1)S(1)}, bf16[128,3072]{1,0:T(8,128)(2,1)S(1)}, u32[]{:S(2)}, u32[]{:S(2)}) collective-permute-start(bf16[128,3072]{1,0:T(8,128)(2,1)S(1)} %add_convert_fusion.1), channel_id=1, source_target_pairs={{0,64},{8,24},{16,80},{24,40},{32,96},{40,56},{48,112},{56,8},{64,... | collective-permute-start | bytes 2359304 | tf_op jit(solution)/shard_map/ppermute | solution.py:44
  153.7 14.4 %collective-permute-start.16 = (bf16[32,6144]{1,0:T(8,128)(2,1)S(1)}, bf16[32,6144]{1,0:T(8,128)(2,1)S(1)}, u32[]{:S(2)}, u32[]{:S(2)}) collective-permute-start(bf16[32,6144]{1,0:T(8,128)(2,1)S(1)} %get-tuple-element.65), channel_id=1, source_target_pairs={{0,16},{8,72},{16,32},{24,88},{32,48},{40,104},{48,0},{56,120},{64... | collective-permute-start | bytes 1179656 | tf_op jit(solution)/shard_map/ppermute | solution.py:44
  158.6 9.5 %collective-permute-start.17 = (bf16[32,6144]{1,0:T(8,128)(2,1)S(1)}, bf16[32,6144]{1,0:T(8,128)(2,1)S(1)}, u32[]{:S(2)}, u32[]{:S(2)}) collective-permute-start(bf16[32,6144]{1,0:T(8,128)(2,1)S(1)} %get-tuple-element.67), channel_id=1, source_target_pairs={{0,48},{8,200},{16,0},{24,216},{32,16},{40,232},{48,32},{56,248},{... | collective-permute-start | bytes 1179656 | tf_op jit(solution)/shard_map/ppermute | solution.py:44
  158.6 12.0 %collective-permute-start.18 = (bf16[32,6144]{1,0:T(8,128)(2,1)S(1)}, bf16[32,6144]{1,0:T(8,128)(2,1)S(1)}, u32[]{:S(2)}, u32[]{:S(2)}) collective-permute-start(bf16[32,6144]{1,0:T(8,128)(2,1)S(1)} %get-tuple-element.66), channel_id=1, source_target_pairs={{0,32},{8,136},{16,48},{24,152},{32,0},{40,168},{48,16},{56,184},{... | collective-permute-start | bytes 1179656 | tf_op jit(solution)/shard_map/ppermute | solution.py:44
  171.6 19.2 %all-to-all-start.3 = ((bf16[8,32,768]{2,1,0:T(8,128)(2,1)}), bf16[8,32,768]{2,1,0:T(8,128)(2,1)S(1)}, u32[]{:S(2)}, u32[]{:S(2)}) async-start(bf16[8,32,768]{2,1,0:T(8,128)(2,1)} %bitcast.15), calls=%async_computation.3 | async-start | bytes 786432 | tf_op jit(solution)/shard_map/all_to_all | solution.py:366
  (10 other events, 127.3 us)
where the time goes:
time: 192 us
  waiting for transfers between devices  77.7 us (40%)
  starting transfers between devices  43.7 us (23%)
  Pallas kernels  37.3 us (19%)
  blocking collectives  23.8 us (12%)
  local copies, waits for them, and re-layouts  7.28 us (4%)
    ppermute x16, waiting for transfers between devices, send(): lax.ppermute(rows, 'ctx', chip_pairs(lambda core: along_x[(core + axis) %...  51.7 us
    pallas_call x3, Pallas kernels, expert(): pl.pallas_call(lambda *refs: expert_kernel(groups, *refs), out_shape=(jax...  29.2 us
    all_to_all x1, blocking collectives, body(): lax.all_to_all(sent, 'exp', split_axis=0, concat_axis=0, tiled=True)  23.8 us
    ppermute x16, starting transfers between devices, send(): lax.ppermute(rows, 'ctx', chip_pairs(lambda core: along_x[(core + axis) %...  22.3 us
    all_to_all x1, waiting for transfers between devices, body(): lax.all_to_all(summed, 'exp', split_axis=0, concat_axis=0, tiled=True)  11.8 us
    all_to_all x1, starting transfers between devices, body(): lax.all_to_all(pieces, 'ctx', split_axis=0, concat_axis=0, tiled=True)  7.97 us
    all_to_all x1, waiting for transfers between devices, body(): lax.all_to_all(pieces, 'ctx', split_axis=0, concat_axis=0, tiled=True)  7.73 us
    all_to_all x1, starting transfers between devices, body(): lax.all_to_all(summed, 'exp', split_axis=0, concat_axis=0, tiled=True)  7.3 us
  transfers between devices with their start and end apart: 22, of which 13 were waited for; matrix products, arithmetic and copies ran while one was open for 2% of the time, Pallas kernels for 17%

commit v1 on v0

--- a/solution.py
+++ b/solution.py
@@ -50,18 +50,18 @@
 
 def local_kernel(q_ref, k_ref, v_ref, rate_ref, piece_ref, inside_ref, decayed_ref, wide):
     length, width = q_ref.shape
-    heads = rate_ref.shape[1]
+    heads = rate_ref.shape[0]
     head = width // heads
     wide[...] = jnp.zeros_like(wide)
-    wide[:, :heads] = rate_ref[...]
+    wide[:heads] = rate_ref[...]
     rates = wide[...]
     row = lax.broadcasted_iota(jnp.int32, (length, length), 0)
     col = lax.broadcasted_iota(jnp.int32, (length, length), 1)
     causal = row >= col
     lower = causal.astype(F32)
-    cumulated = jnp.dot(lower, rates, precision=HIGHEST, preferred_element_type=F32)
+    cumulated = lax.dot_general(lower, rates, NT, precision=HIGHEST, preferred_element_type=F32)
     across = lax.dot_general(
-        rates, lower, (((0,), (1,)), ((), ())), precision=HIGHEST, preferred_element_type=F32
+        rates[:8], lower, NT, precision=HIGHEST, preferred_element_type=F32
     )
     total = cumulated[length - 1 : length, :]
     states = []
@@ -104,7 +104,7 @@
         ),
         in_specs=[whole()] * 4,
         out_specs=[whole()] * 3,
-        scratch_shapes=[pltpu.VMEM((length, 128), F32)],
+        scratch_shapes=[pltpu.VMEM((128, length), F32)],
         compiler_params=params(56),
     )(query, keys, values, log_decay)
 
@@ -205,21 +205,37 @@
 
 PACKED = 640
 CHUNK = 1536
-LIMIT = 18
-
-
-def expert_kernel(groups, *refs):
-    x_refs, refs = refs[:groups], refs[groups:]
-    up_refs, down_refs, refs = refs[:4], refs[4:6], refs[6:]
-    out_refs, sums = refs[:-1], refs[-1]
-    hidden = up_refs[0].shape[0]
-    width = x_refs[0].shape[1]
-    for at in range(0, width, CHUNK):
-        part = slice(at, at + CHUNK)
-        x = jnp.concatenate([ref[:, part] for ref in x_refs], axis=0)
-        for w, ref in enumerate(up_refs):
-            product = lax.dot_general(ref[:, part], x, NT, preferred_element_type=F32)
-            sums[w] = product if at == 0 else sums[w] + product
+LIMIT = 24
+
+
+def expert_kernel(groups, loads, *refs):
+    x_refs, refs = refs[: 2 * groups], refs[2 * groups :]
+    own_refs, other_refs, refs = refs[:3], refs[3:6], refs[6:]
+    out_refs, refs = refs[: 2 * groups], refs[2 * groups :]
+    copies = ()
+    if loads:
+        here_refs, refs, sems = refs[:3], refs[3:-1], refs[-1]
+        copies = [
+            pltpu.make_async_copy(other_refs[i], here_refs[i], sems.at[i]) for i in range(3)
+        ]
+        for copy in copies:
+            copy.start()
+        other_refs = here_refs
+    sums = refs[0]
+    hidden = own_refs[0].shape[0]
+    for pair, weights in enumerate((own_refs[:2], other_refs[:2])):
+        for w, ref in enumerate(weights):
+            if pair and loads:
+                copies[w].wait()
+            for at in range(0, FEATURES, CHUNK):
+                half, start = divmod(at, HALF)
+                x = [x_ref[:, start : start + CHUNK] for x_ref in x_refs[half::2]]
+                x = jnp.concatenate(x, axis=0)
+                product = lax.dot_general(
+                    ref[:, at : at + CHUNK], x, NT, preferred_element_type=F32
+                )
+                slot = 2 * pair + w
+                sums[slot] = product if at == 0 else sums[slot] + product
 
     rows = groups * GROUP
     blank = PACKED - 2 * hidden
@@ -227,32 +243,62 @@
     activated.append(jnp.zeros((blank, rows), F32))
     activated = jnp.transpose(jnp.concatenate(activated, axis=0)).astype(BF16)
 
+    if loads:
+        copies[2].wait()
     for at in range(0, FEATURES, CHUNK):
         half, start = divmod(at, HALF)
-        weights = [ref[:, at : at + CHUNK] for ref in down_refs]
+        weights = [ref[:, at : at + CHUNK] for ref in (own_refs[2], other_refs[2])]
         weights = jnp.concatenate(weights + [jnp.zeros((blank, CHUNK), BF16)], axis=0)
         product = jnp.dot(activated, weights, preferred_element_type=F32).astype(BF16)
         for g in range(groups):
             out_refs[2 * g + half][:, start : start + CHUNK] = product[g * GROUP : (g + 1) * GROUP]
 
 
-def expert(xs, ups, downs):
-    groups = len(xs)
-    hidden = ups[0].shape[0]
+def expert(xs, own, other, loads=False):
+    groups = len(xs) // 2
+    hidden = own[0].shape[0]
     rows = groups * GROUP
-    return pl.pallas_call(
-        lambda *refs: expert_kernel(groups, *refs),
-        out_shape=(jax.ShapeDtypeStruct((GROUP, HALF), BF16),) * (2 * groups),
-        in_specs=[whole()] * (groups + 6),
-        out_specs=(whole(),) * (2 * groups),
-        scratch_shapes=[pltpu.VMEM((4, hidden, rows), F32)],
+    out_shape = (jax.ShapeDtypeStruct((GROUP, HALF), BF16),) * (2 * groups)
+    scratch = [pltpu.VMEM((4, hidden, rows), F32)]
+    if loads:
+        out_shape += tuple(jax.ShapeDtypeStruct(w.shape, w.dtype) for w in other)
+        scratch.append(pltpu.SemaphoreType.DMA((3,)))
+    out = pl.pallas_call(
+        lambda *refs: expert_kernel(groups, loads, *refs),
+        out_shape=out_shape,
+        in_specs=[whole()] * (2 * groups + 3) + [whole(pl.ANY if loads else pltpu.VMEM)] * 3,
+        out_specs=(whole(),) * len(out_shape),
+        scratch_shapes=scratch,
         compiler_params=params(LIMIT),
         cost_estimate=pl.CostEstimate(
             flops=2 * 256 * FEATURES * 6 * hidden,
             bytes_accessed=FEATURES * 6 * hidden * 2,
             transcendentals=0,
         ),
-    )(*xs, *ups, *downs)
+    )(*xs, *own, *other)
+    return (out[: 2 * groups], out[2 * groups :]) if loads else out
+
+
+def total_kernel(own_ref, *refs):
+    out_ref = refs[-1]
+    parts, _, width = out_ref.shape
+    for i in range(parts):
+        part = slice(i * width, (i + 1) * width)
+        total = own_ref[0, :, part]
+        for ref in refs[:-1]:
+            total += ref[:, part].astype(F32)
+        out_ref[i] = total.astype(BF16)
+
+
+def total_rows(own, arrived, experts):
+    return pl.pallas_call(
+        total_kernel,
+        grid=(1,),
+        out_shape=jax.ShapeDtypeStruct((experts, SLOTS, FEATURES // experts), BF16),
+        in_specs=[pl.BlockSpec((1, SLOTS, FEATURES), lambda i: (0, 0, 0))] + [whole()] * 3,
+        out_specs=whole(),
+        compiler_params=params(16),
+    )(own, *arrived)
 
 
 def mix_kernel(back_ref, lead_ref, next_ref, gates_ref, hidden_ref, out_ref):
@@ -282,7 +328,10 @@
     before = send(block, FIRST, 1)
     opposite = send(block, FIRST, 2)
     blocks = (block, after, before, opposite)
-    return jnp.concatenate(blocks, axis=0)
+    return tuple(
+        jnp.concatenate([b[:, i * HALF : (i + 1) * HALF] for b in blocks], axis=0)
+        for i in range(2)
+    )
 
 
 def added(*terms):
@@ -311,7 +360,7 @@
     other_up = lax.ppermute(up, "ctx", sibling)
     other_down = lax.ppermute(down, "ctx", sibling)
 
-    pieces, inside, decayed = attend_locally(query, keys, values, log_decay, blocks)
+    pieces, inside, decayed = attend_locally(query, keys, values, log_decay.T, blocks)
     pieces = lax.all_to_all(pieces, "ctx", split_axis=0, concat_axis=0, tiled=True)
     place = lax.axis_index("ctx").astype(jnp.int32).reshape(1)
     states = scan_states(place, pieces)
@@ -324,30 +373,29 @@
     )
     arrived = lax.all_to_all(sent, "exp", split_axis=0, concat_axis=0, tiled=True)
     rows = norm_rows(arrived, moe_gain.reshape(1, -1))
-    ups, downs = (gate, up, other_gate, other_up), (down, other_down)
+    mine, other = (gate, up, down), (other_gate, other_up, other_down)
 
     own = gather_first(rows)
-    after = send(own, SECOND, -1)
-    before = send(own, SECOND, 1)
-    here_one, here_two = expert((own,), ups, downs)
-    after, before, here_one, here_two = lax.optimization_barrier(
-        (after, before, here_one, here_two)
-    )
-    opposite_one = send(after[:, :HALF], SECOND, -1)
-    opposite_two = send(before[:, HALF:], SECOND, 1)
-    to_after_one, to_after_two, to_before_one, to_before_two = expert((after, before), ups, downs)
+    after_one = send(own[0], SECOND, -1)
+    before_two = send(own[1], SECOND, 1)
+    after_two = send(own[1], SECOND, -1)
+    before_one = send(own[0], SECOND, 1)
+    opposite = (send(after_one, SECOND, -1), send(before_two, SECOND, 1))
+    beside, other = expert((after_one, after_two, before_one, before_two), mine, other, True)
+    opposite, beside = lax.optimization_barrier((opposite, beside))
+    to_after_one, to_after_two, to_before_one, to_before_two = beside
     from_after_one = send(to_before_one, SECOND, -1)
     from_before_two = send(to_after_two, SECOND, 1)
-    opposite = jnp.concatenate([opposite_one, opposite_two], axis=1)
-    opposite, to_after_one, to_after_two, to_before_one, to_before_two = lax.optimization_barrier(
-        (opposite, to_after_one, to_after_two, to_before_one, to_before_two)
-    )
-    far_one, far_two = expert((opposite,), ups, downs)
-    far_one, far_two, from_after_one, from_before_two = lax.optimization_barrier(
-        (far_one, far_two, from_after_one, from_before_two)
-    )
-    through_after = send(far_one, SECOND, 1)
-    through_before = send(far_two, SECOND, -1)
+    far = expert(opposite, mine, other)
+    far_one, far_two = far
+    through = (send(far_one, SECOND, 1), send(far_two, SECOND, -1))
+    own, from_after_one, from_before_two = lax.optimization_barrier(
+        (own, from_after_one, from_before_two)
+    )
+    here = expert(own, mine, other)
+    through, here = lax.optimization_barrier((through, here))
+    through_after, through_before = through
+    here_one, here_two = here
     from_before_one = send(added(to_after_one, through_after).astype(BF16), SECOND, 1)
     from_after_two = send(added(to_before_two, through_before).astype(BF16), SECOND, -1)
     sums = jnp.concatenate(
@@ -361,8 +409,7 @@
     from_before = send(rounded[1], FIRST, 1)
     from_after = send(rounded[2], FIRST, -1)
     from_opposite = send(rounded[3], FIRST, 2)
-    summed = added(sums[0], from_before, from_after, from_opposite).astype(BF16)
-    summed = jnp.transpose(summed.reshape(SLOTS, experts, -1), (1, 0, 2))
+    summed = total_rows(sums, (from_before, from_after, from_opposite), experts)
     returned = lax.all_to_all(summed, "exp", split_axis=0, concat_axis=0, tiled=True)
     return mix(returned, lead, follow, gate_weights, hidden)
 

time: 192 us -> 179 us (0.932)
  Pallas kernels: 37.3 us -> 28.6 us
  local copies, waits for them, and re-layouts: 7.28 us -> 2.34 us
  waiting for transfers between devices: 77.7 us -> 73.2 us
  starting transfers between devices: 43.7 us -> 47.6 us
    pallas_call x3 -> x4, Pallas kernels: 29.2 us -> 20.1 us  [the longest x3 19.1 us: expert(): pl.pallas_call(lambda *refs: expert_kernel(groups, loads, *refs), out_sha...]
    ppermute x16 -> x18, starting transfers between devices: 22.3 us -> 30.2 us  [send(): lax.ppermute(rows, 'ctx', chip_pairs(lambda core: along_x[(core + axis) %...]
    ppermute x16 -> x18, waiting for transfers between devices: 51.7 us -> 47.2 us  [send(): lax.ppermute(rows, 'ctx', chip_pairs(lambda core: along_x[(core + axis) %...]
    unnamed x27 -> x24, local copies, waits for them, and re-layouts: 5.71 us -> 1.57 us
    all_to_all x1, starting transfers between devices: 7.3 us -> 3.45 us  [body(): lax.all_to_all(summed, 'exp', split_axis=0, concat_axis=0, tiled=True)]
  transfers between devices with their start and end apart: 22 -> 24, of which waited for: 13 -> 14; matrix products, arithmetic and copies ran while one was open for 2% -> 1% of each run, Pallas kernels for 17% -> 13%
where the time goes in v1:
time: 179 us; the launch traced here: 177 us
  waiting for transfers between devices  73.2 us (41%)
  starting transfers between devices  47.6 us (27%)
  Pallas kernels  28.6 us (16%)
  blocking collectives  23.8 us (13%)
  local copies, waits for them, and re-layouts  2.34 us (1%)
    ppermute x18, waiting for transfers between devices, send(): lax.ppermute(rows, 'ctx', chip_pairs(lambda core: along_x[(core + axis) %...  47.2 us
    ppermute x18, starting transfers between devices, send(): lax.ppermute(rows, 'ctx', chip_pairs(lambda core: along_x[(core + axis) %...  30.2 us
    all_to_all x1, blocking collectives, body(): lax.all_to_all(sent, 'exp', split_axis=0, concat_axis=0, tiled=True)  23.8 us
    pallas_call x3, Pallas kernels, expert(): pl.pallas_call(lambda *refs: expert_kernel(groups, loads, *refs), out_sha...  19.1 us
    all_to_all x1, waiting for transfers between devices, body(): lax.all_to_all(summed, 'exp', split_axis=0, concat_axis=0, tiled=True)  11.7 us
    all_to_all x1, waiting for transfers between devices, body(): lax.all_to_all(pieces, 'ctx', split_axis=0, concat_axis=0, tiled=True)  7.73 us
    all_to_all x1, starting transfers between devices, body(): lax.all_to_all(pieces, 'ctx', split_axis=0, concat_axis=0, tiled=True)  7.71 us
    all_to_all x1, waiting for transfers between devices, body(): lax.all_to_all(states, 'ctx', split_axis=0, concat_axis=0, tiled=True)  6.53 us
  transfers between devices with their start and end apart: 24, of which 14 were waited for; matrix products, arithmetic and copies ran while one was open for 1% of the time, Pallas kernels for 13%

profile of v1, /device:TPU:2, one launch (start us, length us, event | category | flops | bytes accessed | tf_op | source)
XLA Modules:
  0.0 177.3 jit_solution(13802966369654573620)
XLA Ops:
  0.6 3.5 %shard_map.118 = (bf16[32,32,128]{2,1,0:T(8,128)(2,1)}, f32[112,768]{1,0:T(8,128)}, bf16[112,768]{1,0:T(8,128)(2,1)}) custom-call(bf16[112,768]{1,0:T(8,128)(2,1)} %q_ref.1, bf16[112,768]{1,0:T(8,128)(2,1)} %k_ref.1, bf16[112,768]{1,0:T(8,128)(2,1)} %v_ref.1, f32[6,112]{1,0:T(8,128)} %bitcast.32), custom_call_target="tpu_custom_call" | custom-call | tf_op jit(solution)/shard_map/pallas_call | solution.py:98
  4.1 7.7 %all-to-all-start = ((bf16[32,32,128]{2,1,0:T(8,128)(2,1)}), bf16[32,32,128]{2,1,0:T(8,128)(2,1)}, u32[]{:S(2)}, u32[]{:S(2)}) async-start(bf16[32,32,128]{2,1,0:T(8,128)(2,1)} %get-tuple-element.41), calls=%async_computation | async-start | bytes 524288 | tf_op jit(solution)/shard_map/all_to_all | solution.py:364
  11.8 7.7 %all-to-all-done.pieces_ref = bf16[32,32,128]{2,1,0:T(8,128)(2,1)} async-done(((bf16[32,32,128]{2,1,0:T(8,128)(2,1)}), bf16[32,32,128]{2,1,0:T(8,128)(2,1)}, u32[]{:S(2)}, u32[]{:S(2)}) %all-to-all-start) | async-done | bytes 262176 | tf_op jit(solution)/shard_map/all_to_all | solution.py:364
  21.4 5.6 %all-to-all-start.1 = ((bf16[32,32,128]{2,1,0:T(8,128)(2,1)}), bf16[32,32,128]{2,1,0:T(8,128)(2,1)}, u32[]{:S(2)}, u32[]{:S(2)}) async-start(bf16[32,32,128]{2,1,0:T(8,128)(2,1)} %copy-done.3), calls=%async_computation.1 | async-start | bytes 524288 | tf_op jit(solution)/shard_map/all_to_all | solution.py:367
  28.3 6.5 %all-to-all-done.1.state_ref = bf16[32,32,128]{2,1,0:T(8,128)(2,1)} async-done(((bf16[32,32,128]{2,1,0:T(8,128)(2,1)}), bf16[32,32,128]{2,1,0:T(8,128)(2,1)}, u32[]{:S(2)}, u32[]{:S(2)}) %all-to-all-start.1) | async-done | bytes 262176 | tf_op jit(solution)/shard_map/all_to_all | solution.py:367
  34.9 2.8 %shard_map.120 = (bf16[112,768]{1,0:T(8,128)(2,1)}, bf16[8,32,768]{2,1,0:T(8,128)(2,1)}, bf16[112,256]{1,0:T(8,128)(2,1)}, bf16[112,256]{1,0:T(8,128)(2,1)}) custom-call(bf16[32,32,128]{2,1,0:T(8,128)(2,1)} %all-to-all-done.1.state_ref, f32[112,768]{1,0:T(8,128)} %get-tuple-element.43.inside_ref, bf16[112,768]{1,0:T(8,128)(2,1)} %get-tuple-element.44.decayed_ref, ...), custom_call_target="tpu_custom_call" | custom-call | tf_op jit(solution)/shard_map/pallas_call | solution.py:172
  37.6 23.8 %all_to_all.20.rows_ref = bf16[8,32,768]{2,1,0:T(8,128)(2,1)S(1)} all-to-all(bf16[8,32,768]{2,1,0:T(8,128)(2,1)} %get-tuple-element.45), channel_id=1, replica_groups=mesh['ctx'=32,'exp'=8] {'exp'}, dimensions={0} | all-to-all | bytes 786432 | tf_op jit(solution)/shard_map/all_to_all | solution.py:374
  66.5 7.2 %collective-permute-done.3 = bf16[32,6144]{1,0:T(8,128)(2,1)S(1)} collective-permute-done((bf16[32,6144]{1,0:T(8,128)(2,1)S(1)}, bf16[32,6144]{1,0:T(8,128)(2,1)S(1)}, u32[]{:S(2)}, u32[]{:S(2)}) %collective-permute-start.3) | collective-permute-done | bytes 393248 | tf_op jit(solution)/shard_map/ppermute | solution.py:44
  79.4 7.8 %collective-permute-done.8.refs_3_ = bf16[128,3072]{1,0:T(8,128)(2,1)S(1)} collective-permute-done((bf16[128,3072]{1,0:T(8,128)(2,1)S(1)}, bf16[128,3072]{1,0:T(8,128)(2,1)S(1)}, u32[]{:S(2)}, u32[]{:S(2)}) %collective-permute-start.8) | collective-permute-done | bytes 786464 | tf_op jit(solution)/shard_map/ppermute | solution.py:44
  87.2 3.4 %collective-permute-start.7 = (bf16[128,3072]{1,0:T(8,128)(2,1)S(1)}, bf16[128,3072]{1,0:T(8,128)(2,1)S(1)}, u32[]{:S(2)}, u32[]{:S(2)}) collective-permute-start(bf16[128,3072]{1,0:T(8,128)(2,1)S(1)} %collective-permute-done.6.refs_0_), channel_id=1, source_target_pairs={{0,192},{8,56},{16,208},{24,8},{32,224},{40,24},{48,240},{56,40},{... | collective-permute-start | bytes 2359304 | tf_op jit(solution)/shard_map/ppermute | solution.py:44
  90.5 4.7 %collective-permute-done.10.refs_1_ = bf16[128,3072]{1,0:T(8,128)(2,1)S(1)} collective-permute-done((bf16[128,3072]{1,0:T(8,128)(2,1)S(1)}, bf16[128,3072]{1,0:T(8,128)(2,1)S(1)}, u32[]{:S(2)}, u32[]{:S(2)}) %collective-permute-start.10) | collective-permute-done | bytes 786464 | tf_op jit(solution)/shard_map/ppermute | solution.py:44
  95.6 8.8 %shard_map.122 = (bf16[128,3072]{1,0:T(8,128)(2,1)S(1)}, bf16[128,3072]{1,0:T(8,128)(2,1)S(1)}, bf16[128,3072]{1,0:T(8,128)(2,1)S(1)}, bf16[128,3072]{1,0:T(8,12...) custom-call(bf16[128,3072]{1,0:T(8,128)(2,1)S(1)} %collective-permute-done., ...), custom_call_target="tpu_custom_call" | custom-call | flops 5435817984 | bytes 21233664 | tf_op jit(solution)/shard_map/pallas_call | solution.py:266
  104.4 3.5 %collective-permute-start.14 = (bf16[128,3072]{1,0:T(8,128)(2,1)S(1)}, bf16[128,3072]{1,0:T(8,128)(2,1)S(1)}, u32[]{:S(2)}, u32[]{:S(2)}) collective-permute-start(bf16[128,3072]{1,0:T(8,128)(2,1)S(1)} %get-tuple-element.60), channel_id=1, source_target_pairs={{0,192},{8,56},{16,208},{24,8},{32,224},{40,24},{48,240},{56,40},{... | collective-permute-start | bytes 2359304 | tf_op jit(solution)/shard_map/ppermute | solution.py:44
  107.9 5.2 %shard_map.123 = (bf16[128,3072]{1,0:T(8,128)(2,1)S(1)}, bf16[128,3072]{1,0:T(8,128)(2,1)S(1)}) custom-call(bf16[128,3072]{1,0:T(8,128)(2,1)S(1)} %collective-permute-done.7.refs_0_, bf16[128,3072]{1,0:T(8,128)(2,1)S(1)} %collective-permute-done.9.refs_1_, bf16[288,6144]{1,0:T(8,128)(2,1)S(1)} %bitcast.19, bf16[288,6144]{1,0:T(8,128)(2,1)S(1)} %bitcast.23, ...), custom_call_target="tpu_custom_call" | custom-call | flops 5435817984 | bytes 21233664 | tf_op jit(solution)/shard_map/pallas_call | solution.py:266
  113.2 3.5 %collective-permute-start.13 = (bf16[128,3072]{1,0:T(8,128)(2,1)S(1)}, bf16[128,3072]{1,0:T(8,128)(2,1)S(1)}, u32[]{:S(2)}, u32[]{:S(2)}) collective-permute-start(bf16[128,3072]{1,0:T(8,128)(2,1)S(1)} %get-tuple-element.59), channel_id=1, source_target_pairs={{0,192},{8,56},{16,208},{24,8},{32,224},{40,24},{48,240},{56,40},{... | collective-permute-start | bytes 2359304 | tf_op jit(solution)/shard_map/ppermute | solution.py:44
  117.4 3.7 %collective-permute-done.15 = bf16[128,3072]{1,0:T(8,128)(2,1)S(1)} collective-permute-done((bf16[128,3072]{1,0:T(8,128)(2,1)S(1)}, bf16[128,3072]{1,0:T(8,128)(2,1)S(1)}, u32[]{:S(2)}, u32[]{:S(2)}) %collective-permute-start.15) | collective-permute-done | bytes 786464 | tf_op jit(solution)/shard_map/ppermute | solution.py:44
  121.1 5.2 %shard_map.124 = (bf16[128,3072]{1,0:T(8,128)(2,1)S(1)}, bf16[128,3072]{1,0:T(8,128)(2,1)S(1)}) custom-call(bf16[128,3072]{1,0:T(8,128)(2,1)S(1)} %pad_maximum_fusion.1.refs_0_, bf16[128,3072]{1,0:T(8,128)(2,1)S(1)} %pad_maximum_fusion.2.refs_1_, bf16[288,6144]{1,0:T(8,128)(2,1)S(1)} %bitcast.20, bf16[288,6144]{1,0:T(8,128)(2,1)S(1)} %bitcast.24, ...), custom_call_target="tpu_custom_call" | custom-call | flops 5435817984 | bytes 21233664 | tf_op jit(solution)/shard_map/pallas_call | solution.py:266
  126.3 3.2 %collective-permute-done.12 = bf16[128,3072]{1,0:T(8,128)(2,1)S(1)} collective-permute-done((bf16[128,3072]{1,0:T(8,128)(2,1)S(1)}, bf16[128,3072]{1,0:T(8,128)(2,1)S(1)}, u32[]{:S(2)}, u32[]{:S(2)}) %collective-permute-start.12) | collective-permute-done | bytes 786464 | tf_op jit(solution)/shard_map/ppermute | solution.py:44
  130.0 3.3 %collective-permute-start.17 = (bf16[128,3072]{1,0:T(8,128)(2,1)S(1)}, bf16[128,3072]{1,0:T(8,128)(2,1)S(1)}, u32[]{:S(2)}, u32[]{:S(2)}) collective-permute-start(bf16[128,3072]{1,0:T(8,128)(2,1)S(1)} %add_convert_fusion), channel_id=1, source_target_pairs={{0,192},{8,56},{16,208},{24,8},{32,224},{40,24},{48,240},{56,40},{... | collective-permute-start | bytes 2359304 | tf_op jit(solution)/shard_map/ppermute | solution.py:44
  133.3 9.7 %collective-permute-done.16 = bf16[128,3072]{1,0:T(8,128)(2,1)S(1)} collective-permute-done((bf16[128,3072]{1,0:T(8,128)(2,1)S(1)}, bf16[128,3072]{1,0:T(8,128)(2,1)S(1)}, u32[]{:S(2)}, u32[]{:S(2)}) %collective-permute-start.16) | collective-permute-done | bytes 786464 | tf_op jit(solution)/shard_map/ppermute | solution.py:44
  150.3 3.6 %collective-permute-done.18.refs_0_ = bf16[32,6144]{1,0:T(8,128)(2,1)S(1)} collective-permute-done((bf16[32,6144]{1,0:T(8,128)(2,1)S(1)}, bf16[32,6144]{1,0:T(8,128)(2,1)S(1)}, u32[]{:S(2)}, u32[]{:S(2)}) %collective-permute-start.18) | collective-permute-done | bytes 393248 | tf_op jit(solution)/shard_map/ppermute | solution.py:44
  154.7 5.5 %collective-permute-done.20.refs_2_ = bf16[32,6144]{1,0:T(8,128)(2,1)S(1)} collective-permute-done((bf16[32,6144]{1,0:T(8,128)(2,1)S(1)}, bf16[32,6144]{1,0:T(8,128)(2,1)S(1)}, u32[]{:S(2)}, u32[]{:S(2)}) %collective-permute-start.20) | collective-permute-done | bytes 393248 | tf_op jit(solution)/shard_map/ppermute | solution.py:44
  161.1 3.5 %all-to-all-start.3 = ((bf16[8,32,768]{2,1,0:T(8,128)(2,1)}), bf16[8,32,768]{2,1,0:T(8,128)(2,1)S(1)}, u32[]{:S(2)}, u32[]{:S(2)}) async-start(bf16[8,32,768]{2,1,0:T(8,128)(2,1)} %shard_map.125), calls=%async_computation.3 | async-start | bytes 786432 | tf_op jit(solution)/shard_map/all_to_all | solution.py:413
  164.7 11.7 %all-to-all-done.3.back_ref = bf16[8,32,768]{2,1,0:T(8,128)(2,1)S(1)} async-done(((bf16[8,32,768]{2,1,0:T(8,128)(2,1)}), bf16[8,32,768]{2,1,0:T(8,128)(2,1)S(1)}, u32[]{:S(2)}, u32[]{:S(2)}) %all-to-all-start.3) | async-done | bytes 393248 | tf_op jit(solution)/shard_map/all_to_all | solution.py:413
  (72 shorter events, 26.1 us)
Async XLA Ops:
  0.0 34.8 %collective-permute-start = (bf16[288,6144]{1,0:T(8,128)(2,1)}, bf16[288,6144]{1,0:T(8,128)(2,1)}, u32[]{:S(2)}, u32[]{:S(2)}) collective-permute-start(bf16[288,6144]{1,0:T(8,128)(2,1)} %bitcast.17), channel_id=1, source_target_pairs={{0,8},{8,0},{16,24},{24,16},{32,40},{40,32},{48,56},{56,48},{64,72... | collective-permute-start | bytes 10616840 | tf_op jit(solution)/shard_map/ppermute | solution.py:359
  0.0 34.8 %collective-permute-start.1 = (bf16[288,6144]{1,0:T(8,128)(2,1)}, bf16[288,6144]{1,0:T(8,128)(2,1)}, u32[]{:S(2)}, u32[]{:S(2)}) collective-permute-start(bf16[288,6144]{1,0:T(8,128)(2,1)} %bitcast.21), channel_id=1, source_target_pairs={{0,8},{8,0},{16,24},{24,16},{32,40},{40,32},{48,56},{56,48},{64,72... | collective-permute-start | bytes 10616840 | tf_op jit(solution)/shard_map/ppermute | solution.py:360
  0.5 34.3 %collective-permute-start.2 = (bf16[288,6144]{1,0:T(8,128)(2,1)}, bf16[288,6144]{1,0:T(8,128)(2,1)}, u32[]{:S(2)}, u32[]{:S(2)}) collective-permute-start(bf16[288,6144]{1,0:T(8,128)(2,1)} %bitcast.25), channel_id=1, source_target_pairs={{0,8},{8,0},{16,24},{24,16},{32,40},{40,32},{48,56},{56,48},{64,72... | collective-permute-start | bytes 10616840 | tf_op jit(solution)/shard_map/ppermute | solution.py:361
  4.1 15.5 %all-to-all-start = ((bf16[32,32,128]{2,1,0:T(8,128)(2,1)}), bf16[32,32,128]{2,1,0:T(8,128)(2,1)}, u32[]{:S(2)}, u32[]{:S(2)}) async-start(bf16[32,32,128]{2,1,0:T(8,128)(2,1)} %get-tuple-element.41), calls=%async_computation | async-start | bytes 524288 | tf_op jit(solution)/shard_map/all_to_all | solution.py:364
  21.4 13.5 %all-to-all-start.1 = ((bf16[32,32,128]{2,1,0:T(8,128)(2,1)}), bf16[32,32,128]{2,1,0:T(8,128)(2,1)}, u32[]{:S(2)}, u32[]{:S(2)}) async-start(bf16[32,32,128]{2,1,0:T(8,128)(2,1)} %copy-done.3), calls=%async_computation.1 | async-start | bytes 524288 | tf_op jit(solution)/shard_map/all_to_all | solution.py:367
  61.6 12.1 %collective-permute-start.3 = (bf16[32,6144]{1,0:T(8,128)(2,1)S(1)}, bf16[32,6144]{1,0:T(8,128)(2,1)S(1)}, u32[]{:S(2)}, u32[]{:S(2)}) collective-permute-start(bf16[32,6144]{1,0:T(8,128)(2,1)S(1)} %shard_map.121), channel_id=1, source_target_pairs={{0,48},{8,200},{16,0},{24,216},{32,16},{40,232},{48,32},{56,248},{... | collective-permute-start | bytes 1179656 | tf_op jit(solution)/shard_map/ppermute | solution.py:44
  63.0 10.8 %collective-permute-start.4 = (bf16[32,6144]{1,0:T(8,128)(2,1)S(1)}, bf16[32,6144]{1,0:T(8,128)(2,1)S(1)}, u32[]{:S(2)}, u32[]{:S(2)}) collective-permute-start(bf16[32,6144]{1,0:T(8,128)(2,1)S(1)} %shard_map.121), channel_id=1, source_target_pairs={{0,16},{8,72},{16,32},{24,88},{32,48},{40,104},{48,0},{56,120},{64... | collective-permute-start | bytes 1179656 | tf_op jit(solution)/shard_map/ppermute | solution.py:44
  63.7 10.0 %collective-permute-start.5 = (bf16[32,6144]{1,0:T(8,128)(2,1)S(1)}, bf16[32,6144]{1,0:T(8,128)(2,1)S(1)}, u32[]{:S(2)}, u32[]{:S(2)}) collective-permute-start(bf16[32,6144]{1,0:T(8,128)(2,1)S(1)} %shard_map.121), channel_id=1, source_target_pairs={{0,32},{8,136},{16,48},{24,152},{32,0},{40,168},{48,16},{56,184},{... | collective-permute-start | bytes 1179656 | tf_op jit(solution)/shard_map/ppermute | solution.py:44
  73.9 13.3 %collective-permute-start.8 = (bf16[128,3072]{1,0:T(8,128)(2,1)S(1)}, bf16[128,3072]{1,0:T(8,128)(2,1)S(1)}, u32[]{:S(2)}, u32[]{:S(2)}) collective-permute-start(bf16[128,3072]{1,0:T(8,128)(2,1)S(1)} %pad_maximum_fusion.2.refs_1_), channel_id=1, source_target_pairs={{0,64},{8,24},{16,80},{24,40},{32,96},{40,56},{48,112},{56,8},{64,... | collective-permute-start | bytes 2359304 | tf_op jit(solution)/shard_map/ppermute | solution.py:44
  74.7 12.5 %collective-permute-start.6 = (bf16[128,3072]{1,0:T(8,128)(2,1)S(1)}, bf16[128,3072]{1,0:T(8,128)(2,1)S(1)}, u32[]{:S(2)}, u32[]{:S(2)}) collective-permute-start(bf16[128,3072]{1,0:T(8,128)(2,1)S(1)} %pad_maximum_fusion.1.refs_0_), channel_id=1, source_target_pairs={{0,192},{8,56},{16,208},{24,8},{32,224},{40,24},{48,240},{56,40},{... | collective-permute-start | bytes 2359304 | tf_op jit(solution)/shard_map/ppermute | solution.py:44
  77.3 17.9 %collective-permute-start.10 = (bf16[128,3072]{1,0:T(8,128)(2,1)S(1)}, bf16[128,3072]{1,0:T(8,128)(2,1)S(1)}, u32[]{:S(2)}, u32[]{:S(2)}) collective-permute-start(bf16[128,3072]{1,0:T(8,128)(2,1)S(1)} %pad_maximum_fusion.2.refs_1_), channel_id=1, source_target_pairs={{0,192},{8,56},{16,208},{24,8},{32,224},{40,24},{48,240},{56,40},{... | collective-permute-start | bytes 2359304 | tf_op jit(solution)/shard_map/ppermute | solution.py:44
  77.4 18.2 %collective-permute-start.11 = (bf16[128,3072]{1,0:T(8,128)(2,1)S(1)}, bf16[128,3072]{1,0:T(8,128)(2,1)S(1)}, u32[]{:S(2)}, u32[]{:S(2)}) collective-permute-start(bf16[128,3072]{1,0:T(8,128)(2,1)S(1)} %pad_maximum_fusion.1.refs_0_), channel_id=1, source_target_pairs={{0,64},{8,24},{16,80},{24,40},{32,96},{40,56},{48,112},{56,8},{64,... | collective-permute-start | bytes 2359304 | tf_op jit(solution)/shard_map/ppermute | solution.py:44
  87.2 17.2 %collective-permute-start.9 = (bf16[128,3072]{1,0:T(8,128)(2,1)S(1)}, bf16[128,3072]{1,0:T(8,128)(2,1)S(1)}, u32[]{:S(2)}, u32[]{:S(2)}) collective-permute-start(bf16[128,3072]{1,0:T(8,128)(2,1)S(1)} %collective-permute-done.8.refs_3_), channel_id=1, source_target_pairs={{0,64},{8,24},{16,80},{24,40},{32,96},{40,56},{48,112},{56,8},{64,... | collective-permute-start | bytes 2359304 | tf_op jit(solution)/shard_map/ppermute | solution.py:44
  87.2 17.2 %collective-permute-start.7 = (bf16[128,3072]{1,0:T(8,128)(2,1)S(1)}, bf16[128,3072]{1,0:T(8,128)(2,1)S(1)}, u32[]{:S(2)}, u32[]{:S(2)}) collective-permute-start(bf16[128,3072]{1,0:T(8,128)(2,1)S(1)} %collective-permute-done.6.refs_0_), channel_id=1, source_target_pairs={{0,192},{8,56},{16,208},{24,8},{32,224},{40,24},{48,240},{56,40},{... | collective-permute-start | bytes 2359304 | tf_op jit(solution)/shard_map/ppermute | solution.py:44
  104.4 13.0 %collective-permute-start.14 = (bf16[128,3072]{1,0:T(8,128)(2,1)S(1)}, bf16[128,3072]{1,0:T(8,128)(2,1)S(1)}, u32[]{:S(2)}, u32[]{:S(2)}) collective-permute-start(bf16[128,3072]{1,0:T(8,128)(2,1)S(1)} %get-tuple-element.60), channel_id=1, source_target_pairs={{0,192},{8,56},{16,208},{24,8},{32,224},{40,24},{48,240},{56,40},{... | collective-permute-start | bytes 2359304 | tf_op jit(solution)/shard_map/ppermute | solution.py:44
  107.9 13.2 %collective-permute-start.15 = (bf16[128,3072]{1,0:T(8,128)(2,1)S(1)}, bf16[128,3072]{1,0:T(8,128)(2,1)S(1)}, u32[]{:S(2)}, u32[]{:S(2)}) collective-permute-start(bf16[128,3072]{1,0:T(8,128)(2,1)S(1)} %get-tuple-element.61), channel_id=1, source_target_pairs={{0,64},{8,24},{16,80},{24,40},{32,96},{40,56},{48,112},{56,8},{64,... | collective-permute-start | bytes 2359304 | tf_op jit(solution)/shard_map/ppermute | solution.py:44
  113.1 16.4 %collective-permute-start.12 = (bf16[128,3072]{1,0:T(8,128)(2,1)S(1)}, bf16[128,3072]{1,0:T(8,128)(2,1)S(1)}, u32[]{:S(2)}, u32[]{:S(2)}) collective-permute-start(bf16[128,3072]{1,0:T(8,128)(2,1)S(1)} %get-tuple-element.58), channel_id=1, source_target_pairs={{0,64},{8,24},{16,80},{24,40},{32,96},{40,56},{48,112},{56,8},{64,... | collective-permute-start | bytes 2359304 | tf_op jit(solution)/shard_map/ppermute | solution.py:44
  113.2 16.3 %collective-permute-start.13 = (bf16[128,3072]{1,0:T(8,128)(2,1)S(1)}, bf16[128,3072]{1,0:T(8,128)(2,1)S(1)}, u32[]{:S(2)}, u32[]{:S(2)}) collective-permute-start(bf16[128,3072]{1,0:T(8,128)(2,1)S(1)} %get-tuple-element.59), channel_id=1, source_target_pairs={{0,192},{8,56},{16,208},{24,8},{32,224},{40,24},{48,240},{56,40},{... | collective-permute-start | bytes 2359304 | tf_op jit(solution)/shard_map/ppermute | solution.py:44
  129.7 13.3 %collective-permute-start.16 = (bf16[128,3072]{1,0:T(8,128)(2,1)S(1)}, bf16[128,3072]{1,0:T(8,128)(2,1)S(1)}, u32[]{:S(2)}, u32[]{:S(2)}) collective-permute-start(bf16[128,3072]{1,0:T(8,128)(2,1)S(1)} %add_convert_fusion.1), channel_id=1, source_target_pairs={{0,64},{8,24},{16,80},{24,40},{32,96},{40,56},{48,112},{56,8},{64,... | collective-permute-start | bytes 2359304 | tf_op jit(solution)/shard_map/ppermute | solution.py:44
  130.0 13.3 %collective-permute-start.17 = (bf16[128,3072]{1,0:T(8,128)(2,1)S(1)}, bf16[128,3072]{1,0:T(8,128)(2,1)S(1)}, u32[]{:S(2)}, u32[]{:S(2)}) collective-permute-start(bf16[128,3072]{1,0:T(8,128)(2,1)S(1)} %add_convert_fusion), channel_id=1, source_target_pairs={{0,192},{8,56},{16,208},{24,8},{32,224},{40,24},{48,240},{56,40},{... | collective-permute-start | bytes 2359304 | tf_op jit(solution)/shard_map/ppermute | solution.py:44
  144.2 9.7 %collective-permute-start.18 = (bf16[32,6144]{1,0:T(8,128)(2,1)S(1)}, bf16[32,6144]{1,0:T(8,128)(2,1)S(1)}, u32[]{:S(2)}, u32[]{:S(2)}) collective-permute-start(bf16[32,6144]{1,0:T(8,128)(2,1)S(1)} %get-tuple-element.79), channel_id=1, source_target_pairs={{0,16},{8,72},{16,32},{24,88},{32,48},{40,104},{48,0},{56,120},{64... | collective-permute-start | bytes 1179656 | tf_op jit(solution)/shard_map/ppermute | solution.py:44
  146.9 7.8 %collective-permute-start.19 = (bf16[32,6144]{1,0:T(8,128)(2,1)S(1)}, bf16[32,6144]{1,0:T(8,128)(2,1)S(1)}, u32[]{:S(2)}, u32[]{:S(2)}) collective-permute-start(bf16[32,6144]{1,0:T(8,128)(2,1)S(1)} %get-tuple-element.78), channel_id=1, source_target_pairs={{0,48},{8,200},{16,0},{24,216},{32,16},{40,232},{48,32},{56,248},{... | collective-permute-start | bytes 1179656 | tf_op jit(solution)/shard_map/ppermute | solution.py:44
  148.2 11.9 %collective-permute-start.20 = (bf16[32,6144]{1,0:T(8,128)(2,1)S(1)}, bf16[32,6144]{1,0:T(8,128)(2,1)S(1)}, u32[]{:S(2)}, u32[]{:S(2)}) collective-permute-start(bf16[32,6144]{1,0:T(8,128)(2,1)S(1)} %get-tuple-element.77), channel_id=1, source_target_pairs={{0,32},{8,136},{16,48},{24,152},{32,0},{40,168},{48,16},{56,184},{... | collective-permute-start | bytes 1179656 | tf_op jit(solution)/shard_map/ppermute | solution.py:44
  161.1 15.3 %all-to-all-start.3 = ((bf16[8,32,768]{2,1,0:T(8,128)(2,1)}), bf16[8,32,768]{2,1,0:T(8,128)(2,1)S(1)}, u32[]{:S(2)}, u32[]{:S(2)}) async-start(bf16[8,32,768]{2,1,0:T(8,128)(2,1)} %shard_map.125), calls=%async_computation.3 | async-start | bytes 786432 | tf_op jit(solution)/shard_map/all_to_all | solution.py:413
  (11 other events, 333.8 us)

commit v2 on v1

v2 whole, which is shorter than its diff:
```python
import jax
import jax.numpy as jnp
from jax import lax
from jax.experimental import pallas as pl
from jax.experimental.pallas import tpu as pltpu
from jax.sharding import PartitionSpec as P

STABILIZER = 1e-05
HIGHEST = lax.Precision.HIGHEST
F32 = jnp.float32
BF16 = jnp.bfloat16
NT = (((1,), (1,)), ((), ()))
TN = (((0,), (0,)), ((), ()))
SIDE = 4
CORES = 2
SLOTS = 32
GROUP = SIDE * SLOTS
PIECE = 24
FEATURES = 6144
HALF = FEATURES // 2


def whole(memory=pltpu.VMEM):
    return pl.BlockSpec(memory_space=memory)


def params(mib):
    return pltpu.CompilerParams(vmem_limit_bytes=mib << 20)


def chip_pairs(step, flip=0):
    pairs = []
    for y in range(SIDE):
        for x in range(SIDE):
            for core in range(CORES):
                dy, dx = step(core)
                to = (y + dy) % SIDE * SIDE + (x + dx) % SIDE
                pairs.append(((y * SIDE + x) * CORES + core, to * CORES + (core + flip) % CORES))
    return pairs


def send(rows, axis, distance):
    along_x = ((0, distance), (distance, 0))
    return lax.ppermute(rows, "ctx", chip_pairs(lambda core: along_x[(core + axis) % CORES]))


def silu(v):
    return v / (1.0 + jnp.exp(-v))


def lower_triangle(length):
    row = lax.broadcasted_iota(jnp.int32, (length, length), 0)
    col = lax.broadcasted_iota(jnp.int32, (length, length), 1)
    return row >= col


def widened(rate_ref, wide):
    wide[...] = jnp.zeros_like(wide)
    wide[: rate_ref.shape[0]] = rate_ref[...]
    return wide[...]


def summary_kernel(k_ref, v_ref, rate_ref, piece_ref, wide):
    length, width = k_ref.shape
    heads = rate_ref.shape[0]
    head = width // heads
    lower = lower_triangle(length).astype(F32)
    cumulated = lax.dot_general(
        lower, widened(rate_ref, wide), NT, precision=HIGHEST, preferred_element_type=F32
    )
    total = cumulated[length - 1 : length, :]
    tails = jnp.exp(cumulated - total)
    states = []
    for h in range(heads):
        part = slice(h * head, (h + 1) * head)
        ka = silu(k_ref[:, part].astype(F32)) * tails[:, h : h + 1]
        states.append(
            lax.dot_general(ka.astype(BF16), v_ref[:, part], TN, preferred_element_type=F32)
        )
    first = total.astype(BF16).astype(F32)
    second = (total - first).astype(BF16).astype(F32)
    third = total - first - second
    line = lax.broadcasted_iota(jnp.int32, (8, total.shape[1]), 0)
    notes = jnp.where(line == 0, first, jnp.where(line == 1, second, jnp.where(line == 2, third, 0.0)))
    count = piece_ref.shape[0]
    state = jnp.concatenate(states, axis=0).reshape(count, PIECE, head)
    notes = jnp.broadcast_to(notes[None], (count,) + notes.shape)
    piece_ref[...] = jnp.concatenate([state, notes], axis=1).astype(BF16)


def summarize(keys, values, rates, count):
    return pl.pallas_call(
        summary_kernel,
        out_shape=jax.ShapeDtypeStruct((count, PIECE + 8, 128), BF16),
        in_specs=[whole()] * 3,
        out_specs=whole(),
        scratch_shapes=[pltpu.VMEM((128, keys.shape[0]), F32)],
        compiler_params=params(56),
    )(keys, values, rates)


def local_kernel(q_ref, k_ref, v_ref, rate_ref, routes_ref, inside_ref, decayed_ref, lead_ref, next_ref, wide):
    length, width = q_ref.shape
    heads = rate_ref.shape[0]
    head = width // heads
    causal = lower_triangle(length)
    lower = causal.astype(F32)
    rates = widened(rate_ref, wide)
    cumulated = lax.dot_general(lower, rates, NT, precision=HIGHEST, preferred_element_type=F32)
    across = lax.dot_general(
        rates[:8], lower, NT, precision=HIGHEST, preferred_element_type=F32
    )
    for h in range(heads):
        part = slice(h * head, (h + 1) * head)
        qa = silu(q_ref[:, part].astype(F32))
        ka = silu(k_ref[:, part].astype(F32))
        down = cumulated[:, h : h + 1]
        spread = jnp.where(causal, down - across[h : h + 1, :], 0.0)
        weights = jnp.where(causal, jnp.exp(-spread), 0.0)
        scores = lax.dot_general(qa.astype(BF16), ka.astype(BF16), NT, preferred_element_type=F32)
        inside_ref[:, part] = jnp.dot(
            (scores * weights).astype(BF16), v_ref[:, part], preferred_element_type=F32
        )
        decayed_ref[:, part] = (qa * jnp.exp(-down)).astype(BF16)

    lane = lax.broadcasted_iota(jnp.int32, (length, 128), 1)
    one = (lane == routes_ref[:, 0:1]).astype(F32)
    two = (lane == routes_ref[:, 1:2]).astype(F32)
    row = lax.broadcasted_iota(jnp.int32, (length, length), 0)
    col = lax.broadcasted_iota(jnp.int32, (length, length), 1)
    earlier = (row > col).astype(BF16)
    before = jnp.dot(earlier, (one + two).astype(BF16), preferred_element_type=F32)
    slot_one = jnp.sum(before * one, axis=-1, keepdims=True).astype(jnp.int32)
    slot_two = jnp.sum(before * two, axis=-1, keepdims=True).astype(jnp.int32)
    target = lax.broadcasted_iota(jnp.int32, lead_ref.shape, 1)
    lead = target == routes_ref[:, 0:1] * SLOTS + slot_one
    follow = target == routes_ref[:, 1:2] * SLOTS + slot_two
    lead_ref[...] = lead.astype(F32).astype(BF16)
    next_ref[...] = follow.astype(F32).astype(BF16)


def attend_locally(query, keys, values, rates, routes, experts):
    length, width = query.shape
    return pl.pallas_call(
        local_kernel,
        out_shape=(
            jax.ShapeDtypeStruct((length, width), F32),
            jax.ShapeDtypeStruct((length, width), BF16),
            jax.ShapeDtypeStruct((length, experts * SLOTS), BF16),
            jax.ShapeDtypeStruct((length, experts * SLOTS), BF16),
        ),
        in_specs=[whole()] * 5,
        out_specs=[whole()] * 4,
        scratch_shapes=[pltpu.VMEM((128, length), F32)],
        compiler_params=params(56),
        cost_estimate=pl.CostEstimate(
            flops=2 * 6 * 2 * length * length * width, bytes_accessed=2 << 20, transcendentals=0
        ),
    )(query, keys, values, rates, routes)


def scan_kernel(place_ref, pieces_ref, out_ref):
    count, rows, lanes = pieces_ref.shape
    pieces = pieces_ref[...].astype(F32)
    notes = pieces[:, PIECE:]
    total = notes[:, 0:1] + notes[:, 1:2] + notes[:, 2:3]
    row = lax.broadcasted_iota(jnp.int32, (PIECE, lanes), 0) + place_ref[0] * PIECE
    own = lax.shift_right_logical(row, 7) == lax.broadcasted_iota(jnp.int32, (PIECE, lanes), 1)
    decay = jnp.sum(jnp.where(own[None], jnp.exp(-total), 0.0), axis=-1, keepdims=True)
    state = jnp.zeros((PIECE, lanes), F32)
    blank = jnp.zeros((rows - PIECE, lanes), F32)
    for i in range(count):
        out_ref[i] = jnp.concatenate([state, blank], axis=0).astype(BF16)
        state = decay[i] * state + pieces[i, :PIECE]


def scan_states(place, pieces):
    return pl.pallas_call(
        scan_kernel,
        out_shape=jax.ShapeDtypeStruct(pieces.shape, BF16),
        in_specs=[whole(pltpu.SMEM), whole()],
        out_specs=whole(),
        compiler_params=params(56),
    )(place, pieces)


def hidden_kernel(
    state_ref, inside_ref, decayed_ref, stream_ref, gain_ref, lead_ref, next_ref, hidden_ref, sent_ref
):
    width = stream_ref.shape[1]
    head = 128
    state = state_ref[...].astype(F32)[:, :PIECE].reshape(width, head).astype(BF16)
    placing = lead_ref[...] + next_ref[...]
    parts, rows, _ = sent_ref.shape
    for h in range(width // head):
        part = slice(h * head, (h + 1) * head)
        carried = jnp.dot(decayed_ref[:, part], state[part], preferred_element_type=F32)
        attended = inside_ref[:, part] + carried
        scale = lax.rsqrt(jnp.mean(attended * attended, axis=-1, keepdims=True) + STABILIZER)
        hidden = stream_ref[:, part].astype(F32) + attended * scale * gain_ref[:, part]
        hidden = hidden.astype(BF16)
        hidden_ref[:, part] = hidden
        sent = lax.dot_general(placing, hidden, TN, preferred_element_type=F32)
        sent_ref[:, :, part] = sent.astype(BF16).reshape(parts, rows, head)


def finish_attention(state, inside, decayed, stream, gain, lead, follow, experts):
    length, width = stream.shape
    return pl.pallas_call(
        hidden_kernel,
        out_shape=(
            jax.ShapeDtypeStruct((length, width), BF16),
            jax.ShapeDtypeStruct((experts, SLOTS, width), BF16),
        ),
        in_specs=[whole()] * 7,
        out_specs=[whole()] * 2,
        compiler_params=params(56),
    )(state, inside, decayed, stream, gain, lead, follow)


def norm_kernel(rows_ref, gain_ref, out_ref):
    parts, _, width = rows_ref.shape
    rows = [rows_ref[i].astype(F32) for i in range(parts)]
    squares = sum(jnp.sum(r * r, axis=-1, keepdims=True) for r in rows)
    scale = lax.rsqrt(squares / (parts * width) + STABILIZER)
    for i, r in enumerate(rows):
        part = slice(i * width, (i + 1) * width)
        out_ref[:, part] = (r * scale * gain_ref[:, part]).astype(BF16)


def norm_rows(rows, gain):
    return pl.pallas_call(
        norm_kernel,
        out_shape=jax.ShapeDtypeStruct((SLOTS, FEATURES), BF16),
        in_specs=[whole()] * 2,
        out_specs=whole(),
        compiler_params=params(16),
    )(rows, gain)


PACKED = 640
CHUNK = 1536
LIMIT = 24


def load_kernel(*refs):
    count = len(refs) // 2
    sems = refs[-1]
    copies = [pltpu.make_async_copy(refs[i], refs[count + i], sems.at[i]) for i in range(count)]
    for copy in copies:
        copy.start()
    for copy in copies:
        copy.wait()


def load(weights):
    count = len(weights)
    return pl.pallas_call(
        load_kernel,
        out_shape=tuple(jax.ShapeDtypeStruct(w.shape, w.dtype) for w in weights),
        in_specs=[whole(pl.ANY)] * count,
        out_specs=(whole(),) * count,
        scratch_shapes=[pltpu.SemaphoreType.DMA((count,))],
        compiler_params=params(16),
        cost_estimate=pl.CostEstimate(
            flops=0, bytes_accessed=2 * sum(w.size for w in weights), transcendentals=0
        ),
    )(*weights)


def expert_kernel(layout, count, *refs):
    x_refs, refs = refs[:count], refs[count:]
    weights, refs = refs[:6], refs[6:]
    out_refs, sums = refs[:-1], refs[-1]
    groups = len(layout)
    own_refs, other_refs = weights[:3], weights[3:]
    hidden = own_refs[0].shape[0]
    for slot, ref in enumerate(own_refs[:2] + other_refs[:2]):
        for at in range(0, FEATURES, CHUNK):
            half, start = divmod(at, HALF)
            x = []
            for group in layout:
                for piece in group:
                    index, offset = piece[half]
                    x.append(x_refs[index][:, offset + start : offset + start + CHUNK])
            x = jnp.concatenate(x, axis=0)
            product = lax.dot_general(ref[:, at : at + CHUNK], x, NT, preferred_element_type=F32)
            sums[slot] = product if at == 0 else sums[slot] + product

    rows = groups * GROUP
    blank = PACKED - 2 * hidden
    activated = [silu(sums[2 * w]) * sums[2 * w + 1] for w in range(2)]
    activated.append(jnp.zeros((blank, rows), F32))
    activated = jnp.transpose(jnp.concatenate(activated, axis=0)).astype(BF16)

    for at in range(0, FEATURES, CHUNK):
        half, start = divmod(at, HALF)
        weights = [ref[:, at : at + CHUNK] for ref in (own_refs[2], other_refs[2])]
        weights = jnp.concatenate(weights + [jnp.zeros((blank, CHUNK), BF16)], axis=0)
        product = jnp.dot(activated, weights, preferred_element_type=F32).astype(BF16)
        for g in range(groups):
            out_refs[2 * g + half][:, start : start + CHUNK] = product[g * GROUP : (g + 1) * GROUP]


def expert(groups, own, other):
    xs, layout = [], []
    for group in groups:
        pieces = []
        for piece in group:
            if isinstance(piece, tuple):
                pieces.append(((len(xs), 0), (len(xs) + 1, 0)))
                xs += piece
            else:
                pieces.append(((len(xs), 0), (len(xs), HALF)))
                xs.append(piece)
        layout.append(pieces)
    hidden = own[0].shape[0]
    rows = len(groups) * GROUP
    outs = 2 * len(groups)
    return pl.pallas_call(
        lambda *refs: expert_kernel(layout, len(xs), *refs),
        out_shape=(jax.ShapeDtypeStruct((GROUP, HALF), BF16),) * outs,
        in_specs=[whole()] * (len(xs) + 6),
        out_specs=(whole(),) * outs,
        scratch_shapes=[pltpu.VMEM((4, hidden, rows), F32)],
        compiler_params=params(LIMIT),
        cost_estimate=pl.CostEstimate(
            flops=2 * 256 * FEATURES * 6 * hidden,
            bytes_accessed=FEATURES * 6 * hidden * 2,
            transcendentals=0,
        ),
    )(*xs, *own, *other)


def meet_kernel(here_one, here_two, a_one, a_two, b_one, b_two, own_ref, *out_refs):
    for i, refs in enumerate(((here_one, a_one, b_one), (here_two, a_two, b_two))):
        part = slice(i * HALF, (i + 1) * HALF)
        for block in range(SIDE):
            rows = slice(block * SLOTS, (block + 1) * SLOTS)
            total = sum(ref[rows].astype(F32) for ref in refs)
            if block == 0:
                own_ref[:, part] = total
            else:
                out_refs[block - 1][:, part] = total.astype(BF16)


def meet(*terms):
    block = jax.ShapeDtypeStruct((SLOTS, FEATURES), BF16)
    return pl.pallas_call(
        meet_kernel,
        out_shape=(jax.ShapeDtypeStruct((SLOTS, FEATURES), F32), block, block, block),
        in_specs=[whole()] * 6,
        out_specs=(whole(),) * 4,
        compiler_params=params(16),
    )(*terms)


def total_kernel(own_ref, *refs):
    out_ref = refs[-1]
    parts, _, width = out_ref.shape
    for i in range(parts):
        part = slice(i * width, (i + 1) * width)
        total = own_ref[:, part]
        for ref in refs[:-1]:
            total += ref[:, part].astype(F32)
        out_ref[i] = total.astype(BF16)


def total_rows(own, arrived, experts):
    return pl.pallas_call(
        total_kernel,
        out_shape=jax.ShapeDtypeStruct((experts, SLOTS, FEATURES // experts), BF16),
        in_specs=[whole()] * 4,
        out_specs=whole(),
        compiler_params=params(16),
    )(own, *arrived)


def mix_kernel(back_ref, lead_ref, next_ref, gates_ref, hidden_ref, out_ref):
    rows = back_ref[...].reshape(lead_ref.shape[1], out_ref.shape[1])
    one = jnp.dot(lead_ref[...], rows, preferred_element_type=F32)
    two = jnp.dot(next_ref[...], rows, preferred_element_type=F32)
    gates = gates_ref[...]
    moe = gates[:, 0:1] * one + gates[:, 1:2] * two
    out_ref[...] = (hidden_ref[...].astype(F32) + moe).astype(BF16)


def mix(back, lead, follow, gates, hidden):
    return pl.pallas_call(
        mix_kernel,
        out_shape=jax.ShapeDtypeStruct(hidden.shape, BF16),
        in_specs=[whole()] * 5,
        out_specs=whole(),
        compiler_params=params(16),
    )(back, lead, follow, gates, hidden)


FIRST, SECOND = 0, 1


def neighbours(block, axis):
    return send(block, axis, -1), send(block, axis, 1)


def relayed(after, before, axis):
    return send(after[:, :HALF], axis, -1), send(before[:, HALF:], axis, 1)


def added(*terms):
    return sum(t.astype(F32) for t in terms)


def body(
    query,
    keys,
    values,
    stream,
    log_decay,
    attn_gain,
    routes,
    gate_weights,
    moe_gain,
    w_gate,
    w_up,
    w_down,
):
    experts = w_gate.shape[0] * lax.axis_size("exp")
    blocks = lax.axis_size("ctx")
    gate, up, down = w_gate[0].T, w_up[0].T, w_down[0]
    sibling = chip_pairs(lambda core: (0, 0), 1)
    other_gate = lax.ppermute(gate, "ctx", sibling)
    other_up = lax.ppermute(up, "ctx", sibling)
    other_down = lax.ppermute(down, "ctx", sibling)

    rates = log_decay.T
    pieces = summarize(keys, values, rates, blocks)
    pieces = lax.all_to_all(pieces, "ctx", split_axis=0, concat_axis=0, tiled=True)
    place = lax.axis_index("ctx").astype(jnp.int32).reshape(1)
    states = scan_states(place, pieces)
    states = lax.all_to_all(states, "ctx", split_axis=0, concat_axis=0, tiled=True)
    states, other_gate, other_up, other_down = lax.optimization_barrier(
        (states, other_gate, other_up, other_down)
    )
    inside, decayed, lead, follow = attend_locally(query, keys, values, rates, routes, experts)
    hidden, sent = finish_attention(
        states, inside, decayed, stream, attn_gain.reshape(1, -1), lead, follow, experts
    )
    arrived = lax.all_to_all(sent, "exp", split_axis=0, concat_axis=0, tiled=True)
    rows = norm_rows(arrived, moe_gain.reshape(1, -1))
    mine, other = (gate, up, down), (other_gate, other_up, other_down)

    rows, other = lax.optimization_barrier((rows, other))
    after, before = neighbours(rows, FIRST)
    after, before, other = lax.optimization_barrier((after, before, load(other)))
    near = jnp.concatenate([rows, after, before], axis=0)
    opposite = jnp.concatenate(relayed(after, before, FIRST), axis=1)
    near_after, near_before = neighbours(near, SECOND)
    last_after, last_before = neighbours(opposite, SECOND)
    near_far = relayed(near_after, near_before, SECOND)
    last_far = relayed(last_after, last_before, SECOND)
    beside = expert(
        ((near_after, last_after), (near_before, last_before)), mine, other
    )
    near_far, last_far, beside = lax.optimization_barrier((near_far, last_far, beside))
    to_after_one, to_after_two, to_before_one, to_before_two = beside
    from_after_one = send(to_before_one, SECOND, -1)
    from_before_two = send(to_after_two, SECOND, 1)
    far_one, far_two = expert(((near_far, last_far),), mine, other)
    through = (send(far_one, SECOND, 1), send(far_two, SECOND, -1))
    near, from_after_one, from_before_two = lax.optimization_barrier(
        (near, from_after_one, from_before_two)
    )
    here = expert(((near, opposite),), mine, other)
    through, here = lax.optimization_barrier((through, here))
    through_after, through_before = through
    here_one, here_two = here
    from_before_one = send(added(to_after_one, through_after).astype(BF16), SECOND, 1)
    from_after_two = send(added(to_before_two, through_before).astype(BF16), SECOND, -1)
    kept, to_after, to_before, to_opposite = meet(
        here_one, here_two, from_after_one, from_after_two, from_before_one, from_before_two
    )
    from_opposite = send(to_opposite, FIRST, 2)
    from_before = send(to_after, FIRST, 1)
    from_after = send(to_before, FIRST, -1)
    summed = total_rows(kept, (from_before, from_after, from_opposite), experts)
    returned = lax.all_to_all(summed, "exp", split_axis=0, concat_axis=0, tiled=True)
    return mix(returned, lead, follow, gate_weights, hidden)


def solution(mesh):
    return jax.shard_map(
        body,
        mesh=mesh,
        in_specs=(
            P("ctx", "exp"),
            P("ctx", "exp"),
            P("ctx", "exp"),
            P("ctx", "exp"),
            P("ctx", "exp"),
            P("exp"),
            P("ctx", None),
            P("ctx", None),
            P(),
            P("exp", None, "ctx"),
            P("exp", None, "ctx"),
            P("exp", "ctx", None),
        ),
        out_specs=P("ctx", "exp"),
        check_vma=False,
    )
```

time: 179 us -> 174 us (0.972)
  waiting for transfers between devices: 73.2 us -> 68.9 us
  Pallas kernels: 28.6 us -> 32.7 us
  starting transfers between devices: 47.6 us -> 43.6 us
    ppermute x18 -> x21, starting transfers between devices: 30.2 us -> 25.9 us  [send(): lax.ppermute(rows, 'ctx', chip_pairs(lambda core: along_x[(core + axis) %...]
    pallas_call x5 -> x8, Pallas kernels: 23.5 us -> 27.1 us  [the longest x3 16.8 us: expert(): pl.pallas_call(lambda *refs: expert_kernel(layout, len(xs), *refs), out_s...]
    all_to_all x1, waiting for transfers between devices: 6.53 us -> 3.69 us  [body(): lax.all_to_all(states, 'ctx', split_axis=0, concat_axis=0, tiled=True)]
    ppermute x18 -> x21, waiting for transfers between devices: 47.2 us -> 46.3 us  [send(): lax.ppermute(rows, 'ctx', chip_pairs(lambda core: along_x[(core + axis) %...]
  transfers between devices with their start and end apart: 24 -> 27, of which waited for: 14 -> 18; matrix products, arithmetic and copies ran while one was open for 1% -> 1% of each run, Pallas kernels for 13% -> 16%
where the time goes in v2:
time: 174 us; the launch traced here: 171 us
  waiting for transfers between devices  68.9 us (40%)
  starting transfers between devices  43.6 us (25%)
  Pallas kernels  32.7 us (19%)
  blocking collectives  23.8 us (14%)
    ppermute x21, waiting for transfers between devices, send(): lax.ppermute(rows, 'ctx', chip_pairs(lambda core: along_x[(core + axis) %...  46.3 us
    ppermute x21, starting transfers between devices, send(): lax.ppermute(rows, 'ctx', chip_pairs(lambda core: along_x[(core + axis) %...  25.9 us
    all_to_all x1, blocking collectives, body(): lax.all_to_all(sent, 'exp', split_axis=0, concat_axis=0, tiled=True)  23.8 us
    pallas_call x3, Pallas kernels, expert(): pl.pallas_call(lambda *refs: expert_kernel(layout, len(xs), *refs), out_s...  16.8 us
    all_to_all x1, waiting for transfers between devices, body(): lax.all_to_all(summed, 'exp', split_axis=0, concat_axis=0, tiled=True)  11.2 us
    all_to_all x1, waiting for transfers between devices, body(): lax.all_to_all(pieces, 'ctx', split_axis=0, concat_axis=0, tiled=True)  7.73 us
    all_to_all x1, starting transfers between devices, body(): lax.all_to_all(pieces, 'ctx', split_axis=0, concat_axis=0, tiled=True)  7.71 us
    all_to_all x1, starting transfers between devices, body(): lax.all_to_all(states, 'ctx', split_axis=0, concat_axis=0, tiled=True)  5.9 us
  transfers between devices with their start and end apart: 27, of which 18 were waited for; matrix products, arithmetic and copies ran while one was open for 1% of the time, Pallas kernels for 16%

profile of v2, /device:TPU:2, one launch (start us, length us, event | category | flops | bytes accessed | tf_op | source)
XLA Modules:
  0.0 171.2 jit_solution(12565893415633448500)
XLA Ops:
  3.0 7.7 %all-to-all-start = ((bf16[32,32,128]{2,1,0:T(8,128)(2,1)}), bf16[32,32,128]{2,1,0:T(8,128)(2,1)}, u32[]{:S(2)}, u32[]{:S(2)}) async-start(bf16[32,32,128]{2,1,0:T(8,128)(2,1)} %shard_map.118), calls=%async_computation | async-start | bytes 524288 | tf_op jit(solution)/shard_map/all_to_all | solution.py:437
  10.7 7.7 %all-to-all-done.pieces_ref = bf16[32,32,128]{2,1,0:T(8,128)(2,1)} async-done(((bf16[32,32,128]{2,1,0:T(8,128)(2,1)}), bf16[32,32,128]{2,1,0:T(8,128)(2,1)}, u32[]{:S(2)}, u32[]{:S(2)}) %all-to-all-start) | async-done | bytes 262176 | tf_op jit(solution)/shard_map/all_to_all | solution.py:437
  20.3 5.9 %all-to-all-start.1 = ((bf16[32,32,128]{2,1,0:T(8,128)(2,1)}), bf16[32,32,128]{2,1,0:T(8,128)(2,1)}, u32[]{:S(2)}, u32[]{:S(2)}) async-start(bf16[32,32,128]{2,1,0:T(8,128)(2,1)} %shard_map.119), calls=%async_computation.1 | async-start | bytes 524288 | tf_op jit(solution)/shard_map/all_to_all | solution.py:440
  27.6 2.7 %shard_map.120 = (f32[112,768]{1,0:T(8,128)}, bf16[112,768]{1,0:T(8,128)(2,1)}, bf16[112,256]{1,0:T(8,128)(2,1)}, bf16[112,256]{1,0:T(8,128)(2,1)}) custom-call(bf16[112,768]{1,0:T(8,128)(2,1)} %q_ref.1, bf16[112,768]{1,0:T(8,128)(2,1)} %k_ref.3, bf16[112,768]{1,0:T(8,128)(2,1)} %v_ref.3, f32[6,112]{1,0:T(8,128)} %bitcast.24, s32[112,2]{1,0:T(8,128)} %copy.13.routes_ref), custom_call_target="tpu_custom_call" | custom-call | flops 231211008 | bytes 2097152 | tf_op jit(solution)/shard_map/pallas_call | solution.py:144
  30.3 3.7 %all-to-all-done.1.state_ref = bf16[32,32,128]{2,1,0:T(8,128)(2,1)} async-done(((bf16[32,32,128]{2,1,0:T(8,128)(2,1)}), bf16[32,32,128]{2,1,0:T(8,128)(2,1)}, u32[]{:S(2)}, u32[]{:S(2)}) %all-to-all-start.1) | async-done | bytes 262176 | tf_op jit(solution)/shard_map/all_to_all | solution.py:440
  36.5 23.8 %all_to_all.20.rows_ref = bf16[8,32,768]{2,1,0:T(8,128)(2,1)S(1)} all-to-all(bf16[8,32,768]{2,1,0:T(8,128)(2,1)} %get-tuple-element.59), channel_id=1, replica_groups=mesh['ctx'=32,'exp'=8] {'exp'}, dimensions={0} | all-to-all | bytes 786432 | tf_op jit(solution)/shard_map/all_to_all | solution.py:448
  62.6 3.7 %shard_map.123 = (bf16[288,6144]{1,0:T(8,128)(2,1)S(1)}, bf16[288,6144]{1,0:T(8,128)(2,1)S(1)}, bf16[288,6144]{1,0:T(8,128)(2,1)S(1)}) custom-call(bf16[288,6144]{1,0:T(8,128)(2,1)S(1)} %collective-permute-done.refs_0_, bf16[288,6144]{1,0:T(8,128)(2,1)} %collective-permute-done.1.refs_1_, bf16[288,6144]{1,0:T(8,128)(2,1)} %collective-permute-done.2.refs_2_), custom_call_target="tpu_custom_call" | custom-call | bytes 10616832 | tf_op jit(solution)/shard_map/pallas_call | solution.py:258
  69.7 2.7 %collective-permute-start.9 = (bf16[32,3072]{1,0:T(8,128)(2,1)S(1)}, bf16[32,3072]{1,0:T(8,128)(2,1)S(1)}, u32[]{:S(2)}, u32[]{:S(2)}) collective-permute-start(bf16[32,3072]{1,0:T(8,128)(2,1)S(1)} %slice.20), channel_id=1, source_target_pairs={{0,48},{8,200},{16,0},{24,216},{32,16},{40,232},{48,32},{56,248},{... | collective-permute-start | bytes 589832 | tf_op jit(solution)/shard_map/ppermute | solution.py:44
  74.7 3.1 %collective-permute-done.9 = bf16[32,3072]{1,0:T(8,128)(2,1)S(1)} collective-permute-done((bf16[32,3072]{1,0:T(8,128)(2,1)S(1)}, bf16[32,3072]{1,0:T(8,128)(2,1)S(1)}, u32[]{:S(2)}, u32[]{:S(2)}) %collective-permute-start.9) | collective-permute-done | bytes 196640 | tf_op jit(solution)/shard_map/ppermute | solution.py:44
  77.8 4.7 %collective-permute-done.10 = bf16[32,3072]{1,0:T(8,128)(2,1)S(1)} collective-permute-done((bf16[32,3072]{1,0:T(8,128)(2,1)S(1)}, bf16[32,3072]{1,0:T(8,128)(2,1)S(1)}, u32[]{:S(2)}, u32[]{:S(2)}) %collective-permute-start.10) | collective-permute-done | bytes 196640 | tf_op jit(solution)/shard_map/ppermute | solution.py:44
  85.0 3.8 %collective-permute-done.5.refs_0_ = bf16[96,6144]{1,0:T(8,128)(2,1)S(1)} collective-permute-done((bf16[96,6144]{1,0:T(8,128)(2,1)S(1)}, bf16[96,6144]{1,0:T(8,128)(2,1)S(1)}, u32[]{:S(2)}, u32[]{:S(2)}) %collective-permute-start.5) | collective-permute-done | bytes 1179680 | tf_op jit(solution)/shard_map/ppermute | solution.py:44
  88.8 2.6 %collective-permute-start.6 = (bf16[96,3072]{1,0:T(8,128)(2,1)S(1)}, bf16[96,3072]{1,0:T(8,128)(2,1)S(1)}, u32[]{:S(2)}, u32[]{:S(2)}) collective-permute-start(bf16[96,3072]{1,0:T(8,128)(2,1)S(1)} %slice.24), channel_id=1, source_target_pairs={{0,192},{8,56},{16,208},{24,8},{32,224},{40,24},{48,240},{56,40},{... | collective-permute-start | bytes 1769480 | tf_op jit(solution)/shard_map/ppermute | solution.py:44
  95.6 6.4 %shard_map.124 = (bf16[128,3072]{1,0:T(8,128)(2,1)S(1)}, bf16[128,3072]{1,0:T(8,128)(2,1)S(1)}, bf16[128,3072]{1,0:T(8,128)(2,1)S(1)}, bf16[128,3072]{1,0:T(8,128)(2,1)S(1)}) custom-call(bf16[96,6144]{1,0:T(8,128)(2,1)S(1)} %collective-permute-done.5.refs_0_, bf16[32,6144]{1,0:T(8,128)(2,1)S(1)} %collective-permute-done.11.refs_1_, ...), custom_call_target="tpu_custom_call" | custom-call | flops 5435817984 | bytes 21233664 | tf_op jit(solution)/shard_map/pallas_call | solution.py:320
  102.0 2.7 %collective-permute-done.14.refs_3_ = bf16[32,3072]{1,0:T(8,128)(2,1)S(1)} collective-permute-done((bf16[32,3072]{1,0:T(8,128)(2,1)S(1)}, bf16[32,3072]{1,0:T(8,128)(2,1)S(1)}, u32[]{:S(2)}, u32[]{:S(2)}) %collective-permute-start.14) | collective-permute-done | bytes 196640 | tf_op jit(solution)/shard_map/ppermute | solution.py:44
  106.8 5.2 %shard_map.125 = (bf16[128,3072]{1,0:T(8,128)(2,1)S(1)}, bf16[128,3072]{1,0:T(8,128)(2,1)S(1)}) custom-call(bf16[96,3072]{1,0:T(8,128)(2,1)S(1)} %collective-permute-done.6.refs_0_, bf16[96,3072]{1,0:T(8,128)(2,1)S(1)} %collective-permute-done.8.refs_1_, bf16[32,3072]{1,0:T(8,128)(2,1)S(1)} %collective-permute-done.12.refs_2_, ...), custom_call_target="tpu_custom_call" | custom-call | flops 5435817984 | bytes 21233664 | tf_op jit(solution)/shard_map/pallas_call | solution.py:320
  112.1 3.2 %collective-permute-start.16 = (bf16[128,3072]{1,0:T(8,128)(2,1)S(1)}, bf16[128,3072]{1,0:T(8,128)(2,1)S(1)}, u32[]{:S(2)}, u32[]{:S(2)}) collective-permute-start(bf16[128,3072]{1,0:T(8,128)(2,1)S(1)} %get-tuple-element.84), channel_id=1, source_target_pairs={{0,192},{8,56},{16,208},{24,8},{32,224},{40,24},{48,240},{56,40},{... | collective-permute-start | bytes 2359304 | tf_op jit(solution)/shard_map/ppermute | solution.py:44
  118.5 5.2 %shard_map.126 = (bf16[128,3072]{1,0:T(8,128)(2,1)S(1)}, bf16[128,3072]{1,0:T(8,128)(2,1)S(1)}) custom-call(bf16[96,6144]{1,0:T(8,128)(2,1)S(1)} %constant_dynamic-update-slice_fusion.refs_0_, bf16[32,6144]{1,0:T(8,128)(2,1)S(1)} %constant_dynamic-update-slice_fusion.3.refs_1_, bf16[288,6144]{1,0:T(8,128)(2,1)S(1)} %bitcast.13, ...), custom_call_target="tpu_custom_call" | custom-call | flops 5435817984 | bytes 21233664 | tf_op jit(solution)/shard_map/pallas_call | solution.py:320
  123.7 3.2 %collective-permute-done.15 = bf16[128,3072]{1,0:T(8,128)(2,1)S(1)} collective-permute-done((bf16[128,3072]{1,0:T(8,128)(2,1)S(1)}, bf16[128,3072]{1,0:T(8,128)(2,1)S(1)}, u32[]{:S(2)}, u32[]{:S(2)}) %collective-permute-start.15) | collective-permute-done | bytes 786464 | tf_op jit(solution)/shard_map/ppermute | solution.py:44
  127.7 3.1 %collective-permute-start.19 = (bf16[128,3072]{1,0:T(8,128)(2,1)S(1)}, bf16[128,3072]{1,0:T(8,128)(2,1)S(1)}, u32[]{:S(2)}, u32[]{:S(2)}) collective-permute-start(bf16[128,3072]{1,0:T(8,128)(2,1)S(1)} %add_convert_fusion.1), channel_id=1, source_target_pairs={{0,192},{8,56},{16,208},{24,8},{32,224},{40,24},{48,240},{56,40},{... | collective-permute-start | bytes 2359304 | tf_op jit(solution)/shard_map/ppermute | solution.py:44
  130.7 10.5 %collective-permute-done.20.b_one = bf16[128,3072]{1,0:T(8,128)(2,1)S(1)} collective-permute-done((bf16[128,3072]{1,0:T(8,128)(2,1)S(1)}, bf16[128,3072]{1,0:T(8,128)(2,1)S(1)}, u32[]{:S(2)}, u32[]{:S(2)}) %collective-permute-start.20) | collective-permute-done | bytes 786464 | tf_op jit(solution)/shard_map/ppermute | solution.py:44
  144.6 5.4 %collective-permute-done.21.refs_0_ = bf16[32,6144]{1,0:T(8,128)(2,1)S(1)} collective-permute-done((bf16[32,6144]{1,0:T(8,128)(2,1)S(1)}, bf16[32,6144]{1,0:T(8,128)(2,1)S(1)}, u32[]{:S(2)}, u32[]{:S(2)}) %collective-permute-start.21) | collective-permute-done | bytes 393248 | tf_op jit(solution)/shard_map/ppermute | solution.py:44
  150.1 4.5 %collective-permute-done.23.refs_2_ = bf16[32,6144]{1,0:T(8,128)(2,1)S(1)} collective-permute-done((bf16[32,6144]{1,0:T(8,128)(2,1)S(1)}, bf16[32,6144]{1,0:T(8,128)(2,1)S(1)}, u32[]{:S(2)}, u32[]{:S(2)}) %collective-permute-start.23) | collective-permute-done | bytes 393248 | tf_op jit(solution)/shard_map/ppermute | solution.py:44
  155.5 3.5 %all-to-all-start.3 = ((bf16[8,32,768]{2,1,0:T(8,128)(2,1)}), bf16[8,32,768]{2,1,0:T(8,128)(2,1)S(1)}, u32[]{:S(2)}, u32[]{:S(2)}) async-start(bf16[8,32,768]{2,1,0:T(8,128)(2,1)} %shard_map.128), calls=%async_computation.3 | async-start | bytes 786432 | tf_op jit(solution)/shard_map/all_to_all | solution.py:486
  159.1 11.2 %all-to-all-done.3.back_ref = bf16[8,32,768]{2,1,0:T(8,128)(2,1)S(1)} async-done(((bf16[8,32,768]{2,1,0:T(8,128)(2,1)}), bf16[8,32,768]{2,1,0:T(8,128)(2,1)S(1)}, u32[]{:S(2)}, u32[]{:S(2)}) %all-to-all-start.3) | async-done | bytes 393248 | tf_op jit(solution)/shard_map/all_to_all | solution.py:486
  (79 shorter events, 34.8 us)
Async XLA Ops:
  0.0 34.0 %collective-permute-start = (bf16[288,6144]{1,0:T(8,128)(2,1)}, bf16[288,6144]{1,0:T(8,128)(2,1)S(1)}, u32[]{:S(2)}, u32[]{:S(2)}) collective-permute-start(bf16[288,6144]{1,0:T(8,128)(2,1)} %bitcast.10), channel_id=1, source_target_pairs={{0,8},{8,0},{16,24},{24,16},{32,40},{40,32},{48,56},{56,48},{64,72... | collective-permute-start | bytes 10616840 | tf_op jit(solution)/shard_map/ppermute | solution.py:431
  0.0 34.0 %collective-permute-start.1 = (bf16[288,6144]{1,0:T(8,128)(2,1)}, bf16[288,6144]{1,0:T(8,128)(2,1)}, u32[]{:S(2)}, u32[]{:S(2)}) collective-permute-start(bf16[288,6144]{1,0:T(8,128)(2,1)} %bitcast.14), channel_id=1, source_target_pairs={{0,8},{8,0},{16,24},{24,16},{32,40},{40,32},{48,56},{56,48},{64,72... | collective-permute-start | bytes 10616840 | tf_op jit(solution)/shard_map/ppermute | solution.py:432
  0.5 33.5 %collective-permute-start.2 = (bf16[288,6144]{1,0:T(8,128)(2,1)}, bf16[288,6144]{1,0:T(8,128)(2,1)}, u32[]{:S(2)}, u32[]{:S(2)}) collective-permute-start(bf16[288,6144]{1,0:T(8,128)(2,1)} %bitcast.18), channel_id=1, source_target_pairs={{0,8},{8,0},{16,24},{24,16},{32,40},{40,32},{48,56},{56,48},{64,72... | collective-permute-start | bytes 10616840 | tf_op jit(solution)/shard_map/ppermute | solution.py:433
  3.0 15.5 %all-to-all-start = ((bf16[32,32,128]{2,1,0:T(8,128)(2,1)}), bf16[32,32,128]{2,1,0:T(8,128)(2,1)}, u32[]{:S(2)}, u32[]{:S(2)}) async-start(bf16[32,32,128]{2,1,0:T(8,128)(2,1)} %shard_map.118), calls=%async_computation | async-start | bytes 524288 | tf_op jit(solution)/shard_map/all_to_all | solution.py:437
  20.3 13.6 %all-to-all-start.1 = ((bf16[32,32,128]{2,1,0:T(8,128)(2,1)}), bf16[32,32,128]{2,1,0:T(8,128)(2,1)}, u32[]{:S(2)}, u32[]{:S(2)}) async-start(bf16[32,32,128]{2,1,0:T(8,128)(2,1)} %shard_map.119), calls=%async_computation.1 | async-start | bytes 524288 | tf_op jit(solution)/shard_map/all_to_all | solution.py:440
  60.5 7.9 %collective-permute-start.3 = (bf16[32,6144]{1,0:T(8,128)(2,1)S(1)}, bf16[32,6144]{1,0:T(8,128)(2,1)S(1)}, u32[]{:S(2)}, u32[]{:S(2)}) collective-permute-start(bf16[32,6144]{1,0:T(8,128)(2,1)S(1)} %shard_map.122), channel_id=1, source_target_pairs={{0,48},{8,200},{16,0},{24,216},{32,16},{40,232},{48,32},{56,248},{... | collective-permute-start | bytes 1179656 | tf_op jit(solution)/shard_map/ppermute | solution.py:44
  69.7 8.1 %collective-permute-start.9 = (bf16[32,3072]{1,0:T(8,128)(2,1)S(1)}, bf16[32,3072]{1,0:T(8,128)(2,1)S(1)}, u32[]{:S(2)}, u32[]{:S(2)}) collective-permute-start(bf16[32,3072]{1,0:T(8,128)(2,1)S(1)} %slice.20), channel_id=1, source_target_pairs={{0,48},{8,200},{16,0},{24,216},{32,16},{40,232},{48,32},{56,248},{... | collective-permute-start | bytes 589832 | tf_op jit(solution)/shard_map/ppermute | solution.py:44
  72.5 16.3 %collective-permute-start.5 = (bf16[96,6144]{1,0:T(8,128)(2,1)S(1)}, bf16[96,6144]{1,0:T(8,128)(2,1)S(1)}, u32[]{:S(2)}, u32[]{:S(2)}) collective-permute-start(bf16[96,6144]{1,0:T(8,128)(2,1)S(1)} %constant_dynamic-update-slice_fusion.refs_0_), channel_id=1, source_target_pairs={{0,192},{8,56},{16,208},{24,8},{32,224},{40,24},{48,240},{56,40},{... | collective-permute-start | bytes 3538952 | tf_op jit(solution)/shard_map/ppermute | solution.py:44
  73.7 17.7 %collective-permute-start.7 = (bf16[96,6144]{1,0:T(8,128)(2,1)S(1)}, bf16[96,6144]{1,0:T(8,128)(2,1)S(1)}, u32[]{:S(2)}, u32[]{:S(2)}) collective-permute-start(bf16[96,6144]{1,0:T(8,128)(2,1)S(1)} %constant_dynamic-update-slice_fusion.refs_0_), channel_id=1, source_target_pairs={{0,64},{8,24},{16,80},{24,40},{32,96},{40,56},{48,112},{56,8},{64,... | collective-permute-start | bytes 3538952 | tf_op jit(solution)/shard_map/ppermute | solution.py:44
  74.6 7.9 %collective-permute-start.10 = (bf16[32,3072]{1,0:T(8,128)(2,1)S(1)}, bf16[32,3072]{1,0:T(8,128)(2,1)S(1)}, u32[]{:S(2)}, u32[]{:S(2)}) collective-permute-start(bf16[32,3072]{1,0:T(8,128)(2,1)S(1)} %slice.21), channel_id=1, source_target_pairs={{0,16},{8,72},{16,32},{24,88},{32,48},{40,104},{48,0},{56,120},{64... | collective-permute-start | bytes 589832 | tf_op jit(solution)/shard_map/ppermute | solution.py:44
  82.5 10.4 %collective-permute-start.11 = (bf16[32,6144]{1,0:T(8,128)(2,1)S(1)}, bf16[32,6144]{1,0:T(8,128)(2,1)S(1)}, u32[]{:S(2)}, u32[]{:S(2)}) collective-permute-start(bf16[32,6144]{1,0:T(8,128)(2,1)S(1)} %constant_dynamic-update-slice_fusion.3.refs_1_), channel_id=1, source_target_pairs={{0,192},{8,56},{16,208},{24,8},{32,224},{40,24},{48,240},{56,40},{... | collective-permute-start | bytes 1179656 | tf_op jit(solution)/shard_map/ppermute | solution.py:44
  85.0 10.5 %collective-permute-start.13 = (bf16[32,6144]{1,0:T(8,128)(2,1)S(1)}, bf16[32,6144]{1,0:T(8,128)(2,1)S(1)}, u32[]{:S(2)}, u32[]{:S(2)}) collective-permute-start(bf16[32,6144]{1,0:T(8,128)(2,1)S(1)} %constant_dynamic-update-slice_fusion.3.refs_1_), channel_id=1, source_target_pairs={{0,64},{8,24},{16,80},{24,40},{32,96},{40,56},{48,112},{56,8},{64,... | collective-permute-start | bytes 1179656 | tf_op jit(solution)/shard_map/ppermute | solution.py:44
  88.8 16.0 %collective-permute-start.6 = (bf16[96,3072]{1,0:T(8,128)(2,1)S(1)}, bf16[96,3072]{1,0:T(8,128)(2,1)S(1)}, u32[]{:S(2)}, u32[]{:S(2)}) collective-permute-start(bf16[96,3072]{1,0:T(8,128)(2,1)S(1)} %slice.24), channel_id=1, source_target_pairs={{0,192},{8,56},{16,208},{24,8},{32,224},{40,24},{48,240},{56,40},{... | collective-permute-start | bytes 1769480 | tf_op jit(solution)/shard_map/ppermute | solution.py:44
  91.5 13.3 %collective-permute-start.8 = (bf16[96,3072]{1,0:T(8,128)(2,1)S(1)}, bf16[96,3072]{1,0:T(8,128)(2,1)S(1)}, u32[]{:S(2)}, u32[]{:S(2)}) collective-permute-start(bf16[96,3072]{1,0:T(8,128)(2,1)S(1)} %slice.25), channel_id=1, source_target_pairs={{0,64},{8,24},{16,80},{24,40},{32,96},{40,56},{48,112},{56,8},{64,... | collective-permute-start | bytes 1769480 | tf_op jit(solution)/shard_map/ppermute | solution.py:44
  93.0 9.0 %collective-permute-start.12 = (bf16[32,3072]{1,0:T(8,128)(2,1)S(1)}, bf16[32,3072]{1,0:T(8,128)(2,1)S(1)}, u32[]{:S(2)}, u32[]{:S(2)}) collective-permute-start(bf16[32,3072]{1,0:T(8,128)(2,1)S(1)} %slice.26), channel_id=1, source_target_pairs={{0,192},{8,56},{16,208},{24,8},{32,224},{40,24},{48,240},{56,40},{... | collective-permute-start | bytes 589832 | tf_op jit(solution)/shard_map/ppermute | solution.py:44
  95.4 9.3 %collective-permute-start.14 = (bf16[32,3072]{1,0:T(8,128)(2,1)S(1)}, bf16[32,3072]{1,0:T(8,128)(2,1)S(1)}, u32[]{:S(2)}, u32[]{:S(2)}) collective-permute-start(bf16[32,3072]{1,0:T(8,128)(2,1)S(1)} %slice.27), channel_id=1, source_target_pairs={{0,64},{8,24},{16,80},{24,40},{32,96},{40,56},{48,112},{56,8},{64,... | collective-permute-start | bytes 589832 | tf_op jit(solution)/shard_map/ppermute | solution.py:44
  104.8 12.0 %collective-permute-start.17 = (bf16[128,3072]{1,0:T(8,128)(2,1)S(1)}, bf16[128,3072]{1,0:T(8,128)(2,1)S(1)}, u32[]{:S(2)}, u32[]{:S(2)}) collective-permute-start(bf16[128,3072]{1,0:T(8,128)(2,1)S(1)} %get-tuple-element.85), channel_id=1, source_target_pairs={{0,192},{8,56},{16,208},{24,8},{32,224},{40,24},{48,240},{56,40},{... | collective-permute-start | bytes 2359304 | tf_op jit(solution)/shard_map/ppermute | solution.py:44
  105.3 13.2 %collective-permute-start.18 = (bf16[128,3072]{1,0:T(8,128)(2,1)S(1)}, bf16[128,3072]{1,0:T(8,128)(2,1)S(1)}, u32[]{:S(2)}, u32[]{:S(2)}) collective-permute-start(bf16[128,3072]{1,0:T(8,128)(2,1)S(1)} %get-tuple-element.86), channel_id=1, source_target_pairs={{0,64},{8,24},{16,80},{24,40},{32,96},{40,56},{48,112},{56,8},{64,... | collective-permute-start | bytes 2359304 | tf_op jit(solution)/shard_map/ppermute | solution.py:44
  112.0 15.0 %collective-permute-start.15 = (bf16[128,3072]{1,0:T(8,128)(2,1)S(1)}, bf16[128,3072]{1,0:T(8,128)(2,1)S(1)}, u32[]{:S(2)}, u32[]{:S(2)}) collective-permute-start(bf16[128,3072]{1,0:T(8,128)(2,1)S(1)} %get-tuple-element.83), channel_id=1, source_target_pairs={{0,64},{8,24},{16,80},{24,40},{32,96},{40,56},{48,112},{56,8},{64,... | collective-permute-start | bytes 2359304 | tf_op jit(solution)/shard_map/ppermute | solution.py:44
  112.1 14.9 %collective-permute-start.16 = (bf16[128,3072]{1,0:T(8,128)(2,1)S(1)}, bf16[128,3072]{1,0:T(8,128)(2,1)S(1)}, u32[]{:S(2)}, u32[]{:S(2)}) collective-permute-start(bf16[128,3072]{1,0:T(8,128)(2,1)S(1)} %get-tuple-element.84), channel_id=1, source_target_pairs={{0,192},{8,56},{16,208},{24,8},{32,224},{40,24},{48,240},{56,40},{... | collective-permute-start | bytes 2359304 | tf_op jit(solution)/shard_map/ppermute | solution.py:44
  127.1 14.1 %collective-permute-start.20 = (bf16[128,3072]{1,0:T(8,128)(2,1)S(1)}, bf16[128,3072]{1,0:T(8,128)(2,1)S(1)}, u32[]{:S(2)}, u32[]{:S(2)}) collective-permute-start(bf16[128,3072]{1,0:T(8,128)(2,1)S(1)} %add_convert_fusion), channel_id=1, source_target_pairs={{0,64},{8,24},{16,80},{24,40},{32,96},{40,56},{48,112},{56,8},{64,... | collective-permute-start | bytes 2359304 | tf_op jit(solution)/shard_map/ppermute | solution.py:44
  127.7 13.9 %collective-permute-start.19 = (bf16[128,3072]{1,0:T(8,128)(2,1)S(1)}, bf16[128,3072]{1,0:T(8,128)(2,1)S(1)}, u32[]{:S(2)}, u32[]{:S(2)}) collective-permute-start(bf16[128,3072]{1,0:T(8,128)(2,1)S(1)} %add_convert_fusion.1), channel_id=1, source_target_pairs={{0,192},{8,56},{16,208},{24,8},{32,224},{40,24},{48,240},{56,40},{... | collective-permute-start | bytes 2359304 | tf_op jit(solution)/shard_map/ppermute | solution.py:44
  144.3 10.4 %collective-permute-start.23 = (bf16[32,6144]{1,0:T(8,128)(2,1)S(1)}, bf16[32,6144]{1,0:T(8,128)(2,1)S(1)}, u32[]{:S(2)}, u32[]{:S(2)}) collective-permute-start(bf16[32,6144]{1,0:T(8,128)(2,1)S(1)} %get-tuple-element.101), channel_id=1, source_target_pairs={{0,32},{8,136},{16,48},{24,152},{32,0},{40,168},{48,16},{56,184},{... | collective-permute-start | bytes 1179656 | tf_op jit(solution)/shard_map/ppermute | solution.py:44
  155.5 14.7 %all-to-all-start.3 = ((bf16[8,32,768]{2,1,0:T(8,128)(2,1)}), bf16[8,32,768]{2,1,0:T(8,128)(2,1)S(1)}, u32[]{:S(2)}, u32[]{:S(2)}) async-start(bf16[8,32,768]{2,1,0:T(8,128)(2,1)} %shard_map.128), calls=%async_computation.3 | async-start | bytes 786432 | tf_op jit(solution)/shard_map/all_to_all | solution.py:486
  (13 other events, 234.3 us)

commit v3 on v2

--- a/solution.py
+++ b/solution.py
@@ -463,13 +463,14 @@
     )
     near_far, last_far, beside = lax.optimization_barrier((near_far, last_far, beside))
     to_after_one, to_after_two, to_before_one, to_before_two = beside
+    far = expert(((near_far, last_far),), mine, other)
+    far, near, to_before_one, to_after_two = lax.optimization_barrier(
+        (far, near, to_before_one, to_after_two)
+    )
+    far_one, far_two = far
+    through = (send(far_one, SECOND, 1), send(far_two, SECOND, -1))
     from_after_one = send(to_before_one, SECOND, -1)
     from_before_two = send(to_after_two, SECOND, 1)
-    far_one, far_two = expert(((near_far, last_far),), mine, other)
-    through = (send(far_one, SECOND, 1), send(far_two, SECOND, -1))
-    near, from_after_one, from_before_two = lax.optimization_barrier(
-        (near, from_after_one, from_before_two)
-    )
     here = expert(((near, opposite),), mine, other)
     through, here = lax.optimization_barrier((through, here))
     through_after, through_before = through

time: 174 us -> 172 us (0.989); the launches traced: 171 us -> 171 us
  transfers between devices with their start and end apart: 27 -> 27, of which waited for: 18 -> 17; matrix products, arithmetic and copies ran while one was open for 1% -> 1% of each run, Pallas kernels for 16% -> 13%
where the time goes in v3:
time: 172 us; the launch traced here: 171 us
  waiting for transfers between devices  68 us (40%)
  starting transfers between devices  44.5 us (26%)
  Pallas kernels  32.6 us (19%)
  blocking collectives  23.8 us (14%)
    ppermute x21, waiting for transfers between devices, send(): lax.ppermute(rows, 'ctx', chip_pairs(lambda core: along_x[(core + axis) %...  44.9 us
    ppermute x21, starting transfers between devices, send(): lax.ppermute(rows, 'ctx', chip_pairs(lambda core: along_x[(core + axis) %...  26.8 us
    all_to_all x1, blocking collectives, body(): lax.all_to_all(sent, 'exp', split_axis=0, concat_axis=0, tiled=True)  23.8 us
    pallas_call x3, Pallas kernels, expert(): pl.pallas_call(lambda *refs: expert_kernel(layout, len(xs), *refs), out_s...  16.8 us
    all_to_all x1, waiting for transfers between devices, body(): lax.all_to_all(summed, 'exp', split_axis=0, concat_axis=0, tiled=True)  11.7 us
    all_to_all x1, waiting for transfers between devices, body(): lax.all_to_all(pieces, 'ctx', split_axis=0, concat_axis=0, tiled=True)  7.73 us
    all_to_all x1, starting transfers between devices, body(): lax.all_to_all(pieces, 'ctx', split_axis=0, concat_axis=0, tiled=True)  7.71 us
    all_to_all x1, starting transfers between devices, body(): lax.all_to_all(states, 'ctx', split_axis=0, concat_axis=0, tiled=True)  5.9 us
  transfers between devices with their start and end apart: 27, of which 17 were waited for; matrix products, arithmetic and copies ran while one was open for 1% of the time, Pallas kernels for 13%

profile of v3, /device:TPU:2, one launch (start us, length us, event | category | flops | bytes accessed | tf_op | source)
XLA Modules:
  0.0 171.2 jit_solution(2456581816584246889)
XLA Ops:
  3.0 7.7 %all-to-all-start = ((bf16[32,32,128]{2,1,0:T(8,128)(2,1)}), bf16[32,32,128]{2,1,0:T(8,128)(2,1)}, u32[]{:S(2)}, u32[]{:S(2)}) async-start(bf16[32,32,128]{2,1,0:T(8,128)(2,1)} %shard_map.118), calls=%async_computation | async-start | bytes 524288 | tf_op jit(solution)/shard_map/all_to_all | solution.py:437
  10.7 7.7 %all-to-all-done.pieces_ref = bf16[32,32,128]{2,1,0:T(8,128)(2,1)} async-done(((bf16[32,32,128]{2,1,0:T(8,128)(2,1)}), bf16[32,32,128]{2,1,0:T(8,128)(2,1)}, u32[]{:S(2)}, u32[]{:S(2)}) %all-to-all-start) | async-done | bytes 262176 | tf_op jit(solution)/shard_map/all_to_all | solution.py:437
  20.3 5.9 %all-to-all-start.1 = ((bf16[32,32,128]{2,1,0:T(8,128)(2,1)}), bf16[32,32,128]{2,1,0:T(8,128)(2,1)}, u32[]{:S(2)}, u32[]{:S(2)}) async-start(bf16[32,32,128]{2,1,0:T(8,128)(2,1)} %shard_map.119), calls=%async_computation.1 | async-start | bytes 524288 | tf_op jit(solution)/shard_map/all_to_all | solution.py:440
  27.6 2.7 %shard_map.120 = (f32[112,768]{1,0:T(8,128)}, bf16[112,768]{1,0:T(8,128)(2,1)}, bf16[112,256]{1,0:T(8,128)(2,1)}, bf16[112,256]{1,0:T(8,128)(2,1)}) custom-call(bf16[112,768]{1,0:T(8,128)(2,1)} %q_ref.1, bf16[112,768]{1,0:T(8,128)(2,1)} %k_ref.3, bf16[112,768]{1,0:T(8,128)(2,1)} %v_ref.3, f32[6,112]{1,0:T(8,128)} %bitcast.24, s32[112,2]{1,0:T(8,128)} %copy.13.routes_ref), custom_call_target="tpu_custom_call" | custom-call | flops 231211008 | bytes 2097152 | tf_op jit(solution)/shard_map/pallas_call | solution.py:144
  30.3 3.7 %all-to-all-done.1.state_ref = bf16[32,32,128]{2,1,0:T(8,128)(2,1)} async-done(((bf16[32,32,128]{2,1,0:T(8,128)(2,1)}), bf16[32,32,128]{2,1,0:T(8,128)(2,1)}, u32[]{:S(2)}, u32[]{:S(2)}) %all-to-all-start.1) | async-done | bytes 262176 | tf_op jit(solution)/shard_map/all_to_all | solution.py:440
  36.5 23.8 %all_to_all.20.rows_ref = bf16[8,32,768]{2,1,0:T(8,128)(2,1)S(1)} all-to-all(bf16[8,32,768]{2,1,0:T(8,128)(2,1)} %get-tuple-element.61), channel_id=1, replica_groups=mesh['ctx'=32,'exp'=8] {'exp'}, dimensions={0} | all-to-all | bytes 786432 | tf_op jit(solution)/shard_map/all_to_all | solution.py:448
  62.6 3.7 %shard_map.123 = (bf16[288,6144]{1,0:T(8,128)(2,1)S(1)}, bf16[288,6144]{1,0:T(8,128)(2,1)S(1)}, bf16[288,6144]{1,0:T(8,128)(2,1)S(1)}) custom-call(bf16[288,6144]{1,0:T(8,128)(2,1)S(1)} %collective-permute-done.refs_0_, bf16[288,6144]{1,0:T(8,128)(2,1)} %collective-permute-done.1.refs_1_, bf16[288,6144]{1,0:T(8,128)(2,1)} %collective-permute-done.2.refs_2_), custom_call_target="tpu_custom_call" | custom-call | bytes 10616832 | tf_op jit(solution)/shard_map/pallas_call | solution.py:258
  69.7 2.7 %collective-permute-start.9 = (bf16[32,3072]{1,0:T(8,128)(2,1)S(1)}, bf16[32,3072]{1,0:T(8,128)(2,1)S(1)}, u32[]{:S(2)}, u32[]{:S(2)}) collective-permute-start(bf16[32,3072]{1,0:T(8,128)(2,1)S(1)} %slice.20), channel_id=1, source_target_pairs={{0,48},{8,200},{16,0},{24,216},{32,16},{40,232},{48,32},{56,248},{... | collective-permute-start | bytes 589832 | tf_op jit(solution)/shard_map/ppermute | solution.py:44
  74.7 3.1 %collective-permute-done.9 = bf16[32,3072]{1,0:T(8,128)(2,1)S(1)} collective-permute-done((bf16[32,3072]{1,0:T(8,128)(2,1)S(1)}, bf16[32,3072]{1,0:T(8,128)(2,1)S(1)}, u32[]{:S(2)}, u32[]{:S(2)}) %collective-permute-start.9) | collective-permute-done | bytes 196640 | tf_op jit(solution)/shard_map/ppermute | solution.py:44
  77.8 4.7 %collective-permute-done.10 = bf16[32,3072]{1,0:T(8,128)(2,1)S(1)} collective-permute-done((bf16[32,3072]{1,0:T(8,128)(2,1)S(1)}, bf16[32,3072]{1,0:T(8,128)(2,1)S(1)}, u32[]{:S(2)}, u32[]{:S(2)}) %collective-permute-start.10) | collective-permute-done | bytes 196640 | tf_op jit(solution)/shard_map/ppermute | solution.py:44
  85.0 3.8 %collective-permute-done.5.refs_0_ = bf16[96,6144]{1,0:T(8,128)(2,1)S(1)} collective-permute-done((bf16[96,6144]{1,0:T(8,128)(2,1)S(1)}, bf16[96,6144]{1,0:T(8,128)(2,1)S(1)}, u32[]{:S(2)}, u32[]{:S(2)}) %collective-permute-start.5) | collective-permute-done | bytes 1179680 | tf_op jit(solution)/shard_map/ppermute | solution.py:44
  95.6 6.4 %shard_map.124 = (bf16[128,3072]{1,0:T(8,128)(2,1)S(1)}, bf16[128,3072]{1,0:T(8,128)(2,1)S(1)}, bf16[128,3072]{1,0:T(8,128)(2,1)S(1)}, bf16[128,3072]{1,0:T(8,128)(2,1)S(1)}) custom-call(bf16[96,6144]{1,0:T(8,128)(2,1)S(1)} %collective-permute-done.5.refs_0_, bf16[32,6144]{1,0:T(8,128)(2,1)S(1)} %collective-permute-done.11.refs_1_, ...), custom_call_target="tpu_custom_call" | custom-call | flops 5435817984 | bytes 21233664 | tf_op jit(solution)/shard_map/pallas_call | solution.py:320
  102.0 2.7 %collective-permute-done.14.refs_3_ = bf16[32,3072]{1,0:T(8,128)(2,1)S(1)} collective-permute-done((bf16[32,3072]{1,0:T(8,128)(2,1)S(1)}, bf16[32,3072]{1,0:T(8,128)(2,1)S(1)}, u32[]{:S(2)}, u32[]{:S(2)}) %collective-permute-start.14) | collective-permute-done | bytes 196640 | tf_op jit(solution)/shard_map/ppermute | solution.py:44
  104.8 5.2 %shard_map.125 = (bf16[128,3072]{1,0:T(8,128)(2,1)S(1)}, bf16[128,3072]{1,0:T(8,128)(2,1)S(1)}) custom-call(bf16[96,3072]{1,0:T(8,128)(2,1)S(1)} %collective-permute-done.6.refs_0_, bf16[96,3072]{1,0:T(8,128)(2,1)S(1)} %collective-permute-done.8.refs_1_, bf16[32,3072]{1,0:T(8,128)(2,1)S(1)} %collective-permute-done.12.refs_2_, ...), custom_call_target="tpu_custom_call" | custom-call | flops 5435817984 | bytes 21233664 | tf_op jit(solution)/shard_map/pallas_call | solution.py:320
  110.0 3.2 %collective-permute-start.16 = (bf16[128,3072]{1,0:T(8,128)(2,1)S(1)}, bf16[128,3072]{1,0:T(8,128)(2,1)S(1)}, u32[]{:S(2)}, u32[]{:S(2)}) collective-permute-start(bf16[128,3072]{1,0:T(8,128)(2,1)S(1)} %get-tuple-element.90), channel_id=1, source_target_pairs={{0,192},{8,56},{16,208},{24,8},{32,224},{40,24},{48,240},{56,40},{... | collective-permute-start | bytes 2359304 | tf_op jit(solution)/shard_map/ppermute | solution.py:44
  115.3 5.2 %shard_map.126 = (bf16[128,3072]{1,0:T(8,128)(2,1)S(1)}, bf16[128,3072]{1,0:T(8,128)(2,1)S(1)}) custom-call(bf16[96,6144]{1,0:T(8,128)(2,1)S(1)} %constant_dynamic-update-slice_fusion.refs_0_, bf16[32,6144]{1,0:T(8,128)(2,1)S(1)} %constant_dynamic-update-slice_fusion.3.refs_1_, bf16[288,6144]{1,0:T(8,128)(2,1)S(1)} %bitcast.13, ...), custom_call_target="tpu_custom_call" | custom-call | flops 5435817984 | bytes 21233664 | tf_op jit(solution)/shard_map/pallas_call | solution.py:320
  120.5 2.8 %collective-permute-done.15 = bf16[128,3072]{1,0:T(8,128)(2,1)S(1)} collective-permute-done((bf16[128,3072]{1,0:T(8,128)(2,1)S(1)}, bf16[128,3072]{1,0:T(8,128)(2,1)S(1)}, u32[]{:S(2)}, u32[]{:S(2)}) %collective-permute-start.15) | collective-permute-done | bytes 786464 | tf_op jit(solution)/shard_map/ppermute | solution.py:44
  123.7 3.3 %collective-permute-start.18 = (bf16[128,3072]{1,0:T(8,128)(2,1)S(1)}, bf16[128,3072]{1,0:T(8,128)(2,1)S(1)}, u32[]{:S(2)}, u32[]{:S(2)}) collective-permute-start(bf16[128,3072]{1,0:T(8,128)(2,1)S(1)} %add_convert_fusion.1), channel_id=1, source_target_pairs={{0,192},{8,56},{16,208},{24,8},{32,224},{40,24},{48,240},{56,40},{... | collective-permute-start | bytes 2359304 | tf_op jit(solution)/shard_map/ppermute | solution.py:44
  127.0 4.2 %collective-permute-done.17.a_one = bf16[128,3072]{1,0:T(8,128)(2,1)S(1)} collective-permute-done((bf16[128,3072]{1,0:T(8,128)(2,1)S(1)}, bf16[128,3072]{1,0:T(8,128)(2,1)S(1)}, u32[]{:S(2)}, u32[]{:S(2)}) %collective-permute-start.17) | collective-permute-done | bytes 786464 | tf_op jit(solution)/shard_map/ppermute | solution.py:44
  131.6 8.5 %collective-permute-done.19.b_one = bf16[128,3072]{1,0:T(8,128)(2,1)S(1)} collective-permute-done((bf16[128,3072]{1,0:T(8,128)(2,1)S(1)}, bf16[128,3072]{1,0:T(8,128)(2,1)S(1)}, u32[]{:S(2)}, u32[]{:S(2)}) %collective-permute-start.19) | collective-permute-done | bytes 786464 | tf_op jit(solution)/shard_map/ppermute | solution.py:44
  144.1 4.5 %collective-permute-done.21.refs_0_ = bf16[32,6144]{1,0:T(8,128)(2,1)S(1)} collective-permute-done((bf16[32,6144]{1,0:T(8,128)(2,1)S(1)}, bf16[32,6144]{1,0:T(8,128)(2,1)S(1)}, u32[]{:S(2)}, u32[]{:S(2)}) %collective-permute-start.21) | collective-permute-done | bytes 393248 | tf_op jit(solution)/shard_map/ppermute | solution.py:44
  148.7 5.4 %collective-permute-done.23.refs_2_ = bf16[32,6144]{1,0:T(8,128)(2,1)S(1)} collective-permute-done((bf16[32,6144]{1,0:T(8,128)(2,1)S(1)}, bf16[32,6144]{1,0:T(8,128)(2,1)S(1)}, u32[]{:S(2)}, u32[]{:S(2)}) %collective-permute-start.23) | collective-permute-done | bytes 393248 | tf_op jit(solution)/shard_map/ppermute | solution.py:44
  155.0 3.5 %all-to-all-start.3 = ((bf16[8,32,768]{2,1,0:T(8,128)(2,1)}), bf16[8,32,768]{2,1,0:T(8,128)(2,1)S(1)}, u32[]{:S(2)}, u32[]{:S(2)}) async-start(bf16[8,32,768]{2,1,0:T(8,128)(2,1)} %shard_map.128), calls=%async_computation.3 | async-start | bytes 786432 | tf_op jit(solution)/shard_map/all_to_all | solution.py:487
  158.6 11.7 %all-to-all-done.3.back_ref = bf16[8,32,768]{2,1,0:T(8,128)(2,1)S(1)} async-done(((bf16[8,32,768]{2,1,0:T(8,128)(2,1)}), bf16[8,32,768]{2,1,0:T(8,128)(2,1)S(1)}, u32[]{:S(2)}, u32[]{:S(2)}) %all-to-all-start.3) | async-done | bytes 393248 | tf_op jit(solution)/shard_map/all_to_all | solution.py:487
  (79 shorter events, 34.9 us)
Async XLA Ops:
  0.0 34.0 %collective-permute-start = (bf16[288,6144]{1,0:T(8,128)(2,1)}, bf16[288,6144]{1,0:T(8,128)(2,1)S(1)}, u32[]{:S(2)}, u32[]{:S(2)}) collective-permute-start(bf16[288,6144]{1,0:T(8,128)(2,1)} %bitcast.10), channel_id=1, source_target_pairs={{0,8},{8,0},{16,24},{24,16},{32,40},{40,32},{48,56},{56,48},{64,72... | collective-permute-start | bytes 10616840 | tf_op jit(solution)/shard_map/ppermute | solution.py:431
  0.0 34.0 %collective-permute-start.1 = (bf16[288,6144]{1,0:T(8,128)(2,1)}, bf16[288,6144]{1,0:T(8,128)(2,1)}, u32[]{:S(2)}, u32[]{:S(2)}) collective-permute-start(bf16[288,6144]{1,0:T(8,128)(2,1)} %bitcast.14), channel_id=1, source_target_pairs={{0,8},{8,0},{16,24},{24,16},{32,40},{40,32},{48,56},{56,48},{64,72... | collective-permute-start | bytes 10616840 | tf_op jit(solution)/shard_map/ppermute | solution.py:432
  0.5 33.5 %collective-permute-start.2 = (bf16[288,6144]{1,0:T(8,128)(2,1)}, bf16[288,6144]{1,0:T(8,128)(2,1)}, u32[]{:S(2)}, u32[]{:S(2)}) collective-permute-start(bf16[288,6144]{1,0:T(8,128)(2,1)} %bitcast.18), channel_id=1, source_target_pairs={{0,8},{8,0},{16,24},{24,16},{32,40},{40,32},{48,56},{56,48},{64,72... | collective-permute-start | bytes 10616840 | tf_op jit(solution)/shard_map/ppermute | solution.py:433
  3.0 15.5 %all-to-all-start = ((bf16[32,32,128]{2,1,0:T(8,128)(2,1)}), bf16[32,32,128]{2,1,0:T(8,128)(2,1)}, u32[]{:S(2)}, u32[]{:S(2)}) async-start(bf16[32,32,128]{2,1,0:T(8,128)(2,1)} %shard_map.118), calls=%async_computation | async-start | bytes 524288 | tf_op jit(solution)/shard_map/all_to_all | solution.py:437
  20.3 13.6 %all-to-all-start.1 = ((bf16[32,32,128]{2,1,0:T(8,128)(2,1)}), bf16[32,32,128]{2,1,0:T(8,128)(2,1)}, u32[]{:S(2)}, u32[]{:S(2)}) async-start(bf16[32,32,128]{2,1,0:T(8,128)(2,1)} %shard_map.119), calls=%async_computation.1 | async-start | bytes 524288 | tf_op jit(solution)/shard_map/all_to_all | solution.py:440
  60.5 7.9 %collective-permute-start.3 = (bf16[32,6144]{1,0:T(8,128)(2,1)S(1)}, bf16[32,6144]{1,0:T(8,128)(2,1)S(1)}, u32[]{:S(2)}, u32[]{:S(2)}) collective-permute-start(bf16[32,6144]{1,0:T(8,128)(2,1)S(1)} %shard_map.122), channel_id=1, source_target_pairs={{0,48},{8,200},{16,0},{24,216},{32,16},{40,232},{48,32},{56,248},{... | collective-permute-start | bytes 1179656 | tf_op jit(solution)/shard_map/ppermute | solution.py:44
  69.7 8.1 %collective-permute-start.9 = (bf16[32,3072]{1,0:T(8,128)(2,1)S(1)}, bf16[32,3072]{1,0:T(8,128)(2,1)S(1)}, u32[]{:S(2)}, u32[]{:S(2)}) collective-permute-start(bf16[32,3072]{1,0:T(8,128)(2,1)S(1)} %slice.20), channel_id=1, source_target_pairs={{0,48},{8,200},{16,0},{24,216},{32,16},{40,232},{48,32},{56,248},{... | collective-permute-start | bytes 589832 | tf_op jit(solution)/shard_map/ppermute | solution.py:44
  72.5 16.3 %collective-permute-start.5 = (bf16[96,6144]{1,0:T(8,128)(2,1)S(1)}, bf16[96,6144]{1,0:T(8,128)(2,1)S(1)}, u32[]{:S(2)}, u32[]{:S(2)}) collective-permute-start(bf16[96,6144]{1,0:T(8,128)(2,1)S(1)} %constant_dynamic-update-slice_fusion.refs_0_), channel_id=1, source_target_pairs={{0,192},{8,56},{16,208},{24,8},{32,224},{40,24},{48,240},{56,40},{... | collective-permute-start | bytes 3538952 | tf_op jit(solution)/shard_map/ppermute | solution.py:44
  73.7 17.7 %collective-permute-start.7 = (bf16[96,6144]{1,0:T(8,128)(2,1)S(1)}, bf16[96,6144]{1,0:T(8,128)(2,1)S(1)}, u32[]{:S(2)}, u32[]{:S(2)}) collective-permute-start(bf16[96,6144]{1,0:T(8,128)(2,1)S(1)} %constant_dynamic-update-slice_fusion.refs_0_), channel_id=1, source_target_pairs={{0,64},{8,24},{16,80},{24,40},{32,96},{40,56},{48,112},{56,8},{64,... | collective-permute-start | bytes 3538952 | tf_op jit(solution)/shard_map/ppermute | solution.py:44
  74.6 7.9 %collective-permute-start.10 = (bf16[32,3072]{1,0:T(8,128)(2,1)S(1)}, bf16[32,3072]{1,0:T(8,128)(2,1)S(1)}, u32[]{:S(2)}, u32[]{:S(2)}) collective-permute-start(bf16[32,3072]{1,0:T(8,128)(2,1)S(1)} %slice.21), channel_id=1, source_target_pairs={{0,16},{8,72},{16,32},{24,88},{32,48},{40,104},{48,0},{56,120},{64... | collective-permute-start | bytes 589832 | tf_op jit(solution)/shard_map/ppermute | solution.py:44
  82.5 10.4 %collective-permute-start.11 = (bf16[32,6144]{1,0:T(8,128)(2,1)S(1)}, bf16[32,6144]{1,0:T(8,128)(2,1)S(1)}, u32[]{:S(2)}, u32[]{:S(2)}) collective-permute-start(bf16[32,6144]{1,0:T(8,128)(2,1)S(1)} %constant_dynamic-update-slice_fusion.3.refs_1_), channel_id=1, source_target_pairs={{0,192},{8,56},{16,208},{24,8},{32,224},{40,24},{48,240},{56,40},{... | collective-permute-start | bytes 1179656 | tf_op jit(solution)/shard_map/ppermute | solution.py:44
  85.0 10.5 %collective-permute-start.13 = (bf16[32,6144]{1,0:T(8,128)(2,1)S(1)}, bf16[32,6144]{1,0:T(8,128)(2,1)S(1)}, u32[]{:S(2)}, u32[]{:S(2)}) collective-permute-start(bf16[32,6144]{1,0:T(8,128)(2,1)S(1)} %constant_dynamic-update-slice_fusion.3.refs_1_), channel_id=1, source_target_pairs={{0,64},{8,24},{16,80},{24,40},{32,96},{40,56},{48,112},{56,8},{64,... | collective-permute-start | bytes 1179656 | tf_op jit(solution)/shard_map/ppermute | solution.py:44
  88.8 16.0 %collective-permute-start.6 = (bf16[96,3072]{1,0:T(8,128)(2,1)S(1)}, bf16[96,3072]{1,0:T(8,128)(2,1)S(1)}, u32[]{:S(2)}, u32[]{:S(2)}) collective-permute-start(bf16[96,3072]{1,0:T(8,128)(2,1)S(1)} %slice.24), channel_id=1, source_target_pairs={{0,192},{8,56},{16,208},{24,8},{32,224},{40,24},{48,240},{56,40},{... | collective-permute-start | bytes 1769480 | tf_op jit(solution)/shard_map/ppermute | solution.py:44
  91.5 13.3 %collective-permute-start.8 = (bf16[96,3072]{1,0:T(8,128)(2,1)S(1)}, bf16[96,3072]{1,0:T(8,128)(2,1)S(1)}, u32[]{:S(2)}, u32[]{:S(2)}) collective-permute-start(bf16[96,3072]{1,0:T(8,128)(2,1)S(1)} %slice.25), channel_id=1, source_target_pairs={{0,64},{8,24},{16,80},{24,40},{32,96},{40,56},{48,112},{56,8},{64,... | collective-permute-start | bytes 1769480 | tf_op jit(solution)/shard_map/ppermute | solution.py:44
  93.0 9.0 %collective-permute-start.12 = (bf16[32,3072]{1,0:T(8,128)(2,1)S(1)}, bf16[32,3072]{1,0:T(8,128)(2,1)S(1)}, u32[]{:S(2)}, u32[]{:S(2)}) collective-permute-start(bf16[32,3072]{1,0:T(8,128)(2,1)S(1)} %slice.26), channel_id=1, source_target_pairs={{0,192},{8,56},{16,208},{24,8},{32,224},{40,24},{48,240},{56,40},{... | collective-permute-start | bytes 589832 | tf_op jit(solution)/shard_map/ppermute | solution.py:44
  95.4 9.3 %collective-permute-start.14 = (bf16[32,3072]{1,0:T(8,128)(2,1)S(1)}, bf16[32,3072]{1,0:T(8,128)(2,1)S(1)}, u32[]{:S(2)}, u32[]{:S(2)}) collective-permute-start(bf16[32,3072]{1,0:T(8,128)(2,1)S(1)} %slice.27), channel_id=1, source_target_pairs={{0,64},{8,24},{16,80},{24,40},{32,96},{40,56},{48,112},{56,8},{64,... | collective-permute-start | bytes 589832 | tf_op jit(solution)/shard_map/ppermute | solution.py:44
  109.9 13.3 %collective-permute-start.15 = (bf16[128,3072]{1,0:T(8,128)(2,1)S(1)}, bf16[128,3072]{1,0:T(8,128)(2,1)S(1)}, u32[]{:S(2)}, u32[]{:S(2)}) collective-permute-start(bf16[128,3072]{1,0:T(8,128)(2,1)S(1)} %get-tuple-element.89), channel_id=1, source_target_pairs={{0,64},{8,24},{16,80},{24,40},{32,96},{40,56},{48,112},{56,8},{64,... | collective-permute-start | bytes 2359304 | tf_op jit(solution)/shard_map/ppermute | solution.py:44
  110.0 13.2 %collective-permute-start.16 = (bf16[128,3072]{1,0:T(8,128)(2,1)S(1)}, bf16[128,3072]{1,0:T(8,128)(2,1)S(1)}, u32[]{:S(2)}, u32[]{:S(2)}) collective-permute-start(bf16[128,3072]{1,0:T(8,128)(2,1)S(1)} %get-tuple-element.90), channel_id=1, source_target_pairs={{0,192},{8,56},{16,208},{24,8},{32,224},{40,24},{48,240},{56,40},{... | collective-permute-start | bytes 2359304 | tf_op jit(solution)/shard_map/ppermute | solution.py:44
  113.3 17.9 %collective-permute-start.17 = (bf16[128,3072]{1,0:T(8,128)(2,1)S(1)}, bf16[128,3072]{1,0:T(8,128)(2,1)S(1)}, u32[]{:S(2)}, u32[]{:S(2)}) collective-permute-start(bf16[128,3072]{1,0:T(8,128)(2,1)S(1)} %get-tuple-element.96), channel_id=1, source_target_pairs={{0,192},{8,56},{16,208},{24,8},{32,224},{40,24},{48,240},{56,40},{... | collective-permute-start | bytes 2359304 | tf_op jit(solution)/shard_map/ppermute | solution.py:44
  113.3 18.4 %collective-permute-start.20 = (bf16[128,3072]{1,0:T(8,128)(2,1)S(1)}, bf16[128,3072]{1,0:T(8,128)(2,1)S(1)}, u32[]{:S(2)}, u32[]{:S(2)}) collective-permute-start(bf16[128,3072]{1,0:T(8,128)(2,1)S(1)} %get-tuple-element.101), channel_id=1, source_target_pairs={{0,64},{8,24},{16,80},{24,40},{32,96},{40,56},{48,112},{56,8},{64,... | collective-permute-start | bytes 2359304 | tf_op jit(solution)/shard_map/ppermute | solution.py:44
  123.4 16.7 %collective-permute-start.19 = (bf16[128,3072]{1,0:T(8,128)(2,1)S(1)}, bf16[128,3072]{1,0:T(8,128)(2,1)S(1)}, u32[]{:S(2)}, u32[]{:S(2)}) collective-permute-start(bf16[128,3072]{1,0:T(8,128)(2,1)S(1)} %add_convert_fusion), channel_id=1, source_target_pairs={{0,64},{8,24},{16,80},{24,40},{32,96},{40,56},{48,112},{56,8},{64,... | collective-permute-start | bytes 2359304 | tf_op jit(solution)/shard_map/ppermute | solution.py:44
  123.7 16.5 %collective-permute-start.18 = (bf16[128,3072]{1,0:T(8,128)(2,1)S(1)}, bf16[128,3072]{1,0:T(8,128)(2,1)S(1)}, u32[]{:S(2)}, u32[]{:S(2)}) collective-permute-start(bf16[128,3072]{1,0:T(8,128)(2,1)S(1)} %add_convert_fusion.1), channel_id=1, source_target_pairs={{0,192},{8,56},{16,208},{24,8},{32,224},{40,24},{48,240},{56,40},{... | collective-permute-start | bytes 2359304 | tf_op jit(solution)/shard_map/ppermute | solution.py:44
  142.8 11.2 %collective-permute-start.23 = (bf16[32,6144]{1,0:T(8,128)(2,1)S(1)}, bf16[32,6144]{1,0:T(8,128)(2,1)S(1)}, u32[]{:S(2)}, u32[]{:S(2)}) collective-permute-start(bf16[32,6144]{1,0:T(8,128)(2,1)S(1)} %get-tuple-element.105), channel_id=1, source_target_pairs={{0,32},{8,136},{16,48},{24,152},{32,0},{40,168},{48,16},{56,184},{... | collective-permute-start | bytes 1179656 | tf_op jit(solution)/shard_map/ppermute | solution.py:44
  155.0 15.3 %all-to-all-start.3 = ((bf16[8,32,768]{2,1,0:T(8,128)(2,1)}), bf16[8,32,768]{2,1,0:T(8,128)(2,1)S(1)}, u32[]{:S(2)}, u32[]{:S(2)}) async-start(bf16[8,32,768]{2,1,0:T(8,128)(2,1)} %shard_map.128), calls=%async_computation.3 | async-start | bytes 786432 | tf_op jit(solution)/shard_map/all_to_all | solution.py:487
  (13 other events, 235.9 us)

commit v4 on v3

--- a/solution.py
+++ b/solution.py
@@ -218,11 +218,14 @@
     )(state, inside, decayed, stream, gain, lead, follow)
 
 
-def norm_kernel(rows_ref, gain_ref, out_ref):
+def norm_kernel(rows_ref, far_gain_ref, out_ref, gain_ref, sem):
+    fetch = pltpu.make_async_copy(far_gain_ref, gain_ref, sem)
+    fetch.start()
     parts, _, width = rows_ref.shape
     rows = [rows_ref[i].astype(F32) for i in range(parts)]
     squares = sum(jnp.sum(r * r, axis=-1, keepdims=True) for r in rows)
     scale = lax.rsqrt(squares / (parts * width) + STABILIZER)
+    fetch.wait()
     for i, r in enumerate(rows):
         part = slice(i * width, (i + 1) * width)
         out_ref[:, part] = (r * scale * gain_ref[:, part]).astype(BF16)
@@ -232,8 +235,9 @@
     return pl.pallas_call(
         norm_kernel,
         out_shape=jax.ShapeDtypeStruct((SLOTS, FEATURES), BF16),
-        in_specs=[whole()] * 2,
+        in_specs=[whole(), whole(pl.ANY)],
         out_specs=whole(),
+        scratch_shapes=[pltpu.VMEM((1, FEATURES), F32), pltpu.SemaphoreType.DMA],
         compiler_params=params(16),
     )(rows, gain)
 

time: 172 us -> 172 us (level)
  no operation moved by 1% of the time
where the time goes in v4:
time: 172 us; the launch traced here: 171 us
  waiting for transfers between devices  68 us (40%)
  starting transfers between devices  44.5 us (26%)
  Pallas kernels  32.7 us (19%)
  blocking collectives  23.8 us (14%)
    ppermute x21, waiting for transfers between devices, send(): lax.ppermute(rows, 'ctx', chip_pairs(lambda core: along_x[(core + axis) %...  44.9 us
    ppermute x21, starting transfers between devices, send(): lax.ppermute(rows, 'ctx', chip_pairs(lambda core: along_x[(core + axis) %...  26.8 us
    all_to_all x1, blocking collectives, body(): lax.all_to_all(sent, 'exp', split_axis=0, concat_axis=0, tiled=True)  23.8 us
    pallas_call x3, Pallas kernels, expert(): pl.pallas_call(lambda *refs: expert_kernel(layout, len(xs), *refs), out_s...  16.8 us
    all_to_all x1, waiting for transfers between devices, body(): lax.all_to_all(summed, 'exp', split_axis=0, concat_axis=0, tiled=True)  11.7 us
    all_to_all x1, waiting for transfers between devices, body(): lax.all_to_all(pieces, 'ctx', split_axis=0, concat_axis=0, tiled=True)  7.73 us
    all_to_all x1, starting transfers between devices, body(): lax.all_to_all(pieces, 'ctx', split_axis=0, concat_axis=0, tiled=True)  7.71 us
    all_to_all x1, starting transfers between devices, body(): lax.all_to_all(states, 'ctx', split_axis=0, concat_axis=0, tiled=True)  5.9 us
  transfers between devices with their start and end apart: 27, of which 17 were waited for; matrix products, arithmetic and copies ran while one was open for 1% of the time, Pallas kernels for 13%

profile of v4, /device:TPU:2, one launch (start us, length us, event | category | flops | bytes accessed | tf_op | source)
XLA Modules:
  0.0 171.2 jit_solution(4472512358999351293)
XLA Ops:
  3.0 7.7 %all-to-all-start = ((bf16[32,32,128]{2,1,0:T(8,128)(2,1)}), bf16[32,32,128]{2,1,0:T(8,128)(2,1)}, u32[]{:S(2)}, u32[]{:S(2)}) async-start(bf16[32,32,128]{2,1,0:T(8,128)(2,1)} %shard_map.118), calls=%async_computation | async-start | bytes 524288 | tf_op jit(solution)/shard_map/all_to_all | solution.py:441
  10.7 7.7 %all-to-all-done.pieces_ref = bf16[32,32,128]{2,1,0:T(8,128)(2,1)} async-done(((bf16[32,32,128]{2,1,0:T(8,128)(2,1)}), bf16[32,32,128]{2,1,0:T(8,128)(2,1)}, u32[]{:S(2)}, u32[]{:S(2)}) %all-to-all-start) | async-done | bytes 262176 | tf_op jit(solution)/shard_map/all_to_all | solution.py:441
  20.3 5.9 %all-to-all-start.1 = ((bf16[32,32,128]{2,1,0:T(8,128)(2,1)}), bf16[32,32,128]{2,1,0:T(8,128)(2,1)}, u32[]{:S(2)}, u32[]{:S(2)}) async-start(bf16[32,32,128]{2,1,0:T(8,128)(2,1)} %shard_map.119), calls=%async_computation.1 | async-start | bytes 524288 | tf_op jit(solution)/shard_map/all_to_all | solution.py:444
  27.6 2.7 %shard_map.120 = (f32[112,768]{1,0:T(8,128)}, bf16[112,768]{1,0:T(8,128)(2,1)}, bf16[112,256]{1,0:T(8,128)(2,1)}, bf16[112,256]{1,0:T(8,128)(2,1)}) custom-call(bf16[112,768]{1,0:T(8,128)(2,1)} %q_ref.1, bf16[112,768]{1,0:T(8,128)(2,1)} %k_ref.3, bf16[112,768]{1,0:T(8,128)(2,1)} %v_ref.3, f32[6,112]{1,0:T(8,128)} %bitcast.24, s32[112,2]{1,0:T(8,128)} %copy.13.routes_ref), custom_call_target="tpu_custom_call" | custom-call | flops 231211008 | bytes 2097152 | tf_op jit(solution)/shard_map/pallas_call | solution.py:144
  30.3 3.7 %all-to-all-done.1.state_ref = bf16[32,32,128]{2,1,0:T(8,128)(2,1)} async-done(((bf16[32,32,128]{2,1,0:T(8,128)(2,1)}), bf16[32,32,128]{2,1,0:T(8,128)(2,1)}, u32[]{:S(2)}, u32[]{:S(2)}) %all-to-all-start.1) | async-done | bytes 262176 | tf_op jit(solution)/shard_map/all_to_all | solution.py:444
  36.5 23.8 %all_to_all.20.rows_ref = bf16[8,32,768]{2,1,0:T(8,128)(2,1)S(1)} all-to-all(bf16[8,32,768]{2,1,0:T(8,128)(2,1)} %get-tuple-element.61), channel_id=1, replica_groups=mesh['ctx'=32,'exp'=8] {'exp'}, dimensions={0} | all-to-all | bytes 786432 | tf_op jit(solution)/shard_map/all_to_all | solution.py:452
  62.7 3.7 %shard_map.123 = (bf16[288,6144]{1,0:T(8,128)(2,1)S(1)}, bf16[288,6144]{1,0:T(8,128)(2,1)S(1)}, bf16[288,6144]{1,0:T(8,128)(2,1)S(1)}) custom-call(bf16[288,6144]{1,0:T(8,128)(2,1)S(1)} %collective-permute-done.refs_0_, bf16[288,6144]{1,0:T(8,128)(2,1)} %collective-permute-done.1.refs_1_, bf16[288,6144]{1,0:T(8,128)(2,1)} %collective-permute-done.2.refs_2_), custom_call_target="tpu_custom_call" | custom-call | bytes 10616832 | tf_op jit(solution)/shard_map/pallas_call | solution.py:262
  69.7 2.7 %collective-permute-start.9 = (bf16[32,3072]{1,0:T(8,128)(2,1)S(1)}, bf16[32,3072]{1,0:T(8,128)(2,1)S(1)}, u32[]{:S(2)}, u32[]{:S(2)}) collective-permute-start(bf16[32,3072]{1,0:T(8,128)(2,1)S(1)} %slice.20), channel_id=1, source_target_pairs={{0,48},{8,200},{16,0},{24,216},{32,16},{40,232},{48,32},{56,248},{... | collective-permute-start | bytes 589832 | tf_op jit(solution)/shard_map/ppermute | solution.py:44
  74.7 3.1 %collective-permute-done.9 = bf16[32,3072]{1,0:T(8,128)(2,1)S(1)} collective-permute-done((bf16[32,3072]{1,0:T(8,128)(2,1)S(1)}, bf16[32,3072]{1,0:T(8,128)(2,1)S(1)}, u32[]{:S(2)}, u32[]{:S(2)}) %collective-permute-start.9) | collective-permute-done | bytes 196640 | tf_op jit(solution)/shard_map/ppermute | solution.py:44
  77.8 4.7 %collective-permute-done.10 = bf16[32,3072]{1,0:T(8,128)(2,1)S(1)} collective-permute-done((bf16[32,3072]{1,0:T(8,128)(2,1)S(1)}, bf16[32,3072]{1,0:T(8,128)(2,1)S(1)}, u32[]{:S(2)}, u32[]{:S(2)}) %collective-permute-start.10) | collective-permute-done | bytes 196640 | tf_op jit(solution)/shard_map/ppermute | solution.py:44
  85.0 3.8 %collective-permute-done.5.refs_0_ = bf16[96,6144]{1,0:T(8,128)(2,1)S(1)} collective-permute-done((bf16[96,6144]{1,0:T(8,128)(2,1)S(1)}, bf16[96,6144]{1,0:T(8,128)(2,1)S(1)}, u32[]{:S(2)}, u32[]{:S(2)}) %collective-permute-start.5) | collective-permute-done | bytes 1179680 | tf_op jit(solution)/shard_map/ppermute | solution.py:44
  95.6 6.4 %shard_map.124 = (bf16[128,3072]{1,0:T(8,128)(2,1)S(1)}, bf16[128,3072]{1,0:T(8,128)(2,1)S(1)}, bf16[128,3072]{1,0:T(8,128)(2,1)S(1)}, bf16[128,3072]{1,0:T(8,128)(2,1)S(1)}) custom-call(bf16[96,6144]{1,0:T(8,128)(2,1)S(1)} %collective-permute-done.5.refs_0_, bf16[32,6144]{1,0:T(8,128)(2,1)S(1)} %collective-permute-done.11.refs_1_, ...), custom_call_target="tpu_custom_call" | custom-call | flops 5435817984 | bytes 21233664 | tf_op jit(solution)/shard_map/pallas_call | solution.py:324
  102.0 2.7 %collective-permute-done.14.refs_3_ = bf16[32,3072]{1,0:T(8,128)(2,1)S(1)} collective-permute-done((bf16[32,3072]{1,0:T(8,128)(2,1)S(1)}, bf16[32,3072]{1,0:T(8,128)(2,1)S(1)}, u32[]{:S(2)}, u32[]{:S(2)}) %collective-permute-start.14) | collective-permute-done | bytes 196640 | tf_op jit(solution)/shard_map/ppermute | solution.py:44
  104.8 5.2 %shard_map.125 = (bf16[128,3072]{1,0:T(8,128)(2,1)S(1)}, bf16[128,3072]{1,0:T(8,128)(2,1)S(1)}) custom-call(bf16[96,3072]{1,0:T(8,128)(2,1)S(1)} %collective-permute-done.6.refs_0_, bf16[96,3072]{1,0:T(8,128)(2,1)S(1)} %collective-permute-done.8.refs_1_, bf16[32,3072]{1,0:T(8,128)(2,1)S(1)} %collective-permute-done.12.refs_2_, ...), custom_call_target="tpu_custom_call" | custom-call | flops 5435817984 | bytes 21233664 | tf_op jit(solution)/shard_map/pallas_call | solution.py:324
  110.1 3.2 %collective-permute-start.16 = (bf16[128,3072]{1,0:T(8,128)(2,1)S(1)}, bf16[128,3072]{1,0:T(8,128)(2,1)S(1)}, u32[]{:S(2)}, u32[]{:S(2)}) collective-permute-start(bf16[128,3072]{1,0:T(8,128)(2,1)S(1)} %get-tuple-element.90), channel_id=1, source_target_pairs={{0,192},{8,56},{16,208},{24,8},{32,224},{40,24},{48,240},{56,40},{... | collective-permute-start | bytes 2359304 | tf_op jit(solution)/shard_map/ppermute | solution.py:44
  115.3 5.2 %shard_map.126 = (bf16[128,3072]{1,0:T(8,128)(2,1)S(1)}, bf16[128,3072]{1,0:T(8,128)(2,1)S(1)}) custom-call(bf16[96,6144]{1,0:T(8,128)(2,1)S(1)} %constant_dynamic-update-slice_fusion.refs_0_, bf16[32,6144]{1,0:T(8,128)(2,1)S(1)} %constant_dynamic-update-slice_fusion.3.refs_1_, bf16[288,6144]{1,0:T(8,128)(2,1)S(1)} %bitcast.13, ...), custom_call_target="tpu_custom_call" | custom-call | flops 5435817984 | bytes 21233664 | tf_op jit(solution)/shard_map/pallas_call | solution.py:324
  120.5 2.8 %collective-permute-done.15 = bf16[128,3072]{1,0:T(8,128)(2,1)S(1)} collective-permute-done((bf16[128,3072]{1,0:T(8,128)(2,1)S(1)}, bf16[128,3072]{1,0:T(8,128)(2,1)S(1)}, u32[]{:S(2)}, u32[]{:S(2)}) %collective-permute-start.15) | collective-permute-done | bytes 786464 | tf_op jit(solution)/shard_map/ppermute | solution.py:44
  123.7 3.3 %collective-permute-start.18 = (bf16[128,3072]{1,0:T(8,128)(2,1)S(1)}, bf16[128,3072]{1,0:T(8,128)(2,1)S(1)}, u32[]{:S(2)}, u32[]{:S(2)}) collective-permute-start(bf16[128,3072]{1,0:T(8,128)(2,1)S(1)} %add_convert_fusion.1), channel_id=1, source_target_pairs={{0,192},{8,56},{16,208},{24,8},{32,224},{40,24},{48,240},{56,40},{... | collective-permute-start | bytes 2359304 | tf_op jit(solution)/shard_map/ppermute | solution.py:44
  127.0 4.2 %collective-permute-done.17.a_one = bf16[128,3072]{1,0:T(8,128)(2,1)S(1)} collective-permute-done((bf16[128,3072]{1,0:T(8,128)(2,1)S(1)}, bf16[128,3072]{1,0:T(8,128)(2,1)S(1)}, u32[]{:S(2)}, u32[]{:S(2)}) %collective-permute-start.17) | collective-permute-done | bytes 786464 | tf_op jit(solution)/shard_map/ppermute | solution.py:44
  131.7 8.5 %collective-permute-done.19.b_one = bf16[128,3072]{1,0:T(8,128)(2,1)S(1)} collective-permute-done((bf16[128,3072]{1,0:T(8,128)(2,1)S(1)}, bf16[128,3072]{1,0:T(8,128)(2,1)S(1)}, u32[]{:S(2)}, u32[]{:S(2)}) %collective-permute-start.19) | collective-permute-done | bytes 786464 | tf_op jit(solution)/shard_map/ppermute | solution.py:44
  144.1 4.5 %collective-permute-done.21.refs_0_ = bf16[32,6144]{1,0:T(8,128)(2,1)S(1)} collective-permute-done((bf16[32,6144]{1,0:T(8,128)(2,1)S(1)}, bf16[32,6144]{1,0:T(8,128)(2,1)S(1)}, u32[]{:S(2)}, u32[]{:S(2)}) %collective-permute-start.21) | collective-permute-done | bytes 393248 | tf_op jit(solution)/shard_map/ppermute | solution.py:44
  148.7 5.4 %collective-permute-done.23.refs_2_ = bf16[32,6144]{1,0:T(8,128)(2,1)S(1)} collective-permute-done((bf16[32,6144]{1,0:T(8,128)(2,1)S(1)}, bf16[32,6144]{1,0:T(8,128)(2,1)S(1)}, u32[]{:S(2)}, u32[]{:S(2)}) %collective-permute-start.23) | collective-permute-done | bytes 393248 | tf_op jit(solution)/shard_map/ppermute | solution.py:44
  155.0 3.5 %all-to-all-start.3 = ((bf16[8,32,768]{2,1,0:T(8,128)(2,1)}), bf16[8,32,768]{2,1,0:T(8,128)(2,1)S(1)}, u32[]{:S(2)}, u32[]{:S(2)}) async-start(bf16[8,32,768]{2,1,0:T(8,128)(2,1)} %shard_map.128), calls=%async_computation.3 | async-start | bytes 786432 | tf_op jit(solution)/shard_map/all_to_all | solution.py:491
  158.6 11.7 %all-to-all-done.3.back_ref = bf16[8,32,768]{2,1,0:T(8,128)(2,1)S(1)} async-done(((bf16[8,32,768]{2,1,0:T(8,128)(2,1)}), bf16[8,32,768]{2,1,0:T(8,128)(2,1)S(1)}, u32[]{:S(2)}, u32[]{:S(2)}) %all-to-all-start.3) | async-done | bytes 393248 | tf_op jit(solution)/shard_map/all_to_all | solution.py:491
  (79 shorter events, 34.9 us)
Async XLA Ops:
  0.0 34.0 %collective-permute-start = (bf16[288,6144]{1,0:T(8,128)(2,1)}, bf16[288,6144]{1,0:T(8,128)(2,1)S(1)}, u32[]{:S(2)}, u32[]{:S(2)}) collective-permute-start(bf16[288,6144]{1,0:T(8,128)(2,1)} %bitcast.10), channel_id=1, source_target_pairs={{0,8},{8,0},{16,24},{24,16},{32,40},{40,32},{48,56},{56,48},{64,72... | collective-permute-start | bytes 10616840 | tf_op jit(solution)/shard_map/ppermute | solution.py:435
  0.0 34.0 %collective-permute-start.1 = (bf16[288,6144]{1,0:T(8,128)(2,1)}, bf16[288,6144]{1,0:T(8,128)(2,1)}, u32[]{:S(2)}, u32[]{:S(2)}) collective-permute-start(bf16[288,6144]{1,0:T(8,128)(2,1)} %bitcast.14), channel_id=1, source_target_pairs={{0,8},{8,0},{16,24},{24,16},{32,40},{40,32},{48,56},{56,48},{64,72... | collective-permute-start | bytes 10616840 | tf_op jit(solution)/shard_map/ppermute | solution.py:436
  0.5 33.5 %collective-permute-start.2 = (bf16[288,6144]{1,0:T(8,128)(2,1)}, bf16[288,6144]{1,0:T(8,128)(2,1)}, u32[]{:S(2)}, u32[]{:S(2)}) collective-permute-start(bf16[288,6144]{1,0:T(8,128)(2,1)} %bitcast.18), channel_id=1, source_target_pairs={{0,8},{8,0},{16,24},{24,16},{32,40},{40,32},{48,56},{56,48},{64,72... | collective-permute-start | bytes 10616840 | tf_op jit(solution)/shard_map/ppermute | solution.py:437
  3.0 15.5 %all-to-all-start = ((bf16[32,32,128]{2,1,0:T(8,128)(2,1)}), bf16[32,32,128]{2,1,0:T(8,128)(2,1)}, u32[]{:S(2)}, u32[]{:S(2)}) async-start(bf16[32,32,128]{2,1,0:T(8,128)(2,1)} %shard_map.118), calls=%async_computation | async-start | bytes 524288 | tf_op jit(solution)/shard_map/all_to_all | solution.py:441
  20.3 13.6 %all-to-all-start.1 = ((bf16[32,32,128]{2,1,0:T(8,128)(2,1)}), bf16[32,32,128]{2,1,0:T(8,128)(2,1)}, u32[]{:S(2)}, u32[]{:S(2)}) async-start(bf16[32,32,128]{2,1,0:T(8,128)(2,1)} %shard_map.119), calls=%async_computation.1 | async-start | bytes 524288 | tf_op jit(solution)/shard_map/all_to_all | solution.py:444
  69.7 8.1 %collective-permute-start.9 = (bf16[32,3072]{1,0:T(8,128)(2,1)S(1)}, bf16[32,3072]{1,0:T(8,128)(2,1)S(1)}, u32[]{:S(2)}, u32[]{:S(2)}) collective-permute-start(bf16[32,3072]{1,0:T(8,128)(2,1)S(1)} %slice.20), channel_id=1, source_target_pairs={{0,48},{8,200},{16,0},{24,216},{32,16},{40,232},{48,32},{56,248},{... | collective-permute-start | bytes 589832 | tf_op jit(solution)/shard_map/ppermute | solution.py:44
  72.5 16.3 %collective-permute-start.5 = (bf16[96,6144]{1,0:T(8,128)(2,1)S(1)}, bf16[96,6144]{1,0:T(8,128)(2,1)S(1)}, u32[]{:S(2)}, u32[]{:S(2)}) collective-permute-start(bf16[96,6144]{1,0:T(8,128)(2,1)S(1)} %constant_dynamic-update-slice_fusion.refs_0_), channel_id=1, source_target_pairs={{0,192},{8,56},{16,208},{24,8},{32,224},{40,24},{48,240},{56,40},{... | collective-permute-start | bytes 3538952 | tf_op jit(solution)/shard_map/ppermute | solution.py:44
  73.7 17.7 %collective-permute-start.7 = (bf16[96,6144]{1,0:T(8,128)(2,1)S(1)}, bf16[96,6144]{1,0:T(8,128)(2,1)S(1)}, u32[]{:S(2)}, u32[]{:S(2)}) collective-permute-start(bf16[96,6144]{1,0:T(8,128)(2,1)S(1)} %constant_dynamic-update-slice_fusion.refs_0_), channel_id=1, source_target_pairs={{0,64},{8,24},{16,80},{24,40},{32,96},{40,56},{48,112},{56,8},{64,... | collective-permute-start | bytes 3538952 | tf_op jit(solution)/shard_map/ppermute | solution.py:44
  74.6 7.9 %collective-permute-start.10 = (bf16[32,3072]{1,0:T(8,128)(2,1)S(1)}, bf16[32,3072]{1,0:T(8,128)(2,1)S(1)}, u32[]{:S(2)}, u32[]{:S(2)}) collective-permute-start(bf16[32,3072]{1,0:T(8,128)(2,1)S(1)} %slice.21), channel_id=1, source_target_pairs={{0,16},{8,72},{16,32},{24,88},{32,48},{40,104},{48,0},{56,120},{64... | collective-permute-start | bytes 589832 | tf_op jit(solution)/shard_map/ppermute | solution.py:44
  82.5 10.4 %collective-permute-start.11 = (bf16[32,6144]{1,0:T(8,128)(2,1)S(1)}, bf16[32,6144]{1,0:T(8,128)(2,1)S(1)}, u32[]{:S(2)}, u32[]{:S(2)}) collective-permute-start(bf16[32,6144]{1,0:T(8,128)(2,1)S(1)} %constant_dynamic-update-slice_fusion.3.refs_1_), channel_id=1, source_target_pairs={{0,192},{8,56},{16,208},{24,8},{32,224},{40,24},{48,240},{56,40},{... | collective-permute-start | bytes 1179656 | tf_op jit(solution)/shard_map/ppermute | solution.py:44
  85.0 10.5 %collective-permute-start.13 = (bf16[32,6144]{1,0:T(8,128)(2,1)S(1)}, bf16[32,6144]{1,0:T(8,128)(2,1)S(1)}, u32[]{:S(2)}, u32[]{:S(2)}) collective-permute-start(bf16[32,6144]{1,0:T(8,128)(2,1)S(1)} %constant_dynamic-update-slice_fusion.3.refs_1_), channel_id=1, source_target_pairs={{0,64},{8,24},{16,80},{24,40},{32,96},{40,56},{48,112},{56,8},{64,... | collective-permute-start | bytes 1179656 | tf_op jit(solution)/shard_map/ppermute | solution.py:44
  88.8 16.0 %collective-permute-start.6 = (bf16[96,3072]{1,0:T(8,128)(2,1)S(1)}, bf16[96,3072]{1,0:T(8,128)(2,1)S(1)}, u32[]{:S(2)}, u32[]{:S(2)}) collective-permute-start(bf16[96,3072]{1,0:T(8,128)(2,1)S(1)} %slice.24), channel_id=1, source_target_pairs={{0,192},{8,56},{16,208},{24,8},{32,224},{40,24},{48,240},{56,40},{... | collective-permute-start | bytes 1769480 | tf_op jit(solution)/shard_map/ppermute | solution.py:44
  91.5 13.3 %collective-permute-start.8 = (bf16[96,3072]{1,0:T(8,128)(2,1)S(1)}, bf16[96,3072]{1,0:T(8,128)(2,1)S(1)}, u32[]{:S(2)}, u32[]{:S(2)}) collective-permute-start(bf16[96,3072]{1,0:T(8,128)(2,1)S(1)} %slice.25), channel_id=1, source_target_pairs={{0,64},{8,24},{16,80},{24,40},{32,96},{40,56},{48,112},{56,8},{64,... | collective-permute-start | bytes 1769480 | tf_op jit(solution)/shard_map/ppermute | solution.py:44
  93.0 9.0 %collective-permute-start.12 = (bf16[32,3072]{1,0:T(8,128)(2,1)S(1)}, bf16[32,3072]{1,0:T(8,128)(2,1)S(1)}, u32[]{:S(2)}, u32[]{:S(2)}) collective-permute-start(bf16[32,3072]{1,0:T(8,128)(2,1)S(1)} %slice.26), channel_id=1, source_target_pairs={{0,192},{8,56},{16,208},{24,8},{32,224},{40,24},{48,240},{56,40},{... | collective-permute-start | bytes 589832 | tf_op jit(solution)/shard_map/ppermute | solution.py:44
  95.5 9.3 %collective-permute-start.14 = (bf16[32,3072]{1,0:T(8,128)(2,1)S(1)}, bf16[32,3072]{1,0:T(8,128)(2,1)S(1)}, u32[]{:S(2)}, u32[]{:S(2)}) collective-permute-start(bf16[32,3072]{1,0:T(8,128)(2,1)S(1)} %slice.27), channel_id=1, source_target_pairs={{0,64},{8,24},{16,80},{24,40},{32,96},{40,56},{48,112},{56,8},{64,... | collective-permute-start | bytes 589832 | tf_op jit(solution)/shard_map/ppermute | solution.py:44
  110.0 13.3 %collective-permute-start.15 = (bf16[128,3072]{1,0:T(8,128)(2,1)S(1)}, bf16[128,3072]{1,0:T(8,128)(2,1)S(1)}, u32[]{:S(2)}, u32[]{:S(2)}) collective-permute-start(bf16[128,3072]{1,0:T(8,128)(2,1)S(1)} %get-tuple-element.89), channel_id=1, source_target_pairs={{0,64},{8,24},{16,80},{24,40},{32,96},{40,56},{48,112},{56,8},{64,... | collective-permute-start | bytes 2359304 | tf_op jit(solution)/shard_map/ppermute | solution.py:44
  110.1 13.2 %collective-permute-start.16 = (bf16[128,3072]{1,0:T(8,128)(2,1)S(1)}, bf16[128,3072]{1,0:T(8,128)(2,1)S(1)}, u32[]{:S(2)}, u32[]{:S(2)}) collective-permute-start(bf16[128,3072]{1,0:T(8,128)(2,1)S(1)} %get-tuple-element.90), channel_id=1, source_target_pairs={{0,192},{8,56},{16,208},{24,8},{32,224},{40,24},{48,240},{56,40},{... | collective-permute-start | bytes 2359304 | tf_op jit(solution)/shard_map/ppermute | solution.py:44
  113.3 17.9 %collective-permute-start.17 = (bf16[128,3072]{1,0:T(8,128)(2,1)S(1)}, bf16[128,3072]{1,0:T(8,128)(2,1)S(1)}, u32[]{:S(2)}, u32[]{:S(2)}) collective-permute-start(bf16[128,3072]{1,0:T(8,128)(2,1)S(1)} %get-tuple-element.96), channel_id=1, source_target_pairs={{0,192},{8,56},{16,208},{24,8},{32,224},{40,24},{48,240},{56,40},{... | collective-permute-start | bytes 2359304 | tf_op jit(solution)/shard_map/ppermute | solution.py:44
  113.3 18.4 %collective-permute-start.20 = (bf16[128,3072]{1,0:T(8,128)(2,1)S(1)}, bf16[128,3072]{1,0:T(8,128)(2,1)S(1)}, u32[]{:S(2)}, u32[]{:S(2)}) collective-permute-start(bf16[128,3072]{1,0:T(8,128)(2,1)S(1)} %get-tuple-element.101), channel_id=1, source_target_pairs={{0,64},{8,24},{16,80},{24,40},{32,96},{40,56},{48,112},{56,8},{64,... | collective-permute-start | bytes 2359304 | tf_op jit(solution)/shard_map/ppermute | solution.py:44
  123.5 16.7 %collective-permute-start.19 = (bf16[128,3072]{1,0:T(8,128)(2,1)S(1)}, bf16[128,3072]{1,0:T(8,128)(2,1)S(1)}, u32[]{:S(2)}, u32[]{:S(2)}) collective-permute-start(bf16[128,3072]{1,0:T(8,128)(2,1)S(1)} %add_convert_fusion), channel_id=1, source_target_pairs={{0,64},{8,24},{16,80},{24,40},{32,96},{40,56},{48,112},{56,8},{64,... | collective-permute-start | bytes 2359304 | tf_op jit(solution)/shard_map/ppermute | solution.py:44
  123.7 16.5 %collective-permute-start.18 = (bf16[128,3072]{1,0:T(8,128)(2,1)S(1)}, bf16[128,3072]{1,0:T(8,128)(2,1)S(1)}, u32[]{:S(2)}, u32[]{:S(2)}) collective-permute-start(bf16[128,3072]{1,0:T(8,128)(2,1)S(1)} %add_convert_fusion.1), channel_id=1, source_target_pairs={{0,192},{8,56},{16,208},{24,8},{32,224},{40,24},{48,240},{56,40},{... | collective-permute-start | bytes 2359304 | tf_op jit(solution)/shard_map/ppermute | solution.py:44
  140.8 7.9 %collective-permute-start.22 = (bf16[32,6144]{1,0:T(8,128)(2,1)S(1)}, bf16[32,6144]{1,0:T(8,128)(2,1)S(1)}, u32[]{:S(2)}, u32[]{:S(2)}) collective-permute-start(bf16[32,6144]{1,0:T(8,128)(2,1)S(1)} %get-tuple-element.104), channel_id=1, source_target_pairs={{0,48},{8,200},{16,0},{24,216},{32,16},{40,232},{48,32},{56,248},{... | collective-permute-start | bytes 1179656 | tf_op jit(solution)/shard_map/ppermute | solution.py:44
  142.9 11.2 %collective-permute-start.23 = (bf16[32,6144]{1,0:T(8,128)(2,1)S(1)}, bf16[32,6144]{1,0:T(8,128)(2,1)S(1)}, u32[]{:S(2)}, u32[]{:S(2)}) collective-permute-start(bf16[32,6144]{1,0:T(8,128)(2,1)S(1)} %get-tuple-element.105), channel_id=1, source_target_pairs={{0,32},{8,136},{16,48},{24,152},{32,0},{40,168},{48,16},{56,184},{... | collective-permute-start | bytes 1179656 | tf_op jit(solution)/shard_map/ppermute | solution.py:44
  155.0 15.3 %all-to-all-start.3 = ((bf16[8,32,768]{2,1,0:T(8,128)(2,1)}), bf16[8,32,768]{2,1,0:T(8,128)(2,1)S(1)}, u32[]{:S(2)}, u32[]{:S(2)}) async-start(bf16[8,32,768]{2,1,0:T(8,128)(2,1)} %shard_map.128), calls=%async_computation.3 | async-start | bytes 786432 | tf_op jit(solution)/shard_map/all_to_all | solution.py:491
  (13 other events, 235.9 us)
